TPU v7x, 32 devices: a whole 2x2x4 slice. The times are simulated.
32 devices in a mesh: grp: 8 (over y, x, core), rep: 4 (over z).
Axes of the slice: x: 2, y: 2, z: 4, core: 2. Of those that a mesh axis runs over, the one named last changes fastest.
Arguments:
- inputs: bfloat16 [32, 384, 1536], P(('grp', 'rep')), may hold values from -6 to 6
- conditioning: bfloat16 [32, 130, 768], P(('grp', 'rep')), may hold values from -6 to 6
- positions: int32 [32, 384], P(('grp', 'rep')), may hold values from 0 to 2047, as said below
- slot_valid: int32 [32], P(('grp', 'rep')), may hold values from 0 to 1, as said below
- cotangent: bfloat16 [32, 384, 1536], P(('grp', 'rep')), may hold values from -6 to 6
- norm1_gain: bfloat16 [1536], P('grp'), may hold values from 0.5 to 1.5
- norm1_shift: bfloat16 [1536], P('grp'), may hold values from -1.75 to 1.75
- norm2_gain: bfloat16 [1536], P('grp'), may hold values from 0.5 to 1.5
- norm2_shift: bfloat16 [1536], P('grp'), may hold values from -1.75 to 1.75
- norm3_gain: bfloat16 [1536], P('grp'), may hold values from 0.5 to 1.5
- norm3_shift: bfloat16 [1536], P('grp'), may hold values from -1.75 to 1.75
- w_qkv: bfloat16 [4608, 1536], P('grp'), may hold values from -0.15625 to 0.15625
- w_out: bfloat16 [1536, 1536], P('grp'), may hold values from -1.25 to 1.25
- w_query2: bfloat16 [1536, 1536], P('grp'), may hold values from -0.15625 to 0.15625
- w_kv2: bfloat16 [3072, 768], P('grp'), may hold values from -0.21875 to 0.21875
- w_out2: bfloat16 [1536, 1536], P('grp'), may hold values from -0.875 to 0.875
- w_gate: bfloat16 [6144, 1536], P('grp'), may hold values from -0.15625 to 0.15625
- w_up: bfloat16 [6144, 1536], P('grp'), may hold values from -0.15625 to 0.15625
- w_down: bfloat16 [6144, 1536], P('grp'), may hold values from -0.15625 to 0.15625
Outputs:
- outputs: bfloat16 [32, 384, 1536], P(('grp', 'rep'))
- d_inputs: float32 [32, 384, 1536], P(('grp', 'rep'))
- grad_norm1_gain: float32 [1536], P('grp')
- grad_norm1_shift: float32 [1536], P('grp')
- grad_norm2_gain: float32 [1536], P('grp')
- grad_norm2_shift: float32 [1536], P('grp')
- grad_norm3_gain: float32 [1536], P('grp')
- grad_norm3_shift: float32 [1536], P('grp')
- grad_w_qkv: float32 [4608, 1536], P('grp')
- grad_w_out: float32 [1536, 1536], P('grp')
- grad_w_query2: float32 [1536, 1536], P('grp')
- grad_w_kv2: float32 [3072, 768], P('grp')
- grad_w_out2: float32 [1536, 1536], P('grp')
- grad_w_gate: float32 [6144, 1536], P('grp')
- grad_w_up: float32 [6144, 1536], P('grp')
- grad_w_down: float32 [6144, 1536], P('grp')
Inputs may be any that keep to these rules, and one draw needn't show every extreme that they name: Within a slot, positions rise by 1 or 2 from one token to the next; some slot starts at 0 and some slot ends at 2047. `slot_valid`: exactly 11 slots hold 1.
All inputs are finite; a program needn't handle non-finite values.
Results may differ from a plain program's by a relative error of at most 0.025.
Values may be sent and summed in bfloat16 or wider, within the bound.
A program may use at most 384 MiB of HBM per device.

v0:
```python
import math

import jax
import jax.numpy as jnp
from jax import lax
from jax.sharding import PartitionSpec as P

D = 1536
HEADS = 24
HD = 64
NC = 130


epsilon = 1e-05
score_scale = 0.125


def layer_norm(tensor, gain, shift):
    center = tensor - jnp.mean(tensor, axis=-1, keepdims=True)
    spread = jnp.mean(center * center, axis=-1, keepdims=True)
    return center * lax.rsqrt(spread + epsilon) * gain + shift


def norm_back(tensor, gain, shift, d_normed):
    _, pullback = jax.vjp(layer_norm, tensor, gain, shift)
    return pullback(d_normed)


def swiglu(gate_part, up_part):
    return jax.nn.silu(gate_part) * up_part


def swiglu_back(gate_part, up_part, d_hidden):
    _, pullback = jax.vjp(swiglu, gate_part, up_part)
    return pullback(d_hidden)


def angles(positions, head_size):
    quarter = head_size // 4
    frequency = jnp.exp(jnp.arange(quarter, dtype=jnp.float32) * (-math.log(10000.0) / quarter))
    turned = positions.astype(jnp.float32)[:, None] * frequency[None, :]
    return (jnp.cos(turned)[:, None, :], jnp.sin(turned)[:, None, :])


def rotate(tensor, cosine, sin_table):
    quarter = tensor.shape[-1] // 4
    first_half = tensor[..., :quarter]
    second_half = tensor[..., quarter : 2 * quarter]
    remainder = tensor[..., 2 * quarter :]
    return jnp.concatenate(
        [
            first_half * cosine - second_half * sin_table,
            first_half * sin_table + second_half * cosine,
            remainder,
        ],
        axis=-1,
    )


def dot_nt(left_side, right_side):
    return lax.dot_general(
        left_side, right_side, (((1,), (1,)), ((), ())), preferred_element_type=jnp.float32
    )


def dot_tn(left_side, right_side):
    return lax.dot_general(
        left_side, right_side, (((0,), (0,)), ((), ())), preferred_element_type=jnp.float32
    )


def attend(queries, key_heads, value_heads):
    seq_len = queries.shape[0]
    span = min(seq_len, 512)
    blocked = queries.reshape(seq_len // span, span, queries.shape[1], queries.shape[2])

    def one_block(query_block):
        scores = (
            jnp.einsum("qhd,khd->hqk", query_block, key_heads, preferred_element_type=jnp.float32)
            * score_scale
        )
        largest = jnp.max(scores, axis=-1, keepdims=True)
        shifted = jnp.exp(scores - largest)
        totals = jnp.sum(shifted, axis=-1, keepdims=True)
        probability = (shifted / totals).astype(jnp.bfloat16)
        result = jnp.einsum(
            "hqk,khd->qhd", probability, value_heads, preferred_element_type=jnp.float32
        )
        return (result.astype(jnp.bfloat16), (largest + jnp.log(totals))[..., 0])

    outcome, log_sums = lax.map(one_block, blocked)
    return (outcome.reshape(queries.shape), log_sums)


def attend_back(queries, key_heads, value_heads, log_sums, grad_heads):
    seq_len = queries.shape[0]
    span = min(seq_len, 512)
    block_count = seq_len // span
    query_blocks = queries.reshape(block_count, span, queries.shape[1], queries.shape[2])
    grad_blocks = grad_heads.reshape(block_count, span, queries.shape[1], queries.shape[2])

    def one_block(carried, inputs_block):
        query_block, log_block, grad_block = inputs_block
        scores = (
            jnp.einsum("qhd,khd->hqk", query_block, key_heads, preferred_element_type=jnp.float32)
            * score_scale
        )
        probability = jnp.exp(scores - log_block[..., None])
        d_prob = jnp.einsum(
            "qhd,khd->hqk", grad_block, value_heads, preferred_element_type=jnp.float32
        )
        inner = jnp.sum(probability * d_prob, axis=-1, keepdims=True)
        d_scores = (probability * (d_prob - inner)).astype(jnp.bfloat16)
        d_query = (
            jnp.einsum("hqk,khd->qhd", d_scores, key_heads, preferred_element_type=jnp.float32)
            * score_scale
        )
        d_key = (
            carried[0]
            + jnp.einsum("hqk,qhd->khd", d_scores, query_block, preferred_element_type=jnp.float32)
            * score_scale
        )
        d_value = carried[1] + jnp.einsum(
            "hqk,qhd->khd",
            probability.astype(jnp.bfloat16),
            grad_block,
            preferred_element_type=jnp.float32,
        )
        return ((d_key, d_value), d_query)

    start_zero = jnp.zeros(key_heads.shape, jnp.float32)
    (d_key, d_value), d_query = lax.scan(
        one_block, (start_zero, start_zero), (query_blocks, log_sums, grad_blocks)
    )
    return (d_query.reshape(queries.shape), d_key, d_value)


def project(activation, weight):
    return dot_nt(activation, lax.all_gather(weight, "grp", axis=0, tiled=True))


def project_back(grad_cols, weight):
    return jnp.dot(
        grad_cols,
        lax.all_gather(weight, "grp", axis=0, tiled=True),
        preferred_element_type=jnp.float32,
    )


def reduce_rows(row_term, row_total):
    return lax.psum_scatter(
        row_term(jnp.int32(0), row_total * lax.axis_size("grp")).astype(jnp.bfloat16),
        "grp",
        scatter_dimension=0,
        tiled=True,
    ).astype(jnp.float32)


def column_term(left_side, right_side):

    def block_term(first_row, row_count):
        return dot_tn(left_side, right_side)

    return block_term


def weight_grad(grad_cols, activation):
    return reduce_rows(
        column_term(grad_cols, activation), grad_cols.shape[1] // lax.axis_size("grp")
    )


def ffn_reduce(row_term, row_total):
    return lax.psum_scatter(
        row_term(jnp.int32(0), row_total * lax.axis_size("grp")).astype(jnp.bfloat16),
        "grp",
        scatter_dimension=0,
        tiled=True,
    ).astype(jnp.float32)


def per_device(
    inputs,
    conditioning,
    positions,
    slot_valid,
    cotangent,
    norm1_gain,
    norm1_shift,
    norm2_gain,
    norm2_shift,
    norm3_gain,
    norm3_shift,
    w_qkv,
    w_out,
    w_query2,
    w_kv2,
    w_out2,
    w_gate,
    w_up,
    w_down,
):
    tokens = inputs[0].astype(jnp.float32)
    seq_len = tokens.shape[0]
    cond_rows = conditioning[0]
    gain_one, shift_one, gain_two, shift_two, gain_three, shift_three = (
        lax.all_gather(norm1_gain, "grp", axis=0, tiled=True),
        lax.all_gather(norm1_shift, "grp", axis=0, tiled=True),
        lax.all_gather(norm2_gain, "grp", axis=0, tiled=True),
        lax.all_gather(norm2_shift, "grp", axis=0, tiled=True),
        lax.all_gather(norm3_gain, "grp", axis=0, tiled=True),
        lax.all_gather(norm3_shift, "grp", axis=0, tiled=True),
    )
    gain_one = gain_one.astype(jnp.float32)
    shift_one = shift_one.astype(jnp.float32)
    gain_two = gain_two.astype(jnp.float32)
    shift_two = shift_two.astype(jnp.float32)
    gain_three = gain_three.astype(jnp.float32)
    shift_three = shift_three.astype(jnp.float32)
    cosine, sin_table = angles(positions[0], HD)
    act_one = layer_norm(tokens, gain_one, shift_one).astype(jnp.bfloat16)
    qkv_rows = project(act_one, w_qkv)
    queries = rotate(qkv_rows[:, :D].reshape(seq_len, HEADS, HD), cosine, sin_table).astype(
        jnp.bfloat16
    )
    key_heads = rotate(
        qkv_rows[:, D : 2 * D].reshape(seq_len, HEADS, HD), cosine, sin_table
    ).astype(jnp.bfloat16)
    value_heads = qkv_rows[:, 2 * D :].reshape(seq_len, HEADS, HD).astype(jnp.bfloat16)
    attended, log_one = attend(queries, key_heads, value_heads)
    flat_one = attended.reshape(seq_len, D)
    section_one = tokens + project(flat_one, w_out)
    act_two = layer_norm(section_one, gain_two, shift_two).astype(jnp.bfloat16)
    query_two = project(act_two, w_query2).astype(jnp.bfloat16).reshape(seq_len, HEADS, HD)
    kv_two = project(cond_rows, w_kv2).astype(jnp.bfloat16)
    key_two = kv_two[:, :D].reshape(NC, HEADS, HD)
    value_two = kv_two[:, D:].reshape(NC, HEADS, HD)
    attended_two, log_two = attend(query_two, key_two, value_two)
    flat_two = attended_two.reshape(seq_len, D)
    section_two = section_one + project(flat_two, w_out2)
    act_three = layer_norm(section_two, gain_three, shift_three).astype(jnp.bfloat16)
    pieces = lax.all_gather((w_gate, w_up), "grp", axis=0, tiled=True)
    gate_pre = dot_nt(act_three, pieces[0])
    up_pre = dot_nt(act_three, pieces[1])
    hidden = swiglu(gate_pre, up_pre).astype(jnp.bfloat16)
    mlp_out = jnp.dot(
        hidden,
        lax.all_gather(w_down, "grp", axis=0, tiled=True),
        preferred_element_type=jnp.float32,
    )
    outputs = (section_two + mlp_out).astype(jnp.bfloat16)
    grad_out = cotangent[0].astype(jnp.float32) * slot_valid[0].astype(jnp.float32)
    grad_mlp = grad_out.astype(jnp.bfloat16)
    d_hidden = dot_nt(grad_mlp, lax.all_gather(w_down, "grp", axis=0, tiled=True))
    d_gate_full, d_up_full = swiglu_back(gate_pre, up_pre, d_hidden)
    d_gate = d_gate_full.astype(jnp.bfloat16)
    d_up = d_up_full.astype(jnp.bfloat16)
    pieces = (
        lax.all_gather(w_gate, "grp", axis=0, tiled=True),
        lax.all_gather(w_up, "grp", axis=0, tiled=True),
    )
    d_norm3 = jnp.dot(d_gate, pieces[0], preferred_element_type=jnp.float32) + jnp.dot(
        d_up, pieces[1], preferred_element_type=jnp.float32
    )
    rows_hidden = w_gate.shape[0]
    grad_gate = ffn_reduce(column_term(d_gate, act_three), rows_hidden)
    grad_up = ffn_reduce(column_term(d_up, act_three), rows_hidden)
    grad_down = ffn_reduce(column_term(hidden, grad_mlp), rows_hidden)
    d_ln_three, d_gain_three, d_shift_three = norm_back(
        section_two, gain_three, shift_three, d_norm3
    )
    d_section_two = grad_out + d_ln_three
    d_cross = d_section_two.astype(jnp.bfloat16)
    grad_out_two = weight_grad(d_cross, flat_two)
    d_att_two = project_back(d_cross, w_out2).astype(jnp.bfloat16).reshape(seq_len, HEADS, HD)
    d_query_full, d_key_full, d_value_full = attend_back(
        query_two, key_two, value_two, log_two, d_att_two
    )
    d_query_two = d_query_full.reshape(seq_len, D).astype(jnp.bfloat16)
    d_kv_two = jnp.concatenate(
        [d_key_full.reshape(NC, D), d_value_full.reshape(NC, D)], axis=1
    ).astype(jnp.bfloat16)
    grad_query_two = weight_grad(d_query_two, act_two)
    grad_kv_two = weight_grad(d_kv_two, cond_rows)
    d_norm2 = project_back(d_query_two, w_query2)
    d_ln_two, d_gain_two, d_shift_two = norm_back(section_one, gain_two, shift_two, d_norm2)
    d_section_one = d_section_two + d_ln_two
    d_attn = d_section_one.astype(jnp.bfloat16)
    grad_out_one = weight_grad(d_attn, flat_one)
    d_att = project_back(d_attn, w_out).astype(jnp.bfloat16).reshape(seq_len, HEADS, HD)
    d_query, d_key, d_value = attend_back(queries, key_heads, value_heads, log_one, d_att)
    d_qkv = jnp.concatenate(
        [
            rotate(d_query, cosine, -sin_table).reshape(seq_len, D),
            rotate(d_key, cosine, -sin_table).reshape(seq_len, D),
            d_value.reshape(seq_len, D),
        ],
        axis=1,
    ).astype(jnp.bfloat16)
    grad_qkv = weight_grad(d_qkv, act_one)
    d_norm1 = project_back(d_qkv, w_qkv)
    d_ln_one, d_gain_one, d_shift_one = norm_back(tokens, gain_one, shift_one, d_norm1)
    d_tokens = d_section_one + d_ln_one
    norm_stack = jnp.stack(
        [d_gain_one, d_shift_one, d_gain_two, d_shift_two, d_gain_three, d_shift_three], axis=1
    )

    def norm_term(first_row, row_count):
        return norm_stack

    norm_shard = reduce_rows(norm_term, norm1_gain.shape[0])
    summed = (
        lax.psum(norm_shard.astype(jnp.bfloat16), "rep").astype(jnp.float32),
        lax.psum(grad_qkv.astype(jnp.bfloat16), "rep").astype(jnp.float32),
        lax.psum(grad_out_one.astype(jnp.bfloat16), "rep").astype(jnp.float32),
        lax.psum(grad_query_two.astype(jnp.bfloat16), "rep").astype(jnp.float32),
        lax.psum(grad_kv_two.astype(jnp.bfloat16), "rep").astype(jnp.float32),
        lax.psum(grad_out_two.astype(jnp.bfloat16), "rep").astype(jnp.float32),
        lax.psum(grad_gate.astype(jnp.bfloat16), "rep").astype(jnp.float32),
        lax.psum(grad_up.astype(jnp.bfloat16), "rep").astype(jnp.float32),
        lax.psum(grad_down.astype(jnp.bfloat16), "rep").astype(jnp.float32),
    )
    norm_total = summed[0]
    return (
        outputs[None],
        d_tokens[None],
        norm_total[:, 0],
        norm_total[:, 1],
        norm_total[:, 2],
        norm_total[:, 3],
        norm_total[:, 4],
        norm_total[:, 5],
        summed[1],
        summed[2],
        summed[3],
        summed[4],
        summed[5],
        summed[6],
        summed[7],
        summed[8],
    )


def solution(mesh):
    return jax.shard_map(
        per_device,
        mesh=mesh,
        in_specs=(
            P(("grp", "rep"), None, None),
            P(("grp", "rep"), None, None),
            P(("grp", "rep"), None),
            P(("grp", "rep")),
            P(("grp", "rep"), None, None),
            P("grp"),
            P("grp"),
            P("grp"),
            P("grp"),
            P("grp"),
            P("grp"),
            P("grp", None),
            P("grp", None),
            P("grp", None),
            P("grp", None),
            P("grp", None),
            P("grp", None),
            P("grp", None),
            P("grp", None),
        ),
        out_specs=(
            P(("grp", "rep"), None, None),
            P(("grp", "rep"), None, None),
            P("grp"),
            P("grp"),
            P("grp"),
            P("grp"),
            P("grp"),
            P("grp"),
            P("grp", None),
            P("grp", None),
            P("grp", None),
            P("grp", None),
            P("grp", None),
            P("grp", None),
            P("grp", None),
            P("grp", None),
        ),
        check_vma=False,
    )
```

profile of v0, /device:TPU:24, one launch (start us, length us, event | category | flops | bytes accessed | tf_op | source)
XLA Modules:
  0.0 1780.2 jit_solution(5424196632132398015)
XLA Ops:
  16.2 24.5 %all-reduce.6 = (bf16[1536]{0:T(1024)(128)(2,1)S(1)}, bf16[1536]{0:T(1024)(128)(2,1)S(1)}, bf16[1536]{0:T(1024)(128)(2,1)S(1)}, bf16[1536]{0:T(1024)(128)(2,1)S(...) all-reduce(bf16[1536]{0:T(1024)(128)(2,1)S(1)} %dynamic-update-slic, ...), channel_id=1, replica_groups=mesh['grp'=8,'rep'=4] {'grp'}, use_global_device_ids=true, to_apply=%add.1 | all-reduce | flops 9216 | bytes 36864
  42.4 7.7 all-gather.13.cloned.1.call-done
  50.1 4.0 convolution_convert_fusion.8
  55.6 75.1 %all-gather.9.cloned.1.call-done = bf16[4608,1536]{1,0:T(8,128)(2,1)} async-done(((bf16[576,1536]{1,0:T(8,128)(2,1)}), bf16[4608,1536]{1,0:T(8,128)(2,1)}) %all-gather.9.cloned.1.call-update) | async-done | bytes 14155792 | tf_op jit(solution)/shard_map/all_gather | solution.py:139
  130.7 9.3 fusion.66
  140.2 2.5 fusion.72
  142.7 3.0 copy.72
  148.5 3.3 copy.73
  153.1 2.1 subtract_convert_fusion.3
  155.3 6.6 multiply_reduce_fusion.1
  161.9 7.6 fusion
  169.6 9.3 fusion.36
  179.0 5.2 fusion.75
  186.0 26.2 %all-gather.15.cloned.1.call-done = bf16[1536,1536]{1,0:T(8,128)(2,1)} async-done(((bf16[192,1536]{1,0:T(8,128)(2,1)}), bf16[1536,1536]{1,0:T(8,128)(2,1)}) %all-gather.15.cloned.1.call-update) | async-done | bytes 4718608 | tf_op jit(solution)/shard_map/all_gather | solution.py:139
  212.3 5.1 convolution_convert_fusion.11
  221.7 2.5 fusion.35
  224.2 28.8 %all-gather.17.cloned.1.call-done = bf16[1536,1536]{1,0:T(8,128)(2,1)} async-done(((bf16[192,1536]{1,0:T(8,128)(2,1)}), bf16[1536,1536]{1,0:T(8,128)(2,1)}) %all-gather.17.cloned.1.call-update) | async-done | bytes 4718608 | tf_op jit(solution)/shard_map/all_gather | solution.py:139
  252.9 5.6 fusion.76
  260.4 93.0 %all-gather.21.cloned.1.call-done = bf16[6144,1536]{1,0:T(8,128)(2,1)} async-done(((bf16[768,1536]{1,0:T(8,128)(2,1)}), bf16[6144,1536]{1,0:T(8,128)(2,1)}) %all-gather.21.cloned.1.call-update) | async-done | bytes 18874384 | tf_op jit(solution)/shard_map/all_gather | solution.py:242
  353.4 14.0 fusion.78
  367.4 86.6 %all-gather.19.cloned.1.call-done = bf16[6144,1536]{1,0:T(8,128)(2,1)} async-done(((bf16[768,1536]{1,0:T(8,128)(2,1)}), bf16[6144,1536]{1,0:T(8,128)(2,1)}) %all-gather.19.cloned.1.call-update) | async-done | bytes 18874384 | tf_op jit(solution)/shard_map/all_gather | solution.py:242
  454.1 14.0 fusion.77
  468.1 86.7 %all-gather.23.cloned.1.call-done = bf16[6144,1536]{1,0:T(8,128)(2,1)} async-done(((bf16[768,1536]{1,0:T(8,128)(2,1)}), bf16[6144,1536]{1,0:T(8,128)(2,1)}) %all-gather.23.cloned.1.call-update) | async-done | bytes 18874384 | tf_op jit(solution)/shard_map/all_gather | solution.py:248
  554.8 23.3 %multiply_convert_fusion.1 = (bf16[384,6144]{1,0:T(8,128)(2,1)}, bf16[384,6144]{1,0:T(8,128)(2,1)}, bf16[384,6144]{1,0:T(8,128)(2,1)}) fusion(f32[384,6144]{1,0:T(8,128)} %fusion.77, f32[384,6144]{1,0:T(8,128)} %fusion.78, bf16[6144,1536]{1,0:T(8,128)(2,1)} %all-gather.23.cloned.1.call-done, bf16[1,384,1536]{2,1,0:T(8,128)(2,1)} %param.23, f32[]{:T(128)} %bitcast.12), kind=kOutput, calls=%fused_computation.15 | convolution fusion | flops 7287275520 | bytes 53084164 | tf_op jit(solution)/shard_map/dot_general | solution.py:61
  578.1 12.3 fusion.79
  590.4 12.2 multiply_reduce_fusion.4
  606.1 4.4 convolution_convert_fusion.4
  610.6 5.4 convolution_convert_fusion.10
  616.0 2.1 copy.78
  618.1 4.8 multiply_reduce_fusion.2
  626.7 4.6 convolution_convert_fusion.5
  631.4 2.6 multiply_convert_fusion.5
  634.1 3.7 fusion.41
  637.8 3.5 convolution_convert_fusion.7
  643.0 5.4 multiply_reduce_fusion.5
  651.8 4.5 convolution_convert_fusion.6
  656.4 5.4 convolution_convert_fusion.9
  661.7 1.8 copy.81
  663.6 13.3 multiply_reduce_fusion
  677.6 8.0 multiply_convert_fusion
  687.1 4.0 multiply_bitcast_fusion
  694.3 1.8 pad_maximum_fusion.5
  696.2 2.7 fusion.37
  699.9 13.0 convolution_convert_fusion.3
  714.2 15.5 convolution_convert_fusion
  731.0 15.6 convolution_convert_fusion.1
  746.8 16.5 convolution_convert_fusion.2
  764.5 10.1 fusion.69
  779.6 57.6 %reduce-scatter.14.cloned.1.call-done = bf16[192,1536]{1,0:T(8,128)(2,1)} async-done(((bf16[1536,1536]{1,0:T(8,128)(2,1)}), bf16[192,1536]{1,0:T(8,128)(2,1)}) %reduce-scatter.14.cloned.1.call-update) | async-done | bytes 589840 | tf_op jit(solution)/shard_map/reduce_scatter | solution.py:151
  837.2 104.4 %reduce-scatter.12.cloned.1.call-done = bf16[576,1536]{1,0:T(8,128)(2,1)} async-done(((bf16[4608,1536]{1,0:T(8,128)(2,1)}), bf16[576,1536]{1,0:T(8,128)(2,1)}) %reduce-scatter.12.cloned.1.call-update) | async-done | bytes 1769488 | tf_op jit(solution)/shard_map/reduce_scatter | solution.py:151
  941.5 129.6 %reduce-scatter.26.cloned.1.call-done = bf16[768,1536]{1,0:T(8,128)(2,1)} async-done(((bf16[6144,1536]{1,0:T(8,128)(2,1)}), bf16[768,1536]{1,0:T(8,128)(2,1)}) %reduce-scatter.26.cloned.1.call-update) | async-done | bytes 2359312 | tf_op jit(solution)/shard_map/reduce_scatter | solution.py:174
  1071.2 129.6 %reduce-scatter.24.cloned.1.call-done = bf16[768,1536]{1,0:T(8,128)(2,1)} async-done(((bf16[6144,1536]{1,0:T(8,128)(2,1)}), bf16[768,1536]{1,0:T(8,128)(2,1)}) %reduce-scatter.24.cloned.1.call-update) | async-done | bytes 2359312 | tf_op jit(solution)/shard_map/reduce_scatter | solution.py:174
  1200.7 129.6 %reduce-scatter.22.cloned.1.call-done = bf16[768,1536]{1,0:T(8,128)(2,1)} async-done(((bf16[6144,1536]{1,0:T(8,128)(2,1)}), bf16[768,1536]{1,0:T(8,128)(2,1)}) %reduce-scatter.22.cloned.1.call-update) | async-done | bytes 2359312 | tf_op jit(solution)/shard_map/reduce_scatter | solution.py:174
  1330.4 4.7 add_bitcast_fusion
  1335.1 13.5 fusion.21
  1348.6 19.0 %reduce-scatter.28.cloned.1.call-done = bf16[192,6]{1,0:T(8,128)(2,1)} async-done(((bf16[1536,6]{1,0:T(8,128)(2,1)}), bf16[192,6]{1,0:T(8,128)(2,1)}) %reduce-scatter.28.cloned.1.call-update) | async-done | bytes 2320
  1368.5 8.1 psum.63
  1377.2 378.0 %all-reduce.10.cloned.1.call-done = (bf16[576,1536]{1,0:T(8,128)(2,1)}, bf16[192,1536]{1,0:T(8,128)(2,1)}, bf16[192,1536]{1,0:T(8,128)(2,1)}, bf16[384,768]{1,0:...) async-done(((bf16[576,1536]{1,0:T(8,128)(2,1)}, bf16[192,1536]{1,0:T(8,128)(2,1)}, ...) | async-done | bytes 11206672 | tf_op jit(solution)/shard_map/psum | solution.py:314
  1755.3 2.3 convert_element_type.255
  1757.6 2.3 convert_element_type.257
  1762.1 2.3 convert_element_type.253
  1764.4 2.8 convert_element_type.264
  1767.2 2.8 convert_element_type.266
  1770.1 2.8 convert_element_type.268
  (294 shorter events, 53.8 us)
Async XLA Ops:
  7.2 42.9 %copy-start = (bf16[1,130,768]{2,1,0:T(8,128)(2,1)S(1)}, bf16[1,130,768]{2,1,0:T(8,128)(2,1)}, u32[]{:S(2)}) copy-start(bf16[1,130,768]{2,1,0:T(8,128)(2,1)} %param.20) | copy-start | bytes 599044
  7.2 42.9 %all-gather.13.cloned.1.call-start = ((), (), s32[]{:S(2)}) async-start(), calls=%async_computation.11 | async-start | bytes 5308416 | tf_op jit(solution)/shard_map/all_gather | solution.py:139
  7.9 122.8 %all-gather.9.cloned.1.call-start = ((), (), s32[]{:S(2)}) async-start(), calls=%async_computation.9 | async-start | bytes 15925248 | tf_op jit(solution)/shard_map/all_gather | solution.py:139
  8.7 170.3 %all-gather.11.cloned.1.call-start = ((), (), s32[]{:S(2)}) async-start(), calls=%async_computation.10 | async-start | bytes 5308416 | tf_op jit(solution)/shard_map/all_gather | solution.py:139
  9.4 202.8 %all-gather.15.cloned.1.call-start = ((), (), s32[]{:S(2)}) async-start(), calls=%async_computation.12 | async-start | bytes 5308416 | tf_op jit(solution)/shard_map/all_gather | solution.py:139
  10.0 242.9 %all-gather.17.cloned.1.call-start = ((), (), s32[]{:S(2)}) async-start(), calls=%async_computation.13 | async-start | bytes 5308416 | tf_op jit(solution)/shard_map/all_gather | solution.py:139
  10.6 342.8 %all-gather.21.cloned.1.call-start = ((), (), s32[]{:S(2)}) async-start(), calls=%async_computation.15 | async-start | bytes 21233664 | tf_op jit(solution)/shard_map/all_gather | solution.py:242
  11.2 4.0 copy-start.75
  11.2 4.3 copy-start.76
  11.2 4.5 copy-start.77
  11.2 4.8 copy-start.78
  11.2 29.6 %copy-start.72 = (s32[1,384]{1,0:T(1,128)S(1)}, s32[1,384]{1,0:T(1,128)}, u32[]{:S(2)}) copy-start(s32[1,384]{1,0:T(1,128)} %param.21) | copy-start | bytes 4612
  11.2 29.6 %copy-start.7 = (bf16[1,384,1536]{2,1,0:T(8,128)(2,1)S(1)}, bf16[1,384,1536]{2,1,0:T(8,128)(2,1)}, u32[]{:S(2)}) copy-start(bf16[1,384,1536]{2,1,0:T(8,128)(2,1)} %param.19) | copy-start | bytes 3538948
  11.3 442.8 %all-gather.19.cloned.1.call-start = ((), (), s32[]{:S(2)}) async-start(), calls=%async_computation.14 | async-start | bytes 21233664 | tf_op jit(solution)/shard_map/all_gather | solution.py:242
  12.0 542.8 %all-gather.23.cloned.1.call-start = ((), (), s32[]{:S(2)}) async-start(), calls=%async_computation.16 | async-start | bytes 21233664 | tf_op jit(solution)/shard_map/all_gather | solution.py:248
  12.8 765.5 %reduce-scatter.20.cloned.1.call-start = ((), (), s32[]{:S(2)}) async-start(), calls=%async_computation.21 | async-start | bytes 5308416 | tf_op jit(solution)/shard_map/reduce_scatter | solution.py:151
  40.7 90.0 %copy-start.66 = (f32[1536]{0:T(1024)}, f32[1536]{0:T(1024)S(1)}, u32[]{:S(2)}) copy-start(f32[1536]{0:T(1024)S(1)} %convert_element_type.214) | copy-start | bytes 18436
  40.7 90.0 %copy-start.53 = (f32[1536]{0:T(1024)}, f32[1536]{0:T(1024)S(1)}, u32[]{:S(2)}) copy-start(f32[1536]{0:T(1024)S(1)} %convert_element_type.213) | copy-start | bytes 18436
  40.8 171.5 %copy-start.68 = (f32[1536]{0:T(1024)}, f32[1536]{0:T(1024)S(1)}, u32[]{:S(2)}) copy-start(f32[1536]{0:T(1024)S(1)} %convert_element_type.224) | copy-start | bytes 18436
  41.1 89.6 %copy-start.55 = (f32[384]{0:T(512)}, f32[384]{0:T(512)S(1)}, u32[]{:S(2)}) copy-start(f32[384]{0:T(512)S(1)} %broadcast_multiply_fusion.2) | copy-start | bytes 4612
  41.6 12.5 copy-start.57
  41.6 89.2 %copy-start.61 = (f32[384]{0:T(512)}, f32[384]{0:T(512)S(1)}, u32[]{:S(2)}) copy-start(f32[384]{0:T(512)S(1)} %fusion.52) | copy-start | bytes 4612
  42.4 110.7 %copy-start.48 = (f32[384,16]{0,1:T(8,128)}, f32[384,16]{0,1:T(8,128)S(1)}, u32[]{:S(2)}) copy-start(f32[384,16]{0,1:T(8,128)S(1)} %get-tuple-element.161) | copy-start | bytes 73732
  148.4 6.8 copy-start.17
  153.1 8.8 copy-start.19
  155.2 6.7 copy-start.28
  155.2 6.7 copy-start.30
  155.2 6.7 copy-start.32
  155.2 6.7 copy-start.34
  161.9 7.7 copy-start.46
  161.9 7.7 copy-start.21
  169.6 9.4 copy-start.50
  186.0 31.4 %copy-start.59 = (f32[384]{0:T(512)}, f32[384]{0:T(512)S(1)}, u32[]{:S(2)}) copy-start(f32[384]{0:T(512)S(1)} %multiply_reduce_fusion.9) | copy-start | bytes 4612
  186.0 31.4 %copy-start.63 = (f32[384]{0:T(512)}, f32[384]{0:T(512)S(1)}, u32[]{:S(2)}) copy-start(f32[384]{0:T(512)S(1)} %fusion.53) | copy-start | bytes 4612
  258.5 344.2 %copy-start.3 = (f32[384,1536]{1,0:T(8,128)}, f32[384,1536]{1,0:T(8,128)S(1)}, u32[]{:S(2)}) copy-start(f32[384,1536]{1,0:T(8,128)S(1)} %get-tuple-element.169) | copy-start | bytes 7077892
  578.1 12.3 copy-start.82
  610.6 167.7 %reduce-scatter.16.cloned.1.call-start = ((), (), s32[]{:S(2)}) async-start(), calls=%async_computation.19 | async-start | bytes 5308416 | tf_op jit(solution)/shard_map/reduce_scatter | solution.py:151
  618.1 4.9 copy-start.9
  618.1 5.1 slice-start.4
  618.1 5.4 slice-start.5
  631.3 148.2 %reduce-scatter.18.cloned.1.call-start = ((), (), s32[]{:S(2)}) async-start(), calls=%async_computation.20 | async-start | bytes 5308416 | tf_op jit(solution)/shard_map/reduce_scatter | solution.py:151
  641.4 195.8 %reduce-scatter.14.cloned.1.call-start = ((), (), s32[]{:S(2)}) async-start(), calls=%async_computation.18 | async-start | bytes 5308416 | tf_op jit(solution)/shard_map/reduce_scatter | solution.py:151
  643.0 5.4 copy-start.60
  651.8 4.5 copy-start.16
  656.3 285.2 %reduce-scatter.12.cloned.1.call-start = ((), (), s32[]{:S(2)}) async-start(), calls=%async_computation.17 | async-start | bytes 15925248 | tf_op jit(solution)/shard_map/reduce_scatter | solution.py:151
  663.5 13.4 slice-start
  663.6 13.4 slice-start.1
  663.6 13.4 slice-start.2
  663.6 14.0 slice-start.3
  677.6 8.0 copy-start.20
  677.6 8.0 copy-start.33
  677.6 8.0 copy-start.35
  687.1 5.6 copy-start.49
  687.1 5.6 copy-start.52
  713.0 358.2 %reduce-scatter.26.cloned.1.call-start = ((), (), s32[]{:S(2)}) async-start(), calls=%async_computation.24 | async-start | bytes 21233664 | tf_op jit(solution)/shard_map/reduce_scatter | solution.py:174
  729.8 471.0 %reduce-scatter.24.cloned.1.call-start = ((), (), s32[]{:S(2)}) async-start(), calls=%async_computation.23 | async-start | bytes 21233664 | tf_op jit(solution)/shard_map/reduce_scatter | solution.py:174
  746.7 583.6 %reduce-scatter.22.cloned.1.call-start = ((), (), s32[]{:S(2)}) async-start(), calls=%async_computation.22 | async-start | bytes 21233664 | tf_op jit(solution)/shard_map/reduce_scatter | solution.py:174
  763.3 604.4 %reduce-scatter.28.cloned.1.call-start = ((), (), s32[]{:S(2)}) async-start(), calls=%async_computation.25 | async-start | bytes 442368
  764.5 10.2 copy-start.58
  778.2 977.1 %all-reduce.10.cloned.1.call-start = ((), (), s32[]{:S(2)}) async-start(), calls=%async_computation.26 | async-start | bytes 22413312 | tf_op jit(solution)/shard_map/psum | solution.py:314
  1330.4 4.7 copy-start.4
  1755.2 4.7 copy-start.45
  1755.2 5.7 copy-start.44
  1757.6 4.6 copy-start.39
  (43 other events, 86.4 us)
Sparse Core Ops, SparseCore 0:
  9.9 40.0 all-gather.12
  51.9 78.7 all-gather.8
  132.6 38.9 all-gather.10
  173.3 38.9 all-gather.14
  214.0 38.9 all-gather.16
  254.7 98.7 all-gather.20
  355.3 98.7 all-gather.18
  456.0 98.8 all-gather.22
  610.7 53.8 reduce-scatter.19
  668.3 53.8 reduce-scatter.15
  725.6 53.8 reduce-scatter.17
  783.2 53.8 reduce-scatter.13
  840.8 100.7 reduce-scatter.11
  945.0 126.1 reduce-scatter.25
  1074.6 126.0 reduce-scatter.23
  1204.2 126.0 reduce-scatter.21
  1333.8 33.7 reduce-scatter.27
  1371.0 384.2 all-reduce.9
where the time goes:
time: 1790 us; the launch traced here: 1780 us
  waiting for transfers between devices  1360 us (76%)
  matrix products  275 us (15%)
  other arithmetic  52.9 us (3%)
  local copies, waits for them, and re-layouts  43.1 us (2%)
  blocking collectives  32.6 us (2%)
    reduce_scatter x3, waiting for transfers between devices, ffn_reduce(): lax.psum_scatter(row_term(jnp.int32(0), row_total * lax.axis_size('grp'))...  389 us
    psum x1, waiting for transfers between devices, per_device(): lax.psum(grad_qkv.astype(jnp.bfloat16), 'rep').astype(jnp.float32)  378 us
    all_gather x2, waiting for transfers between devices, per_device(): pieces = lax.all_gather((w_gate, w_up), 'grp', axis=0, tiled=True)  180 us
    reduce_scatter x5, waiting for transfers between devices, reduce_rows(): lax.psum_scatter(row_term(jnp.int32(0), row_total * lax.axis_size('grp'))...  163 us
    all_gather x5, waiting for transfers between devices, project(): return dot_nt(activation, lax.all_gather(weight, 'grp', axis=0, tiled=True))  138 us
    all_gather x1, waiting for transfers between devices, per_device(): lax.all_gather(w_down, 'grp', axis=0, tiled=True)  86.7 us
    dot_general x8, matrix products, dot_nt(): lax.dot_general(left_side, right_side, (((1,), (1,)), ((), ())), preferre...  80.5 us
    dot_general x8, matrix products, dot_tn(): lax.dot_general(left_side, right_side, (((0,), (0,)), ((), ())), preferre...  77.7 us
  transfers between devices with their start and end apart: 18, of which 15 were waited for; matrix products, arithmetic and copies ran while one was open for 16% of the time, Pallas kernels for 0%

commit v1 on v0

--- a/solution.py
+++ b/solution.py
@@ -1,9 +1,14 @@
+import functools
 import math
 
 import jax
 import jax.numpy as jnp
 from jax import lax
+from jax.experimental import pallas as pl
+from jax.experimental.pallas import tpu as pltpu
 from jax.sharding import PartitionSpec as P
+
+MESH = pl.DeviceIdType.MESH
 
 D = 1536
 HEADS = 24
@@ -69,6 +74,14 @@
     )
 
 
+def dot(left_side, right_side):
+    return jnp.dot(left_side, right_side, preferred_element_type=jnp.float32)
+
+
+def part_grad(grad_cols, activation):
+    return dot_tn(grad_cols, activation).astype(jnp.bfloat16)
+
+
 def attend(queries, key_heads, value_heads):
     seq_len = queries.shape[0]
     span = min(seq_len, 512)
@@ -135,48 +148,520 @@
     return (d_query.reshape(queries.shape), d_key, d_value)
 
 
-def project(activation, weight):
-    return dot_nt(activation, lax.all_gather(weight, "grp", axis=0, tiled=True))
-
-
-def project_back(grad_cols, weight):
-    return jnp.dot(
-        grad_cols,
-        lax.all_gather(weight, "grp", axis=0, tiled=True),
-        preferred_element_type=jnp.float32,
-    )
-
-
-def reduce_rows(row_term, row_total):
-    return lax.psum_scatter(
-        row_term(jnp.int32(0), row_total * lax.axis_size("grp")).astype(jnp.bfloat16),
-        "grp",
-        scatter_dimension=0,
-        tiled=True,
-    ).astype(jnp.float32)
-
-
-def column_term(left_side, right_side):
-
-    def block_term(first_row, row_count):
-        return dot_tn(left_side, right_side)
-
-    return block_term
-
-
-def weight_grad(grad_cols, activation):
-    return reduce_rows(
-        column_term(grad_cols, activation), grad_cols.shape[1] // lax.axis_size("grp")
-    )
-
-
-def ffn_reduce(row_term, row_total):
-    return lax.psum_scatter(
-        row_term(jnp.int32(0), row_total * lax.axis_size("grp")).astype(jnp.bfloat16),
-        "grp",
-        scatter_dimension=0,
-        tiled=True,
-    ).astype(jnp.float32)
+def meet(peers, lower=None, upper=None, rep_index=None):
+    barrier = pltpu.get_barrier_semaphore()
+    for peer in peers:
+        pl.semaphore_signal(barrier, inc=1, device_id=peer, device_id_type=MESH)
+    if lower is not None:
+
+        @pl.when(rep_index > 0)
+        def _():
+            pl.semaphore_signal(barrier, inc=1, device_id=lower, device_id_type=MESH)
+
+        @pl.when(rep_index < 3)
+        def _():
+            pl.semaphore_signal(barrier, inc=1, device_id=upper, device_id_type=MESH)
+
+    expected = len(peers)
+    if lower is not None:
+        expected = expected + jnp.where(rep_index > 0, 1, 0) + jnp.where(rep_index < 3, 1, 0)
+    pl.semaphore_wait(barrier, expected)
+
+
+GATHER_WINDOW = 4
+
+
+def gather_kernel(pieces, *refs):
+    count = len(pieces)
+    sources = refs[:count]
+    fulls = refs[count : 2 * count]
+    send_sem, recv_sem, local_sem = refs[2 * count :]
+    me = lax.axis_index("grp")
+    plane = lax.axis_index("rep")
+    odd = lax.rem(plane, 2)
+    first_bit = 2 + 2 * odd
+    second_bit = 6 - first_bit
+    first = me ^ first_bit
+    second = me ^ second_bit
+    across = me ^ 6
+    first_dev = (first, plane)
+    second_dev = (second, plane)
+    rep_dev = (me, plane ^ 1)
+    mate_dev = (me ^ 1, plane)
+    meet([first_dev, second_dev, rep_dev, mate_dev])
+    total = sum(n for n, _ in pieces)
+
+    def each(i, body):
+        base = 0
+        for k, (n, rows) in enumerate(pieces):
+            if n == 1:
+
+                @pl.when(i == base)
+                def _(k=k, rows=rows):
+                    body(k, pl.ds(0, rows))
+
+            else:
+
+                @pl.when((i >= base) & (i < base + n))
+                def _(k=k, rows=rows, base=base):
+                    body(k, pl.ds(pl.multiple_of((i - base) * rows, 16), rows))
+
+            base += n
+
+    def push(k, cut, i, owner, lane, device, own=False):
+        src = sources[k].at[cut] if own else fulls[k].at[owner, cut]
+        return pltpu.make_async_remote_copy(
+            src_ref=src,
+            dst_ref=fulls[k].at[owner, cut],
+            send_sem=send_sem.at[lane, i],
+            recv_sem=recv_sem.at[lane, i],
+            device_id=device,
+            device_id_type=MESH,
+        )
+
+    def stage_own(i):
+        def body(k, cut):
+            push(k, cut, i, me, 0, first_dev, own=True).start()
+            push(k, cut, i, me, 3, mate_dev, own=True).start()
+            pltpu.make_async_copy(sources[k].at[cut], fulls[k].at[me, cut], local_sem.at[i]).start()
+
+        each(i, body)
+
+    def stage_first(i):
+        def body(k, cut):
+            push(k, cut, i, first, 0, first_dev).wait_recv()
+            push(k, cut, i, first, 1, second_dev).start()
+            push(k, cut, i, first, 2, rep_dev).start()
+            push(k, cut, i, first, 4, mate_dev).start()
+
+        each(i, body)
+
+    def stage_rest(i):
+        def body(k, cut):
+            push(k, cut, i, across, 1, second_dev).wait_recv()
+            push(k, cut, i, across, 5, mate_dev).start()
+            push(k, cut, i, second, 2, rep_dev).wait_recv()
+            push(k, cut, i, second, 6, mate_dev).start()
+
+        each(i, body)
+
+    def stage_end(i):
+        def body(k, cut):
+            pltpu.make_async_copy(
+                sources[k].at[cut], fulls[k].at[me, cut], local_sem.at[i]
+            ).wait()
+            push(k, cut, i, me, 0, first_dev, own=True).wait_send()
+            push(k, cut, i, first, 1, second_dev).wait_send()
+            push(k, cut, i, first, 2, rep_dev).wait_send()
+            push(k, cut, i, me, 3, mate_dev, own=True).wait()
+            push(k, cut, i, first, 4, mate_dev).wait()
+            push(k, cut, i, across, 5, mate_dev).wait()
+            push(k, cut, i, second, 6, mate_dev).wait()
+
+        each(i, body)
+
+    def step(t, carry):
+        for stage, lag in ((stage_own, 0), (stage_first, GATHER_WINDOW), (stage_rest, GATHER_WINDOW + 2)):
+            i = t - lag
+
+            @pl.when((i >= 0) & (i < total))
+            def _(stage=stage, i=i):
+                stage(i)
+
+        return carry
+
+    lax.fori_loop(0, total + GATHER_WINDOW + 2, step, 0)
+
+    def finish(i, carry):
+        stage_end(i)
+        return carry
+
+    lax.fori_loop(0, total, finish, 0)
+
+
+def gather_all(arrays, rows):
+    groups = lax.axis_size("grp")
+    if groups != 8 or lax.axis_size("rep") % 2 != 0:
+        return [lax.all_gather(a, "grp", axis=0) for a in arrays]
+    pieces = tuple((a.shape[0] // n, n) for a, n in zip(arrays, rows))
+    total = sum(n for n, _ in pieces)
+    hbm = pl.BlockSpec(memory_space=pltpu.HBM)
+    return pl.pallas_call(
+        functools.partial(gather_kernel, pieces),
+        out_shape=[jax.ShapeDtypeStruct((groups,) + a.shape, a.dtype) for a in arrays],
+        in_specs=[hbm] * len(arrays),
+        out_specs=[hbm] * len(arrays),
+        scratch_shapes=[
+            pltpu.SemaphoreType.DMA((7, total)),
+            pltpu.SemaphoreType.DMA((7, total)),
+            pltpu.SemaphoreType.DMA((total,)),
+        ],
+        compiler_params=pltpu.CompilerParams(collective_id=0, has_side_effects=True),
+    )(*arrays)
+
+
+CUT = 48
+FCUT = 96
+MATE_SLOTS = 6
+OWN_SLOTS = 3
+SUM_SLOTS = 8
+FFN_SLOTS = 12
+
+
+def reduce_kernel(pieces, ffn_count, *refs):
+    count = len(pieces)
+    parts = refs[:count]
+    ffn = refs[count : count + 3]
+    out_a, out_f = refs[count + 3 : count + 5]
+    (
+        mate_buf,
+        own_buf,
+        sums,
+        one_buf,
+        two_buf,
+        done,
+        ffn_buf,
+        low_a,
+        up_a,
+        low_f,
+        up_f,
+        mate_send,
+        mate_recv,
+        own_sem,
+        one_send,
+        one_recv,
+        two_send,
+        two_recv,
+        ffn_sem,
+        chain_send,
+        chain_recv,
+        out_sem,
+        credit,
+    ) = refs[count + 5 :]
+    me = lax.axis_index("grp")
+    plane = lax.axis_index("rep")
+    core = lax.rem(me, 2)
+    x = lax.rem(me // 2, 2)
+    y = me // 4
+    mate_dev = (me ^ 1, plane)
+    x_dev = (me ^ 2, plane)
+    y_dev = (me ^ 4, plane)
+    low_dev = (me, plane - 1)
+    up_dev = (me, plane + 1)
+    meet([mate_dev, x_dev, y_dev], low_dev, up_dev, plane)
+    total = sum(pieces)
+    chain_total = ffn_count + total
+
+    def each(i, body):
+        base = 0
+        for k, n in enumerate(pieces):
+
+            @pl.when((i >= base) & (i < base + n))
+            def _(k=k, base=base):
+                body(k, pl.ds(pl.multiple_of((i - base) * CUT, 16), CUT))
+
+            base += n
+
+    def mate_copy(k, cut, slot):
+        return pltpu.make_async_remote_copy(
+            src_ref=parts[k].at[:, :, 1 - core, cut],
+            dst_ref=mate_buf.at[slot],
+            send_sem=mate_send.at[slot],
+            recv_sem=mate_recv.at[slot],
+            device_id=mate_dev,
+            device_id_type=MESH,
+        )
+
+    def own_copy(k, cut, slot):
+        return pltpu.make_async_copy(
+            parts[k].at[:, :, core, cut], own_buf.at[slot], own_sem.at[slot]
+        )
+
+    def load(i):
+        @pl.when(i >= MATE_SLOTS)
+        def _():
+            pl.semaphore_wait(credit, 1)
+            mate_copy(0, pl.ds(0, CUT), lax.rem(i, MATE_SLOTS)).wait_send()
+
+        def body(k, cut):
+            mate_copy(k, cut, lax.rem(i, MATE_SLOTS)).start()
+            own_copy(k, cut, lax.rem(i, OWN_SLOTS)).start()
+
+        each(i, body)
+
+    def one_copy(i, slot, by_x):
+        return pltpu.make_async_remote_copy(
+            src_ref=sums.at[slot, :, 1 - x] if by_x else sums.at[slot, 1 - y],
+            dst_ref=one_buf.at[i],
+            send_sem=one_send.at[slot],
+            recv_sem=one_recv.at[i],
+            device_id=x_dev if by_x else y_dev,
+            device_id_type=MESH,
+        )
+
+    def two_copy(i, slot, by_x):
+        return pltpu.make_async_remote_copy(
+            src_ref=sums.at[slot, 1 - y, x] if by_x else sums.at[slot, y, 1 - x],
+            dst_ref=two_buf.at[i],
+            send_sem=two_send.at[slot],
+            recv_sem=two_recv.at[i],
+            device_id=y_dev if by_x else x_dev,
+            device_id_type=MESH,
+        )
+
+    def either(i, body):
+        @pl.when(lax.rem(i, 2) == 0)
+        def _():
+            body(True)
+
+        @pl.when(lax.rem(i, 2) == 1)
+        def _():
+            body(False)
+
+    def add(a, b):
+        return (a.astype(jnp.float32) + b.astype(jnp.float32)).astype(jnp.bfloat16)
+
+    def pair(i):
+        mate_slot, own_slot, slot = (
+            lax.rem(i, MATE_SLOTS),
+            lax.rem(i, OWN_SLOTS),
+            lax.rem(i, SUM_SLOTS),
+        )
+        mate_copy(0, pl.ds(0, CUT), mate_slot).wait_recv()
+        own_copy(0, pl.ds(0, CUT), own_slot).wait()
+        for u in range(2):
+            for v in range(2):
+                sums[slot, u, v] = add(own_buf[own_slot, u, v], mate_buf[mate_slot, u, v])
+
+        @pl.when(i + MATE_SLOTS < total)
+        def _():
+            pl.semaphore_signal(credit, inc=1, device_id=mate_dev, device_id_type=MESH)
+
+        either(i, lambda by_x: one_copy(i, slot, by_x).start())
+
+    def plane_one(i):
+        slot = lax.rem(i, SUM_SLOTS)
+
+        def body(by_x):
+            one_copy(i, slot, by_x).wait_recv()
+            for u in range(2):
+                if by_x:
+                    sums[slot, u, x] = add(sums[slot, u, x], one_buf[i, u])
+                else:
+                    sums[slot, y, u] = add(sums[slot, y, u], one_buf[i, u])
+            two_copy(i, slot, by_x).start()
+
+        either(i, body)
+
+    def plane_two(i):
+        slot = lax.rem(i, SUM_SLOTS)
+
+        def body(by_x):
+            two_copy(i, slot, by_x).wait_recv()
+            done[i] = add(sums[slot, y, x], two_buf[i])
+            one_copy(i, slot, by_x).wait_send()
+            two_copy(i, slot, by_x).wait_send()
+
+        either(i, body)
+
+    def ffn_load(j):
+        for k in range(3):
+
+            @pl.when(j // (ffn_count // 3) == k)
+            def _(k=k):
+                row = pl.multiple_of((j - k * (ffn_count // 3)) * FCUT, 16)
+                pltpu.make_async_copy(
+                    ffn[k].at[pl.ds(row, FCUT)],
+                    ffn_buf.at[lax.rem(j, FFN_SLOTS)],
+                    ffn_sem.at[lax.rem(j, FFN_SLOTS)],
+                ).start()
+
+    def ffn_wait(j):
+        pltpu.make_async_copy(
+            ffn[0].at[pl.ds(0, FCUT)],
+            ffn_buf.at[lax.rem(j, FFN_SLOTS)],
+            ffn_sem.at[lax.rem(j, FFN_SLOTS)],
+        ).wait()
+
+    def views(j, is_ffn):
+        if is_ffn:
+            rows = pl.ds(pl.multiple_of(j * FCUT, 16), FCUT)
+            return ffn_buf.at[lax.rem(j, FFN_SLOTS)], low_f.at[j], up_f.at[j], out_f.at[rows]
+        i = j - ffn_count
+        rows = pl.ds(pl.multiple_of(i * CUT, 16), CUT)
+        return done.at[i], low_a.at[i], up_a.at[i], out_a.at[rows]
+
+    def chain(j, lane, src, dst, device):
+        return pltpu.make_async_remote_copy(
+            src_ref=src,
+            dst_ref=dst,
+            send_sem=chain_send.at[lane, j],
+            recv_sem=chain_recv.at[lane, j],
+            device_id=device,
+            device_id_type=MESH,
+        )
+
+    def kinds(j, body):
+        @pl.when(j < ffn_count)
+        def _():
+            body(*views(j, True))
+
+        @pl.when(j >= ffn_count)
+        def _():
+            body(*views(j, False))
+
+    def inward(j):
+        @pl.when(j < ffn_count)
+        def _():
+            ffn_wait(j)
+
+        def body(mine, low, up, out):
+            @pl.when(plane == 0)
+            def _():
+                chain(j, 0, mine, low, up_dev).start()
+
+            @pl.when(plane == 3)
+            def _():
+                chain(j, 1, mine, up, low_dev).start()
+
+        kinds(j, body)
+
+    def middle(j):
+        def body(mine, low, up, out):
+            @pl.when(plane == 2)
+            def _():
+                chain(j, 1, mine, up, low_dev).wait_recv()
+                mine[...] = add(mine[...], up[...])
+                chain(j, 1, mine, up, low_dev).start()
+
+        kinds(j, body)
+
+    def root(j):
+        def body(mine, low, up, out):
+            @pl.when(plane == 1)
+            def _():
+                chain(j, 0, mine, low, up_dev).wait_recv()
+                chain(j, 1, mine, up, low_dev).wait_recv()
+                mine[...] = (
+                    mine[...].astype(jnp.float32)
+                    + low[...].astype(jnp.float32)
+                    + up[...].astype(jnp.float32)
+                ).astype(jnp.bfloat16)
+                chain(j, 0, mine, out, up_dev).start()
+                chain(j, 1, mine, out, low_dev).start()
+                pltpu.make_async_copy(mine, out, out_sem.at[j]).start()
+
+        kinds(j, body)
+
+    def outward(j):
+        def body(mine, low, up, out):
+            @pl.when(plane == 2)
+            def _():
+                chain(j, 0, mine, out, up_dev).wait_recv()
+                chain(j, 0, out, out, up_dev).start()
+
+        kinds(j, body)
+
+    def drain(j):
+        def body(mine, low, up, out):
+            @pl.when(plane == 0)
+            def _():
+                chain(j, 0, mine, low, up_dev).wait_send()
+                chain(j, 1, mine, out, low_dev).wait_recv()
+
+            @pl.when(plane == 3)
+            def _():
+                chain(j, 1, mine, up, low_dev).wait_send()
+                chain(j, 0, mine, out, up_dev).wait_recv()
+
+            @pl.when(plane == 1)
+            def _():
+                chain(j, 0, mine, out, up_dev).wait_send()
+                chain(j, 1, mine, out, low_dev).wait_send()
+                pltpu.make_async_copy(mine, out, out_sem.at[j]).wait()
+
+            @pl.when(plane == 2)
+            def _():
+                chain(j, 1, mine, up, low_dev).wait_send()
+                chain(j, 0, out, out, up_dev).wait_send()
+
+        kinds(j, body)
+
+    stages = (
+        (load, 0, total),
+        (ffn_load, 0, ffn_count),
+        (inward, 1, chain_total),
+        (pair, 1, total),
+        (plane_one, 3, total),
+        (middle, 3, chain_total),
+        (plane_two, 5, total),
+        (root, 5, chain_total),
+        (outward, 7, chain_total),
+        (drain, 9, chain_total),
+    )
+
+    def step(t, carry):
+        for stage, lag, limit in stages:
+            i = t - lag
+
+            @pl.when((i >= 0) & (i < limit))
+            def _(stage=stage, i=i):
+                stage(i)
+
+        return carry
+
+    lax.fori_loop(0, chain_total + 9, step, 0)
+    for i in range(max(total - MATE_SLOTS, 0), total):
+        mate_copy(0, pl.ds(0, CUT), i % MATE_SLOTS).wait_send()
+
+
+def reduce_all(parts, ffn):
+    pieces = tuple(p.shape[3] // CUT for p in parts)
+    total = sum(pieces)
+    wide = parts[0].shape[-1]
+    ffn_rows = sum(f.shape[0] for f in ffn)
+    ffn_count = ffn_rows // FCUT
+    chain_total = total + ffn_count
+    hbm = pl.BlockSpec(memory_space=pltpu.HBM)
+    low = jnp.bfloat16
+    dma = pltpu.SemaphoreType.DMA
+    return pl.pallas_call(
+        functools.partial(reduce_kernel, pieces, ffn_count),
+        out_shape=[
+            jax.ShapeDtypeStruct((total * CUT, wide), low),
+            jax.ShapeDtypeStruct((ffn_rows, wide), low),
+        ],
+        in_specs=[hbm] * (len(parts) + 3),
+        out_specs=[hbm] * 2,
+        scratch_shapes=[
+            pltpu.VMEM((MATE_SLOTS, 2, 2, CUT, wide), low),
+            pltpu.VMEM((OWN_SLOTS, 2, 2, CUT, wide), low),
+            pltpu.VMEM((SUM_SLOTS, 2, 2, CUT, wide), low),
+            pltpu.VMEM((total, 2, CUT, wide), low),
+            pltpu.VMEM((total, CUT, wide), low),
+            pltpu.VMEM((total, CUT, wide), low),
+            pltpu.VMEM((FFN_SLOTS, FCUT, wide), low),
+            pltpu.VMEM((total, CUT, wide), low),
+            pltpu.VMEM((total, CUT, wide), low),
+            pltpu.VMEM((ffn_count, FCUT, wide), low),
+            pltpu.VMEM((ffn_count, FCUT, wide), low),
+            dma((MATE_SLOTS,)),
+            dma((MATE_SLOTS,)),
+            dma((OWN_SLOTS,)),
+            dma((SUM_SLOTS,)),
+            dma((total,)),
+            dma((SUM_SLOTS,)),
+            dma((total,)),
+            dma((FFN_SLOTS,)),
+            dma((2, chain_total)),
+            dma((2, chain_total)),
+            dma((chain_total,)),
+            pltpu.SemaphoreType.REGULAR,
+        ],
+        compiler_params=pltpu.CompilerParams(
+            collective_id=1, has_side_effects=True, vmem_limit_bytes=60 * 1024 * 1024
+        ),
+    )(*parts, *ffn)
 
 
 def per_device(
@@ -203,23 +688,24 @@
     tokens = inputs[0].astype(jnp.float32)
     seq_len = tokens.shape[0]
     cond_rows = conditioning[0]
-    gain_one, shift_one, gain_two, shift_two, gain_three, shift_three = (
-        lax.all_gather(norm1_gain, "grp", axis=0, tiled=True),
-        lax.all_gather(norm1_shift, "grp", axis=0, tiled=True),
-        lax.all_gather(norm2_gain, "grp", axis=0, tiled=True),
-        lax.all_gather(norm2_shift, "grp", axis=0, tiled=True),
-        lax.all_gather(norm3_gain, "grp", axis=0, tiled=True),
-        lax.all_gather(norm3_shift, "grp", axis=0, tiled=True),
-    )
-    gain_one = gain_one.astype(jnp.float32)
-    shift_one = shift_one.astype(jnp.float32)
-    gain_two = gain_two.astype(jnp.float32)
-    shift_two = shift_two.astype(jnp.float32)
-    gain_three = gain_three.astype(jnp.float32)
-    shift_three = shift_three.astype(jnp.float32)
+    norms = jnp.stack(
+        [norm1_gain, norm1_shift, norm2_gain, norm2_shift, norm3_gain, norm3_shift], axis=0
+    )
+    own_width = norms.shape[1]
+    norms = jnp.pad(norms, ((0, 10), (0, -own_width % 128)))
+    norms, full_qkv, full_out, full_kv2, full_query2, full_out2 = gather_all(
+        [norms, w_qkv, w_out, w_kv2, w_query2, w_out2], [16, 48, 48, 96, 48, 48]
+    )
+    norms = jnp.swapaxes(norms[:, :6, :own_width], 0, 1).reshape(6, D).astype(jnp.float32)
+    gain_one, shift_one, gain_two, shift_two, gain_three, shift_three = (norms[k] for k in range(6))
+    full_qkv = full_qkv.reshape(-1, D)
+    full_out = full_out.reshape(-1, D)
+    full_kv2 = full_kv2.reshape(-1, cond_rows.shape[1])
+    full_query2 = full_query2.reshape(-1, D)
+    full_out2 = full_out2.reshape(-1, D)
     cosine, sin_table = angles(positions[0], HD)
     act_one = layer_norm(tokens, gain_one, shift_one).astype(jnp.bfloat16)
-    qkv_rows = project(act_one, w_qkv)
+    qkv_rows = dot_nt(act_one, full_qkv)
     queries = rotate(qkv_rows[:, :D].reshape(seq_len, HEADS, HD), cosine, sin_table).astype(
         jnp.bfloat16
     )
@@ -229,50 +715,43 @@
     value_heads = qkv_rows[:, 2 * D :].reshape(seq_len, HEADS, HD).astype(jnp.bfloat16)
     attended, log_one = attend(queries, key_heads, value_heads)
     flat_one = attended.reshape(seq_len, D)
-    section_one = tokens + project(flat_one, w_out)
+    section_one = tokens + dot_nt(flat_one, full_out)
     act_two = layer_norm(section_one, gain_two, shift_two).astype(jnp.bfloat16)
-    query_two = project(act_two, w_query2).astype(jnp.bfloat16).reshape(seq_len, HEADS, HD)
-    kv_two = project(cond_rows, w_kv2).astype(jnp.bfloat16)
+    query_two = dot_nt(act_two, full_query2).astype(jnp.bfloat16).reshape(seq_len, HEADS, HD)
+    kv_two = dot_nt(cond_rows, full_kv2).astype(jnp.bfloat16)
     key_two = kv_two[:, :D].reshape(NC, HEADS, HD)
     value_two = kv_two[:, D:].reshape(NC, HEADS, HD)
     attended_two, log_two = attend(query_two, key_two, value_two)
     flat_two = attended_two.reshape(seq_len, D)
-    section_two = section_one + project(flat_two, w_out2)
+    section_two = section_one + dot_nt(flat_two, full_out2)
     act_three = layer_norm(section_two, gain_three, shift_three).astype(jnp.bfloat16)
-    pieces = lax.all_gather((w_gate, w_up), "grp", axis=0, tiled=True)
-    gate_pre = dot_nt(act_three, pieces[0])
-    up_pre = dot_nt(act_three, pieces[1])
-    hidden = swiglu(gate_pre, up_pre).astype(jnp.bfloat16)
-    mlp_out = jnp.dot(
-        hidden,
-        lax.all_gather(w_down, "grp", axis=0, tiled=True),
-        preferred_element_type=jnp.float32,
-    )
-    outputs = (section_two + mlp_out).astype(jnp.bfloat16)
     grad_out = cotangent[0].astype(jnp.float32) * slot_valid[0].astype(jnp.float32)
     grad_mlp = grad_out.astype(jnp.bfloat16)
-    d_hidden = dot_nt(grad_mlp, lax.all_gather(w_down, "grp", axis=0, tiled=True))
+    all_grad = lax.all_gather(grad_mlp, "grp", axis=0, tiled=True)
+    all_act = lax.all_gather(act_three, "grp", axis=0, tiled=True)
+    gate_pre = dot_nt(all_act, w_gate)
+    up_pre = dot_nt(all_act, w_up)
+    hidden = swiglu(gate_pre, up_pre).astype(jnp.bfloat16)
+    mlp_part = dot(hidden, w_down).astype(jnp.bfloat16)
+    mlp_out = lax.psum_scatter(mlp_part, "grp", scatter_dimension=0, tiled=True)
+    outputs = (section_two + mlp_out.astype(jnp.float32)).astype(jnp.bfloat16)
+    d_hidden = dot_nt(all_grad, w_down)
     d_gate_full, d_up_full = swiglu_back(gate_pre, up_pre, d_hidden)
     d_gate = d_gate_full.astype(jnp.bfloat16)
     d_up = d_up_full.astype(jnp.bfloat16)
-    pieces = (
-        lax.all_gather(w_gate, "grp", axis=0, tiled=True),
-        lax.all_gather(w_up, "grp", axis=0, tiled=True),
-    )
-    d_norm3 = jnp.dot(d_gate, pieces[0], preferred_element_type=jnp.float32) + jnp.dot(
-        d_up, pieces[1], preferred_element_type=jnp.float32
-    )
-    rows_hidden = w_gate.shape[0]
-    grad_gate = ffn_reduce(column_term(d_gate, act_three), rows_hidden)
-    grad_up = ffn_reduce(column_term(d_up, act_three), rows_hidden)
-    grad_down = ffn_reduce(column_term(hidden, grad_mlp), rows_hidden)
+    d_norm3_part = (dot(d_gate, w_gate) + dot(d_up, w_up)).astype(jnp.bfloat16)
+    d_norm3 = lax.psum_scatter(d_norm3_part, "grp", scatter_dimension=0, tiled=True)
+    d_norm3 = d_norm3.astype(jnp.float32)
+    grad_gate = dot_tn(d_gate, all_act).astype(jnp.bfloat16)
+    grad_up = dot_tn(d_up, all_act).astype(jnp.bfloat16)
+    grad_down = dot_tn(hidden, all_grad).astype(jnp.bfloat16)
     d_ln_three, d_gain_three, d_shift_three = norm_back(
         section_two, gain_three, shift_three, d_norm3
     )
     d_section_two = grad_out + d_ln_three
     d_cross = d_section_two.astype(jnp.bfloat16)
-    grad_out_two = weight_grad(d_cross, flat_two)
-    d_att_two = project_back(d_cross, w_out2).astype(jnp.bfloat16).reshape(seq_len, HEADS, HD)
+    grad_out_two = part_grad(d_cross, flat_two)
+    d_att_two = dot(d_cross, full_out2).astype(jnp.bfloat16).reshape(seq_len, HEADS, HD)
     d_query_full, d_key_full, d_value_full = attend_back(
         query_two, key_two, value_two, log_two, d_att_two
     )
@@ -280,14 +759,14 @@
     d_kv_two = jnp.concatenate(
         [d_key_full.reshape(NC, D), d_value_full.reshape(NC, D)], axis=1
     ).astype(jnp.bfloat16)
-    grad_query_two = weight_grad(d_query_two, act_two)
-    grad_kv_two = weight_grad(d_kv_two, cond_rows)
-    d_norm2 = project_back(d_query_two, w_query2)
+    grad_query_two = part_grad(d_query_two, act_two)
+    grad_kv_two = part_grad(d_kv_two, cond_rows)
+    d_norm2 = dot(d_query_two, full_query2)
     d_ln_two, d_gain_two, d_shift_two = norm_back(section_one, gain_two, shift_two, d_norm2)
     d_section_one = d_section_two + d_ln_two
     d_attn = d_section_one.astype(jnp.bfloat16)
-    grad_out_one = weight_grad(d_attn, flat_one)
-    d_att = project_back(d_attn, w_out).astype(jnp.bfloat16).reshape(seq_len, HEADS, HD)
+    grad_out_one = part_grad(d_attn, flat_one)
+    d_att = dot(d_attn, full_out).astype(jnp.bfloat16).reshape(seq_len, HEADS, HD)
     d_query, d_key, d_value = attend_back(queries, key_heads, value_heads, log_one, d_att)
     d_qkv = jnp.concatenate(
         [
@@ -297,47 +776,68 @@
         ],
         axis=1,
     ).astype(jnp.bfloat16)
-    grad_qkv = weight_grad(d_qkv, act_one)
-    d_norm1 = project_back(d_qkv, w_qkv)
+    grad_qkv = part_grad(d_qkv, act_one)
+    d_norm1 = dot(d_qkv, full_qkv)
     d_ln_one, d_gain_one, d_shift_one = norm_back(tokens, gain_one, shift_one, d_norm1)
     d_tokens = d_section_one + d_ln_one
     norm_stack = jnp.stack(
-        [d_gain_one, d_shift_one, d_gain_two, d_shift_two, d_gain_three, d_shift_three], axis=1
-    )
-
-    def norm_term(first_row, row_count):
-        return norm_stack
-
-    norm_shard = reduce_rows(norm_term, norm1_gain.shape[0])
-    summed = (
-        lax.psum(norm_shard.astype(jnp.bfloat16), "rep").astype(jnp.float32),
-        lax.psum(grad_qkv.astype(jnp.bfloat16), "rep").astype(jnp.float32),
-        lax.psum(grad_out_one.astype(jnp.bfloat16), "rep").astype(jnp.float32),
-        lax.psum(grad_query_two.astype(jnp.bfloat16), "rep").astype(jnp.float32),
-        lax.psum(grad_kv_two.astype(jnp.bfloat16), "rep").astype(jnp.float32),
-        lax.psum(grad_out_two.astype(jnp.bfloat16), "rep").astype(jnp.float32),
-        lax.psum(grad_gate.astype(jnp.bfloat16), "rep").astype(jnp.float32),
-        lax.psum(grad_up.astype(jnp.bfloat16), "rep").astype(jnp.float32),
-        lax.psum(grad_down.astype(jnp.bfloat16), "rep").astype(jnp.float32),
-    )
-    norm_total = summed[0]
+        [d_gain_one, d_shift_one, d_gain_two, d_shift_two, d_gain_three, d_shift_three], axis=0
+    ).astype(jnp.bfloat16)
+    groups = lax.axis_size("grp")
+    attention_parts = [grad_qkv, grad_out_one, grad_query_two, grad_out_two, grad_kv_two]
+    ffn_parts = [grad_gate, grad_up, grad_down]
+    if groups == 8 and lax.axis_size("rep") == 4:
+        norm_part = jnp.swapaxes(norm_stack.reshape(6, groups, own_width), 0, 1)
+        norm_part = norm_part.reshape(groups, 1, 6 * own_width)
+        norm_part = jnp.pad(norm_part, ((0, 0), (0, CUT - 1), (0, D - 6 * own_width)))
+        kv2_rows = grad_kv_two.shape[0] // groups // 2
+        kv2_part = grad_kv_two.reshape(groups, 2, kv2_rows, D // 2)
+        kv2_part = jnp.swapaxes(kv2_part, 1, 2).reshape(groups, kv2_rows, D)
+        parts = attention_parts[:4] + [kv2_part, norm_part]
+        parts = [p.reshape(2, 2, 2, -1, D) for p in parts]
+        total_a, total_f = reduce_all(parts, ffn_parts)
+        ends = []
+        for p in parts:
+            ends.append((ends[-1] if ends else 0) + p.shape[3])
+        pieces = [total_a[e - p.shape[3] : e] for e, p in zip(ends, parts)]
+        norm_total = pieces[5][0, : 6 * own_width].reshape(6, own_width)
+        kv2_total = jnp.swapaxes(pieces[4].reshape(kv2_rows, 2, D // 2), 0, 1)
+        pieces[4] = kv2_total.reshape(2 * kv2_rows, D // 2)
+        attention_sums = pieces[:5]
+        own = w_gate.shape[0]
+        ffn_sums = [total_f[k * own : (k + 1) * own] for k in range(3)]
+    else:
+        norm_total = lax.psum(norm_stack, ("grp", "rep"))
+        norm_total = lax.dynamic_slice_in_dim(
+            norm_total, lax.axis_index("grp") * own_width, own_width, axis=1
+        )
+        attention_sums = [
+            lax.psum_scatter(g, "grp", scatter_dimension=0, tiled=True) for g in attention_parts
+        ]
+        attention_sums = [lax.psum(g, "rep") for g in attention_sums]
+        ffn_sums = [lax.psum(g, "rep") for g in ffn_parts]
+    norm_total = norm_total.astype(jnp.float32)
+    grad_qkv, grad_out_one, grad_query_two, grad_out_two, grad_kv_two = (
+        g.astype(jnp.float32) for g in attention_sums
+    )
+    grad_gate, grad_up, grad_down = (g.astype(jnp.float32) for g in ffn_sums)
     return (
         outputs[None],
         d_tokens[None],
-        norm_total[:, 0],
-        norm_total[:, 1],
-        norm_total[:, 2],
-        norm_total[:, 3],
-        norm_total[:, 4],
-        norm_total[:, 5],
-        summed[1],
-        summed[2],
-        summed[3],
-        summed[4],
-        summed[5],
-        summed[6],
-        summed[7],
-        summed[8],
+        norm_total[0],
+        norm_total[1],
+        norm_total[2],
+        norm_total[3],
+        norm_total[4],
+        norm_total[5],
+        grad_qkv,
+        grad_out_one,
+        grad_query_two,
+        grad_kv_two,
+        grad_out_two,
+        grad_gate,
+        grad_up,
+        grad_down,
     )
 
 

time: 1790 us -> 1040 us (0.58)
  waiting for transfers between devices: 1360 us -> 200 us
  Pallas kernels: 0 us -> 416 us
  local copies, waits for them, and re-layouts: 43.1 us -> 80.3 us
  blocking collectives: 32.6 us -> 0 us
  matrix products: 275 us -> 249 us
    reduce_scatter x8 -> x2, waiting for transfers between devices: 552 us -> 105 us  [the longest x1 76.5 us: per_device(): mlp_out = lax.psum_scatter(mlp_part, 'grp', scatter_dimension=0, tiled=True)]
    pallas_call x0 -> x2, Pallas kernels: none -> 416 us  [the longest x1 284 us: reduce_all(): pl.pallas_call(functools.partial(reduce_kernel, pieces, ffn_count), out_s...]
    psum x1 -> x0, waiting for transfers between devices: 378 us -> none  [per_device(): lax.psum(grad_qkv.astype(jnp.bfloat16), 'rep').astype(jnp.float32)]
    all_gather x8 -> x2, waiting for transfers between devices: 404 us -> 94.6 us  [the longest x1 57 us: per_device(): all_act = lax.all_gather(act_three, 'grp', axis=0, tiled=True)]
    unnamed x1 -> x0, blocking collectives: 24.5 us -> none
    unnamed x19 -> x4, waiting for transfers between devices: 24.2 us -> 0.07 us
  transfers between devices with their start and end apart: 18 -> 4, of which waited for: 15 -> 4; matrix products, arithmetic and copies ran while one was open for 16% -> 7% of each run, Pallas kernels for 0% -> 0%
where the time goes in v1:
time: 1040 us; the launch traced here: 1020 us
  Pallas kernels  416 us (40%)
  matrix products  249 us (24%)
  waiting for transfers between devices  200 us (19%)
  local copies, waits for them, and re-layouts  80.3 us (8%)
  other arithmetic  60.5 us (6%)
  between operations  15.8 us (2%)
    pallas_call x1, Pallas kernels, reduce_all(): pl.pallas_call(functools.partial(reduce_kernel, pieces, ffn_count), out_s...  284 us
    pallas_call x1, Pallas kernels, gather_all(): pl.pallas_call(functools.partial(gather_kernel, pieces), out_shape=[jax.S...  132 us
    reduce_scatter x1, waiting for transfers between devices, per_device(): mlp_out = lax.psum_scatter(mlp_part, 'grp', scatter_dimension=0, tiled=True)  76.5 us
    dot_general x8, matrix products, dot_tn(): lax.dot_general(left_side, right_side, (((0,), (0,)), ((), ())), preferre...  68.1 us
    dot_general x8, matrix products, dot_nt(): lax.dot_general(left_side, right_side, (((1,), (1,)), ((), ())), preferre...  64.2 us
    dot_general x7, matrix products, dot(): return jnp.dot(left_side, right_side, preferred_element_type=jnp.float32)  63.2 us
    all_gather x1, waiting for transfers between devices, per_device(): all_act = lax.all_gather(act_three, 'grp', axis=0, tiled=True)  57 us
    all_gather x1, waiting for transfers between devices, per_device(): all_grad = lax.all_gather(grad_mlp, 'grp', axis=0, tiled=True)  37.6 us
  transfers between devices with their start and end apart: 4, of which 4 were waited for; matrix products, arithmetic and copies ran while one was open for 7% of the time, Pallas kernels for 0%

profile of v1, /device:TPU:24, one launch (start us, length us, event | category | flops | bytes accessed | tf_op | source)
XLA Modules:
  0.0 1021.0 jit_solution(2245026496279689164)
XLA Ops:
  13.5 1.5 convert_reduce_fusion
  15.6 1.7 fusion.33
  19.8 131.9 %shard_map.306 = (bf16[8,16,256]{2,1,0:T(8,128)(2,1)}, bf16[8,576,1536]{2,1,0:T(8,128)(2,1)}, bf16[8,192,1536]{2,1,0:T(8,128)(2,1)}, bf16[8,384,768]{2,1,0:T(8,1...) custom-call(bf16[16,256]{1,0:T(8,128)(2,1)} %pad.8.refs_0_, bf16[576,1536]{1,0:T(8,128)(2,1)} %refs_1_.1, ...), custom_call_target="tpu_custom_call" | custom-call | tf_op jit(solution)/shard_map/pallas_call | solution.py:289
  155.4 9.2 fusion.54
  165.7 2.5 fusion.88
  172.4 4.0 fusion.12
  177.4 2.2 copy.82
  179.6 2.2 copy.81
  181.8 3.0 copy.60
  184.8 2.4 copy.59
  187.2 2.2 slice.245
  189.4 3.0 copy.61
  193.8 1.5 fusion.70
  195.4 1.9 subtract_convert_fusion.3
  197.3 6.4 multiply_reduce_fusion.1
  203.8 7.5 fusion
  211.4 8.3 fusion.43
  219.7 2.1 fusion.91
  223.5 3.1 convolution_convert_fusion.12
  226.6 1.7 copy.63
  228.3 2.7 multiply_reduce_fusion.3
  231.9 1.6 copy-done.2
  233.6 1.4 fusion.42
  236.6 2.2 fusion.92
  240.2 1.5 add_convert_fusion.2
  243.7 57.0 %all-gather.3.cloned.1.call-done = bf16[3072,1536]{1,0:T(8,128)(2,1)} async-done(((bf16[384,1536]{1,0:T(8,128)(2,1)}), bf16[3072,1536]{1,0:T(8,128)(2,1)}) %all-gather.3.cloned.1.call-update) | async-done | bytes 9437200 | tf_op jit(solution)/shard_map/all_gather | solution.py:731
  300.7 13.6 %fusion.94 = f32[3072,768]{1,0:T(8,128)} fusion(bf16[3072,1536]{1,0:T(8,128)(2,1)} %all-gather.3.cloned.1.call-done, bf16[768,1536]{1,0:T(8,128)(2,1)} %param.36), kind=kOutput, calls=%fused_computation.201 | convolution fusion | flops 7247757312 | bytes 21233664 | tf_op jit(solution)/shard_map/dot_general | solution.py:66
  314.3 10.2 fusion.93
  324.5 37.6 %all-gather.5.cloned.1.call-done = bf16[3072,1536]{1,0:T(8,128)(2,1)} async-done(((bf16[384,1536]{1,0:T(8,128)(2,1)}), bf16[3072,1536]{1,0:T(8,128)(2,1)}) %all-gather.5.cloned.1.call-update) | async-done | bytes 9437200 | tf_op jit(solution)/shard_map/all_gather | solution.py:730
  362.0 19.9 %multiply_convert_fusion.1 = (bf16[3072,768]{1,0:T(8,128)(2,1)}, bf16[3072,768]{1,0:T(8,128)(2,1)}, bf16[3072,768]{1,0:T(8,128)(2,1)}) fusion(f32[3072,768]{1,0:T(8,128)} %fusion.93, f32[3072,768]{1,0:T(8,128)} %fusion.94, bf16[3072,1536]{1,0:T(8,128)(2,1)} %all-gather.5.cloned.1.call-done, bf16[768,1536]{1,0:T(8,128)(2,1)S(1)} %copy-done), kind=kOutput, calls=%fused_computation.14 | convolution fusion | flops 7285506048 | bytes 44826624 | tf_op jit(solution)/shard_map/dot_general | solution.py:66
  381.9 13.9 %fusion.95 = f32[3072,1536]{1,0:T(8,128)} fusion(bf16[3072,768]{1,0:T(8,128)(2,1)} %get-tuple-element.142, bf16[768,1536]{1,0:T(8,128)(2,1)} %param.35), kind=kOutput, calls=%fused_computation.202 | convolution fusion | flops 7247757312 | bytes 25952256 | tf_op jit(solution)/shard_map/dot_general | solution.py:78
  395.8 14.4 %add_convert_fusion = bf16[3072,1536]{1,0:T(8,128)(2,1)} fusion(f32[3072,1536]{1,0:T(8,128)} %fusion.95, bf16[3072,768]{1,0:T(8,128)(2,1)S(1)} %copy-done.84, bf16[768,1536]{1,0:T(8,128)(2,1)S(1)} %copy-done.79), kind=kOutput, calls=%fused_computation.1 | convolution fusion | flops 7257194496 | bytes 35389440 | tf_op jit(solution)/shard_map/dot_general | solution.py:78
  410.2 12.2 %convolution_convert_fusion.1 = bf16[3072,1536]{1,0:T(8,128)(2,1)} fusion(bf16[3072,768]{1,0:T(8,128)(2,1)} %get-tuple-element.143, bf16[768,1536]{1,0:T(8,128)(2,1)S(1)} %copy-done), kind=kOutput, calls=%fused_computation.10 | convolution fusion | flops 7252475904 | bytes 16515072 | tf_op jit(solution)/shard_map/dot_general | solution.py:78
  424.5 13.9 %convolution_convert_fusion.7.refs_8_ = bf16[768,1536]{1,0:T(8,128)(2,1)} fusion(bf16[3072,768]{1,0:T(8,128)(2,1)} %get-tuple-element.143, bf16[3072,1536]{1,0:T(8,128)(2,1)} %all-gather.5.cloned.1.call-done), kind=kOutput, calls=%fused_computation.44 | convolution fusion | flops 7248936960 | bytes 16515072 | tf_op jit(solution)/shard_map/dot_general | solution.py:72
  438.4 10.5 %convolution_convert_fusion.8.refs_7_ = bf16[768,1536]{1,0:T(8,128)(2,1)} fusion(bf16[3072,768]{1,0:T(8,128)(2,1)} %get-tuple-element.141, bf16[3072,1536]{1,0:T(8,128)(2,1)S(1)} %bitcast.215), kind=kOutput, calls=%fused_computation.45 | convolution fusion | flops 7248936960 | bytes 16515072 | tf_op jit(solution)/shard_map/dot_general | solution.py:72
  448.9 9.2 convolution_convert_fusion.9.refs_6_
  458.1 28.7 %reduce-scatter.5.cloned.1.call-done = bf16[384,1536]{1,0:T(8,128)(2,1)} async-done(((bf16[3072,1536]{1,0:T(8,128)(2,1)}), bf16[384,1536]{1,0:T(8,128)(2,1)}) %reduce-scatter.5.cloned.1.call-update) | async-done | bytes 1179664 | tf_op jit(solution)/shard_map/reduce_scatter | solution.py:743
  486.8 2.8 fusion.32
  490.2 76.5 %reduce-scatter.3.cloned.1.call-done = bf16[384,1536]{1,0:T(8,128)(2,1)} async-done(((bf16[3072,1536]{1,0:T(8,128)(2,1)}), bf16[384,1536]{1,0:T(8,128)(2,1)}) %reduce-scatter.3.cloned.1.call-update) | async-done | bytes 1179664 | tf_op jit(solution)/shard_map/reduce_scatter | solution.py:736
  566.7 3.3 fusion.87
  571.4 4.4 convolution_convert_fusion.11
  575.8 4.3 convolution_convert_fusion.2
  580.9 4.7 fusion.48
  585.6 3.8 multiply_reduce_fusion.2
  590.8 2.1 multiply_convert_fusion.5
  594.6 5.5 multiply_reduce_fusion.4
  600.0 4.9 convolution_convert_fusion.3
  608.5 2.0 convolution_convert_fusion.10
  610.6 4.3 convolution_convert_fusion.4
  615.7 8.9 fusion.44
  624.5 10.4 %multiply_reduce_fusion = (f32[24,384]{1,0:T(8,128)S(1)}, f32[24,384,384]{1,2,0:T(8,128)}) fusion(f32[24,384,384]{1,2,0:T(8,128)} %get-tuple-element.178, f32[24,384]{1,0:T(8,128)S(1)} %copy-done.40, bf16[384,24,64]{0,2,1:T(8,128)(2,1)S(1)} %bitcast.172, bf16[384,24,64]{0,2,1:T(8,128)(2,1)S(1)} %bitcast.188), kind=kOutput, calls=%fused_computation.3 | convolution fusion | flops 467131392 | bytes 30744576 | tf_op jit(solution)/shard_map/while/body/eval_jaxpr/qhd,khd->hqk/dot_general | solution.py:122
  635.0 7.3 multiply_convert_fusion
  642.4 2.6 multiply_bitcast_fusion
  649.0 10.9 %fusion.85 = (bf16[1536]{0:T(1024)(128)(2,1)}, f32[384]{0:T(512)}, f32[384,1536]{1,0:T(8,128)}) fusion(f32[1536]{0:T(1024)S(1)} %copy-done.54, f32[384]{0:T(512)S(1)} %copy-done.59, bf16[1,384,1536]{2,1,0:T(8,128)(2,1)S(1)} %copy-done.8, bf16[4608,1536]{1,0:T(8,128)(2,1)} %bitcast.213, bf16[384,1536]{0,1:T(8,128)(2,1)S(1)} %bitcast.194, ...), kind=kOutput, calls=%fused_computation.192 | convolution fusion | flops 5449971712 | bytes 21245952 | tf_op jit(solution)/shard_map/dot_general | solution.py:78
  659.9 16.1 %convolution_convert_fusion = bf16[4608,1536]{1,0:T(8,128)(2,1)} fusion(bf16[384,1536]{0,1:T(8,128)(2,1)S(1)} %bitcast.195, bf16[384,1536]{0,1:T(8,128)(2,1)S(1)} %bitcast.200, bf16[384,1536]{0,1:T(8,128)(2,1)S(1)} %bitcast.198, bf16[1,384,1536]{2,1,0:T(8,128)(2,1)S(1)} %copy-done.8, f32[1536]{0:T(1024)S(1)} %copy-done.71, f32[384]{0:T(512)S(1)} %copy-done.68, ...), kind=kOutput, calls=%fused_computation | convolution fusion | flops 5457051648 | bytes 18889728 | tf_op jit(solution)/shard_map/dot_general | solution.py:72
  678.6 4.9 convolution_convert_fusion.5
  683.5 9.4 copy.85
  692.9 11.3 %reshape_reshape.16.refs_4_ = bf16[2,2,2,192,1536]{4,3,2,1,0:T(8,128)(2,1)} reshape(bf16[8,192,2,768]{3,2,1,0:T(2,128)(2,1)} %bitcast.169) | data formatting | bytes 9437184 | tf_op jit(solution)/shard_map/reshape;reshape | solution.py:797
  704.3 2.7 fusion.30
  708.3 283.8 %shard_map.307 = (bf16[1392,1536]{1,0:T(8,128)(2,1)}, bf16[2304,1536]{1,0:T(8,128)(2,1)}) custom-call(bf16[2,2,2,576,1536]{4,3,2,1,0:T(8,128)(2,1)} %bitcast.170, bf16[2,2,2,192,1536]{4,3,2,1,0:T(8,128)(2,1)} %bitcast.186, bf16[2,2,2,192,1536]{4,3,2,1,0:T(8,128)(2,1)} %bitcast.185, bf16[2,2,2,192,1536]{4,3,2,1,0:T(8,128)(2,1)} %bitcast.184, ...), custom_call_target="tpu_custom_call" | custom-call | tf_op jit(solution)/shard_map/pallas_call | solution.py:628
  992.9 3.9 slice_convert_fusion.4
  996.8 2.0 slice_convert_fusion.9
  1000.4 2.2 add_bitcast_fusion
  1005.1 9.0 slice_convert_fusion.1
  (294 shorter events, 52.5 us)
Async XLA Ops:
  7.2 354.9 %copy-start = (bf16[768,1536]{1,0:T(8,128)(2,1)S(1)}, bf16[768,1536]{1,0:T(8,128)(2,1)}, u32[]{:S(2)}) copy-start(bf16[768,1536]{1,0:T(8,128)(2,1)} %param.37) | copy-start | bytes 7077892
  7.2 293.5 %all-gather.3.cloned.1.call-start = ((), (), s32[]{:S(2)}) async-start(), calls=%async_computation.2 | async-start | bytes 10616832 | tf_op jit(solution)/shard_map/all_gather | solution.py:731
  17.9 137.5 %copy-start.7 = (bf16[1,384,1536]{2,1,0:T(8,128)(2,1)S(1)}, bf16[1,384,1536]{2,1,0:T(8,128)(2,1)}, u32[]{:S(2)}) copy-start(bf16[1,384,1536]{2,1,0:T(8,128)(2,1)} %param.19) | copy-start | bytes 3538948
  154.0 10.6 %copy-start.53 = (f32[1536]{0:T(1024)}, f32[1536]{0:T(1024)S(1)}, u32[]{:S(2)}) copy-start(f32[1536]{0:T(1024)S(1)} %mul.419) | copy-start | bytes 18436
  169.7 53.2 %copy-start.55 = (f32[1536]{0:T(1024)}, f32[1536]{0:T(1024)S(1)}, u32[]{:S(2)}) copy-start(f32[1536]{0:T(1024)S(1)} %mul.440) | copy-start | bytes 18436
  192.4 4.9 copy-start.22
  193.8 9.9 copy-start.24
  197.3 6.5 copy-start.31
  197.3 6.5 copy-start.33
  197.3 6.5 copy-start.35
  197.3 6.5 copy-start.37
  203.8 7.6 copy-start.42
  203.8 7.6 copy-start.26
  203.8 15.9 %slice-start.9 = ((s8[4718592]{0:T(1024)(128)(4,1)}), s8[4194304]{0:T(1024)(128)(4,1)S(1)}, s32[]{:S(2)}) async-start(s8[4718592]{0:T(1024)(128)(4,1)} %bitcast.216), calls=%async_computation.15 | async-start | bytes 8388608
  211.3 8.3 copy-start.48
  211.4 8.3 slice-start.10
  219.7 3.8 slice-start.13
  219.7 3.7 slice-start.14
  231.0 4.2 slice-start.15
  231.9 3.1 copy-start.50
  233.6 3.0 slice-start.16
  235.0 3.7 copy-start.82
  241.7 120.3 %all-gather.5.cloned.1.call-start = ((), (), s32[]{:S(2)}) async-start(), calls=%async_computation.4 | async-start | bytes 10616832 | tf_op jit(solution)/shard_map/all_gather | solution.py:730
  243.7 243.2 %reduce-scatter.5.cloned.1.call-start = ((), (), s32[]{:S(2)}) async-start(), calls=%async_computation.5 | async-start | bytes 10616832 | tf_op jit(solution)/shard_map/reduce_scatter | solution.py:743
  300.7 13.6 %copy-start.77 = (bf16[3072,1536]{1,0:T(8,128)(2,1)S(1)}, bf16[3072,1536]{1,0:T(8,128)(2,1)}, u32[]{:S(2)}) copy-start(bf16[3072,1536]{1,0:T(8,128)(2,1)} %all-gather.3.cloned.1.call-done) | copy-start | bytes 28311556
  300.7 13.6 %copy-start.78 = (bf16[768,1536]{1,0:T(8,128)(2,1)S(1)}, bf16[768,1536]{1,0:T(8,128)(2,1)}, u32[]{:S(2)}) copy-start(bf16[768,1536]{1,0:T(8,128)(2,1)} %param.35) | copy-start | bytes 7077892
  381.9 13.9 %copy-start.79 = (bf16[768,1536]{1,0:T(8,128)(2,1)S(1)}, bf16[768,1536]{1,0:T(8,128)(2,1)}, u32[]{:S(2)}) copy-start(bf16[768,1536]{1,0:T(8,128)(2,1)} %param.36) | copy-start | bytes 7077892
  381.9 13.9 %copy-start.84 = (bf16[3072,768]{1,0:T(8,128)(2,1)S(1)}, bf16[3072,768]{1,0:T(8,128)(2,1)}, u32[]{:S(2)}) copy-start(bf16[3072,768]{1,0:T(8,128)(2,1)} %get-tuple-element.141) | copy-start | bytes 14155780
  410.2 156.6 %reduce-scatter.3.cloned.1.call-start = ((), (), s32[]{:S(2)}) async-start(), calls=%async_computation.3 | async-start | bytes 10616832 | tf_op jit(solution)/shard_map/reduce_scatter | solution.py:736
  422.4 15.9 %slice-start.6 = ((s8[9437184]{0:T(1024)(128)(4,1)}), s8[1048576]{0:T(1024)(128)(4,1)S(1)}, s32[]{:S(2)}) async-start(s8[9437184]{0:T(1024)(128)(4,1)} %bitcast.214), calls=%async_computation.12 | async-start | bytes 2097152
  424.5 13.9 %slice-start.7 = ((s8[9437184]{0:T(1024)(128)(4,1)}), s8[4194304]{0:T(1024)(128)(4,1)S(1)}, s32[]{:S(2)}) async-start(s8[9437184]{0:T(1024)(128)(4,1)} %bitcast.214), calls=%async_computation.13 | async-start | bytes 8388608
  424.5 13.9 %slice-start.8 = ((s8[9437184]{0:T(1024)(128)(4,1)}), s8[4194304]{0:T(1024)(128)(4,1)S(1)}, s32[]{:S(2)}) async-start(s8[9437184]{0:T(1024)(128)(4,1)} %bitcast.214), calls=%async_computation.14 | async-start | bytes 8388608
  424.5 24.4 %slice-start.17 = ((s8[4718592]{0:T(1024)(128)(4,1)}), s8[4194304]{0:T(1024)(128)(4,1)S(1)}, s32[]{:S(2)}) async-start(s8[4718592]{0:T(1024)(128)(4,1)} %bitcast.234), calls=%async_computation.23 | async-start | bytes 8388608
  438.4 10.5 %slice-start.18 = ((s8[4718592]{0:T(1024)(128)(4,1)}), s8[524288]{0:T(1024)(128)(4,1)S(1)}, s32[]{:S(2)}) async-start(s8[4718592]{0:T(1024)(128)(4,1)} %bitcast.234), calls=%async_computation.24 | async-start | bytes 1048576
  448.9 38.0 %copy-start.4 = (f32[384,1536]{1,0:T(8,128)S(1)}, f32[384,1536]{1,0:T(8,128)}, u32[]{:S(2)}) copy-start(f32[384,1536]{1,0:T(8,128)} %copy-done.3) | copy-start | bytes 7077892
  486.8 2.8 copy-start.67
  486.8 79.9 %copy-start.9 = (bf16[384,1536]{1,0:T(8,128)(2,1)S(1)}, bf16[384,1536]{1,0:T(8,128)(2,1)}, u32[]{:S(2)}) copy-start(bf16[384,1536]{1,0:T(8,128)(2,1)} %reduce-scatter.5.cloned.1.call-done) | copy-start | bytes 3538948
  566.7 3.3 copy-start.11
  571.4 4.4 copy-start.83
  580.9 4.8 copy-start.30
  580.9 4.7 copy-start.41
  580.9 8.6 slice-start.4
  585.6 3.9 slice-start.5
  594.6 5.5 copy-start.73
  600.0 4.9 copy-start.65
  605.0 3.2 slice-start.11
  615.6 8.9 copy-start.27
  615.6 8.9 copy-start.40
  615.6 19.3 %slice-start = ((s8[14155776]{0:T(1024)(128)(4,1)}), s8[4194304]{0:T(1024)(128)(4,1)S(1)}, s32[]{:S(2)}) async-start(s8[14155776]{0:T(1024)(128)(4,1)} %bitcast.165), calls=%async_computation.6 | async-start | bytes 8388608
  615.6 19.3 %slice-start.1 = ((s8[14155776]{0:T(1024)(128)(4,1)}), s8[4194304]{0:T(1024)(128)(4,1)S(1)}, s32[]{:S(2)}) async-start(s8[14155776]{0:T(1024)(128)(4,1)} %bitcast.165), calls=%async_computation.7 | async-start | bytes 8388608
  624.5 10.4 %slice-start.2 = ((s8[14155776]{0:T(1024)(128)(4,1)}), s8[4194304]{0:T(1024)(128)(4,1)S(1)}, s32[]{:S(2)}) async-start(s8[14155776]{0:T(1024)(128)(4,1)} %bitcast.165), calls=%async_computation.8 | async-start | bytes 8388608
  624.5 10.4 %slice-start.3 = ((s8[14155776]{0:T(1024)(128)(4,1)}), s8[1572864]{0:T(1024)(128)(4,1)S(1)}, s32[]{:S(2)}) async-start(s8[14155776]{0:T(1024)(128)(4,1)} %bitcast.165), calls=%async_computation.9 | async-start | bytes 3145728
  635.0 7.3 copy-start.23
  635.0 7.3 copy-start.36
  635.0 7.3 copy-start.38
  649.0 11.0 %copy-start.68 = (f32[384]{0:T(512)S(1)}, f32[384]{0:T(512)}, u32[]{:S(2)}) copy-start(f32[384]{0:T(512)} %fusion.71) | copy-start | bytes 4612
  649.0 11.0 %copy-start.71 = (f32[1536]{0:T(1024)S(1)}, f32[1536]{0:T(1024)}, u32[]{:S(2)}) copy-start(f32[1536]{0:T(1024)} %add.152) | copy-start | bytes 18436
  692.9 11.3 %copy-start.63 = (f32[384]{0:T(512)S(1)}, f32[384]{0:T(512)}, u32[]{:S(2)}) copy-start(f32[384]{0:T(512)} %copy-done.62) | copy-start | bytes 4612
  692.9 11.3 %copy-start.75 = (f32[384]{0:T(512)S(1)}, f32[384]{0:T(512)}, u32[]{:S(2)}) copy-start(f32[384]{0:T(512)} %get-tuple-element.130) | copy-start | bytes 4612
  692.9 11.3 %copy-start.74 = (bf16[1536]{0:T(1024)(128)(2,1)S(1)}, bf16[1536]{0:T(1024)(128)(2,1)}, u32[]{:S(2)}) copy-start(bf16[1536]{0:T(1024)(128)(2,1)} %get-tuple-element.129) | copy-start | bytes 9220
  992.9 3.9 copy-start.28
  996.8 2.9 copy-start.18
  996.8 3.7 copy-start.20
  1005.1 9.0 copy-start.1
  (44 other events, 72.8 us)
Sparse Core Ops, SparseCore 0:
  241.8 58.8 all-gather.2
  303.2 58.8 all-gather.4
  410.3 76.4 reduce-scatter.4
  490.2 76.4 reduce-scatter.2

commit v2 on v1

--- a/solution.py
+++ b/solution.py
@@ -9,6 +9,7 @@
 from jax.sharding import PartitionSpec as P
 
 MESH = pl.DeviceIdType.MESH
+VMEM_LIMIT = 63 * 1024 * 1024
 
 D = 1536
 HEADS = 24
@@ -311,8 +312,11 @@
 def reduce_kernel(pieces, ffn_count, *refs):
     count = len(pieces)
     parts = refs[:count]
-    ffn = refs[count : count + 3]
-    out_a, out_f = refs[count + 3 : count + 5]
+    ffn = refs[count : count + (3 if ffn_count else 0)]
+    refs = refs[len(ffn) :]
+    out_a = refs[count]
+    out_f = refs[count + 1] if ffn_count else None
+    refs = refs[count + (2 if ffn_count else 1) :]
     (
         mate_buf,
         own_buf,
@@ -337,7 +341,7 @@
         chain_recv,
         out_sem,
         credit,
-    ) = refs[count + 5 :]
+    ) = refs
     me = lax.axis_index("grp")
     plane = lax.axis_index("rep")
     core = lax.rem(me, 2)
@@ -502,18 +506,22 @@
         )
 
     def kinds(j, body):
-        @pl.when(j < ffn_count)
-        def _():
-            body(*views(j, True))
+        if ffn_count:
+
+            @pl.when(j < ffn_count)
+            def _():
+                body(*views(j, True))
 
         @pl.when(j >= ffn_count)
         def _():
             body(*views(j, False))
 
     def inward(j):
-        @pl.when(j < ffn_count)
-        def _():
-            ffn_wait(j)
+        if ffn_count:
+
+            @pl.when(j < ffn_count)
+            def _():
+                ffn_wait(j)
 
         def body(mine, low, up, out):
             @pl.when(plane == 0)
@@ -590,15 +598,17 @@
     stages = (
         (load, 0, total),
         (ffn_load, 0, ffn_count),
-        (inward, 1, chain_total),
         (pair, 1, total),
         (plane_one, 3, total),
-        (middle, 3, chain_total),
         (plane_two, 5, total),
-        (root, 5, chain_total),
-        (outward, 7, chain_total),
-        (drain, 9, chain_total),
+        (inward, 5, chain_total),
+        (middle, 7, chain_total),
+        (root, 9, chain_total),
+        (outward, 11, chain_total),
+        (drain, 13, chain_total),
     )
+    if not ffn_count:
+        stages = stages[:1] + stages[2:]
 
     def step(t, carry):
         for stage, lag, limit in stages:
@@ -610,7 +620,7 @@
 
         return carry
 
-    lax.fori_loop(0, chain_total + 9, step, 0)
+    lax.fori_loop(0, chain_total + 13, step, 0)
     for i in range(max(total - MATE_SLOTS, 0), total):
         mate_copy(0, pl.ds(0, CUT), i % MATE_SLOTS).wait_send()
 
@@ -630,9 +640,9 @@
         out_shape=[
             jax.ShapeDtypeStruct((total * CUT, wide), low),
             jax.ShapeDtypeStruct((ffn_rows, wide), low),
-        ],
-        in_specs=[hbm] * (len(parts) + 3),
-        out_specs=[hbm] * 2,
+        ][: 2 if ffn else 1],
+        in_specs=[hbm] * (len(parts) + len(ffn)),
+        out_specs=[hbm] * (2 if ffn else 1),
         scratch_shapes=[
             pltpu.VMEM((MATE_SLOTS, 2, 2, CUT, wide), low),
             pltpu.VMEM((OWN_SLOTS, 2, 2, CUT, wide), low),
@@ -640,11 +650,11 @@
             pltpu.VMEM((total, 2, CUT, wide), low),
             pltpu.VMEM((total, CUT, wide), low),
             pltpu.VMEM((total, CUT, wide), low),
-            pltpu.VMEM((FFN_SLOTS, FCUT, wide), low),
+            pltpu.VMEM((FFN_SLOTS if ffn else 1, FCUT, wide), low),
             pltpu.VMEM((total, CUT, wide), low),
             pltpu.VMEM((total, CUT, wide), low),
-            pltpu.VMEM((ffn_count, FCUT, wide), low),
-            pltpu.VMEM((ffn_count, FCUT, wide), low),
+            pltpu.VMEM((max(ffn_count, 1), FCUT, wide), low),
+            pltpu.VMEM((max(ffn_count, 1), FCUT, wide), low),
             dma((MATE_SLOTS,)),
             dma((MATE_SLOTS,)),
             dma((OWN_SLOTS,)),
@@ -659,9 +669,315 @@
             pltpu.SemaphoreType.REGULAR,
         ],
         compiler_params=pltpu.CompilerParams(
-            collective_id=1, has_side_effects=True, vmem_limit_bytes=60 * 1024 * 1024
+            collective_id=1, has_side_effects=True, vmem_limit_bytes=VMEM_LIMIT
         ),
     )(*parts, *ffn)
+
+
+STEP_CHIP = (0, 0, 1, 2, 1, 2, 3, 3)
+STEP_HALF = (0, 1, 0, 1, 1, 0, 0, 1)
+TILE = 256
+
+
+def ffn_kernel(
+    act_in,
+    cot_in,
+    gate_in,
+    up_in,
+    down_in,
+    out_ref,
+    dn_ref,
+    grad_gate,
+    grad_up,
+    grad_down,
+    act,
+    cot,
+    w_gate,
+    w_up,
+    w_down,
+    hidden,
+    d_gate,
+    d_up,
+    pair,
+    mine,
+    stage,
+    passed,
+    final,
+    tile_buf,
+    weight_sem,
+    cot_sem,
+    own_sem,
+    act_send,
+    act_recv,
+    pair_send,
+    pair_recv,
+    flow_send,
+    flow_recv,
+    tile_sem,
+    end_sem,
+):
+    me = lax.axis_index("grp")
+    plane = lax.axis_index("rep")
+    mate_dev, x_dev, y_dev = (me ^ 1, plane), (me ^ 2, plane), (me ^ 4, plane)
+    half = act.shape[2]
+    seq_len = 2 * half
+    rows, wide = w_gate.shape
+    low = jnp.bfloat16
+    meet([mate_dev, x_dev, y_dev])
+
+    def remote(src, dst, send, recv, device):
+        return pltpu.make_async_remote_copy(
+            src_ref=src,
+            dst_ref=dst,
+            send_sem=send,
+            recv_sem=recv,
+            device_id=device,
+            device_id_type=MESH,
+        )
+
+    own = [act_in.at[pl.ds(h * half, half)] for h in range(2)]
+
+    def act_copy(t, other):
+        if other:
+            src, device = (own[t] if t < 2 else act.at[t, 0]), mate_dev
+        else:
+            src, device = {
+                2: (own[0], x_dev),
+                3: (own[1], y_dev),
+                4: (own[1], x_dev),
+                5: (own[0], y_dev),
+                6: (act.at[2, 0], y_dev),
+                7: (act.at[3, 0], x_dev),
+            }[t]
+        return remote(
+            src, act.at[t, other], act_send.at[t, other], act_recv.at[t, other], device
+        )
+
+    for t in (2, 3, 4, 5):
+        act_copy(t, 0).start()
+    for t in (0, 1):
+        act_copy(t, 1).start()
+    own_copies = [pltpu.make_async_copy(own[t], act.at[t, 0], own_sem.at[t]) for t in range(2)]
+    for copy in own_copies:
+        copy.start()
+    weights = [
+        pltpu.make_async_copy(src, dst, weight_sem.at[k])
+        for k, (src, dst) in enumerate(((gate_in, w_gate), (up_in, w_up), (down_in, w_down)))
+    ]
+    for copy in weights:
+        copy.start()
+    cot_copies = []
+    for t in range(8):
+        for other in range(2):
+            owner = me ^ (2 * STEP_CHIP[t] + other)
+            row = pl.multiple_of(owner * seq_len + STEP_HALF[t] * half, 16)
+            copy = pltpu.make_async_copy(
+                cot_in.at[pl.ds(row, half)], cot.at[t, other], cot_sem.at[t, other]
+            )
+            copy.start()
+            cot_copies.append(copy)
+
+    def pair_copy(kind, t):
+        return remote(
+            stage.at[kind], pair.at[kind, t], pair_send.at[kind], pair_recv.at[kind, t], mate_dev
+        )
+
+    def flow(kind, lane):
+        src, dst, device = (
+            (pair.at[kind, 2], final.at[kind, 0], x_dev),
+            (pair.at[kind, 4], final.at[kind, 1], x_dev),
+            (pair.at[kind, 5], final.at[kind, 2], y_dev),
+            (pair.at[kind, 3], final.at[kind, 3], y_dev),
+            (pair.at[kind, 6], passed.at[kind, 0], x_dev),
+            (pair.at[kind, 7], passed.at[kind, 1], y_dev),
+        )[lane]
+        return remote(src, dst, flow_send.at[kind, lane], flow_recv.at[kind, lane], device)
+
+    def add(*terms):
+        total = terms[0].astype(jnp.float32)
+        for term in terms[1:]:
+            total = total + term.astype(jnp.float32)
+        return total.astype(low)
+
+    def forward_tiles(t):
+        def tile(n, carry):
+            cut = pl.ds(pl.multiple_of(n * TILE, TILE), TILE)
+            tokens = act[t].reshape(seq_len, wide)
+            gate = dot_nt(tokens, w_gate[cut])
+            up = dot_nt(tokens, w_up[cut])
+            d_hidden = dot_nt(cot[t].reshape(seq_len, wide), w_down[cut])
+            sigmoid = 1.0 / (1.0 + jnp.exp(-gate))
+            silu = gate * sigmoid
+            hidden[t, :, cut] = (silu * up).astype(low)
+            d_gate[t, :, cut] = (
+                d_hidden * up * (sigmoid * (1.0 + gate * (1.0 - sigmoid)))
+            ).astype(low)
+            d_up[t, :, cut] = (d_hidden * silu).astype(low)
+            return carry
+
+        lax.fori_loop(0, rows // TILE, tile, 0)
+
+    def backward_tiles(t):
+        def tile(n, carry):
+            cut = pl.ds(pl.multiple_of(n * TILE, TILE), TILE)
+            out = dot(hidden[t], w_down[:, cut])
+            mine[0, :, cut] = out[:half].astype(low)
+            stage[0, :, cut] = out[half:].astype(low)
+            dn = dot(d_gate[t], w_gate[:, cut]) + dot(d_up[t], w_up[:, cut])
+            mine[1, :, cut] = dn[:half].astype(low)
+            stage[1, :, cut] = dn[half:].astype(low)
+            return carry
+
+        lax.fori_loop(0, wide // TILE, tile, 0)
+
+    def join(t, events):
+        for kind in range(2):
+            pair_copy(kind, t).wait()
+            pair[kind, t] = add(pair[kind, t], mine[kind])
+            for when, lane in events:
+                if when is None:
+                    flow(kind, lane).start()
+                else:
+
+                    @pl.when(t == when)
+                    def _(kind=kind, lane=lane):
+                        flow(kind, lane).start()
+
+    for copy in own_copies + weights:
+        copy.wait()
+
+    def step(t, carry):
+        for at in (2, 4, 6):
+
+            @pl.when(t == at)
+            def _(at=at):
+                for u in (at, at + 1):
+                    act_copy(u, 0).wait_recv()
+                    if at == 2:
+                        act_copy(u + 4, 0).start()
+                    act_copy(u, 1).start()
+
+        remote(
+            act.at[t, 0], act.at[t, 1], act_send.at[t, 1], act_recv.at[t, 1], mate_dev
+        ).wait_recv()
+        for other in range(2):
+            pltpu.make_async_copy(
+                cot_in.at[pl.ds(0, half)], cot.at[t, other], cot_sem.at[t, other]
+            ).wait()
+        forward_tiles(t)
+
+        @pl.when(t > 0)
+        def _():
+            join(t - 1, ((2, 0), (3, 3), (6, 4)))
+
+        backward_tiles(t)
+        for kind in range(2):
+            pair_copy(kind, t).start()
+        return carry
+
+    lax.fori_loop(0, 8, step, 0)
+    join(7, ((None, 5),))
+
+    def write(target, slot, cut):
+        return pltpu.make_async_copy(
+            tile_buf.at[slot], target.at[:, cut], tile_sem.at[slot]
+        )
+
+    tiles = wide // TILE
+    for k, (left, right, target) in enumerate(
+        ((d_gate, act, grad_gate), (d_up, act, grad_up), (hidden, cot, grad_down))
+    ):
+
+        def tile(n, carry, k=k, left=left, right=right, target=target):
+            cut = pl.ds(pl.multiple_of(n * TILE, TILE), TILE)
+            slot = lax.rem(n, 2)
+
+            @pl.when(k * tiles + n >= 2)
+            def _():
+                write(target, slot, cut).wait()
+
+            tile_buf[slot] = dot_tn(
+                left[...].reshape(8 * seq_len, rows),
+                right[:, :, :, cut].reshape(8 * seq_len, TILE),
+            ).astype(low)
+            write(target, slot, cut).start()
+            return carry
+
+        lax.fori_loop(0, tiles, tile, 0)
+    for slot in range(2):
+        write(grad_down, slot, pl.ds(0, TILE)).wait()
+
+    for kind in range(2):
+        for lane, t, onward in ((4, 5, 2), (5, 4, 1)):
+            flow(kind, lane).wait_recv()
+            pair[kind, t] = add(pair[kind, t], passed[kind, lane - 4])
+            flow(kind, onward).start()
+    ends = []
+    for kind, target in enumerate((out_ref, dn_ref)):
+        for h in range(2):
+            flow(kind, h).wait_recv()
+            flow(kind, 2 + h).wait_recv()
+            pair[kind, h] = add(pair[kind, h], final[kind, h], final[kind, 2 + h])
+            copy = pltpu.make_async_copy(
+                pair.at[kind, h], target.at[pl.ds(h * half, half)], end_sem.at[kind, h]
+            )
+            copy.start()
+            ends.append(copy)
+    for copy in ends:
+        copy.wait()
+    for kind in range(2):
+        for lane in range(6):
+            flow(kind, lane).wait_send()
+    for t in range(8):
+        act_copy(t, 1).wait_send()
+        if t >= 2:
+            act_copy(t, 0).wait_send()
+
+
+def ffn_all(act, cot, w_gate, w_up, w_down):
+    seq_len, wide = act.shape
+    rows = w_gate.shape[0]
+    half = seq_len // 2
+    low = jnp.bfloat16
+    hbm = pl.BlockSpec(memory_space=pltpu.HBM)
+    dma = pltpu.SemaphoreType.DMA
+    return pl.pallas_call(
+        ffn_kernel,
+        out_shape=[jax.ShapeDtypeStruct((seq_len, wide), low)] * 2
+        + [jax.ShapeDtypeStruct((rows, wide), low)] * 3,
+        in_specs=[hbm] * 5,
+        out_specs=[hbm] * 5,
+        scratch_shapes=[
+            pltpu.VMEM((8, 2, half, wide), low),
+            pltpu.VMEM((8, 2, half, wide), low),
+            pltpu.VMEM((rows, wide), low),
+            pltpu.VMEM((rows, wide), low),
+            pltpu.VMEM((rows, wide), low),
+            pltpu.VMEM((8, seq_len, rows), low),
+            pltpu.VMEM((8, seq_len, rows), low),
+            pltpu.VMEM((8, seq_len, rows), low),
+            pltpu.VMEM((2, 8, half, wide), low),
+            pltpu.VMEM((2, half, wide), low),
+            pltpu.VMEM((2, half, wide), low),
+            pltpu.VMEM((2, 2, half, wide), low),
+            pltpu.VMEM((2, 4, half, wide), low),
+            pltpu.VMEM((2, rows, TILE), low),
+            dma((3,)),
+            dma((8, 2)),
+            dma((2,)),
+            dma((8, 2)),
+            dma((8, 2)),
+            dma((2,)),
+            dma((2, 8)),
+            dma((2, 6)),
+            dma((2, 6)),
+            dma((2,)),
+            dma((2, 2)),
+        ],
+        compiler_params=pltpu.CompilerParams(
+            collective_id=2, has_side_effects=True, vmem_limit_bytes=VMEM_LIMIT
+        ),
+    )(act, cot, w_gate, w_up, w_down)
 
 
 def per_device(
@@ -728,23 +1044,29 @@
     grad_out = cotangent[0].astype(jnp.float32) * slot_valid[0].astype(jnp.float32)
     grad_mlp = grad_out.astype(jnp.bfloat16)
     all_grad = lax.all_gather(grad_mlp, "grp", axis=0, tiled=True)
-    all_act = lax.all_gather(act_three, "grp", axis=0, tiled=True)
-    gate_pre = dot_nt(all_act, w_gate)
-    up_pre = dot_nt(all_act, w_up)
-    hidden = swiglu(gate_pre, up_pre).astype(jnp.bfloat16)
-    mlp_part = dot(hidden, w_down).astype(jnp.bfloat16)
-    mlp_out = lax.psum_scatter(mlp_part, "grp", scatter_dimension=0, tiled=True)
+    if lax.axis_size("grp") == 8:
+        mlp_out, d_norm3, grad_gate, grad_up, grad_down = ffn_all(
+            act_three, all_grad, w_gate, w_up, w_down
+        )
+    else:
+        all_act = lax.all_gather(act_three, "grp", axis=0, tiled=True)
+        gate_pre = dot_nt(all_act, w_gate)
+        up_pre = dot_nt(all_act, w_up)
+        hidden = swiglu(gate_pre, up_pre).astype(jnp.bfloat16)
+        mlp_part = dot(hidden, w_down).astype(jnp.bfloat16)
+        mlp_out = lax.psum_scatter(mlp_part, "grp", scatter_dimension=0, tiled=True)
+        d_hidden = dot_nt(all_grad, w_down)
+        d_gate_full, d_up_full = swiglu_back(gate_pre, up_pre, d_hidden)
+        d_gate = d_gate_full.astype(jnp.bfloat16)
+        d_up = d_up_full.astype(jnp.bfloat16)
+        d_norm3_part = (dot(d_gate, w_gate) + dot(d_up, w_up)).astype(jnp.bfloat16)
+        d_norm3 = lax.psum_scatter(d_norm3_part, "grp", scatter_dimension=0, tiled=True)
+        grad_gate = dot_tn(d_gate, all_act).astype(jnp.bfloat16)
+        grad_up = dot_tn(d_up, all_act).astype(jnp.bfloat16)
+        grad_down = dot_tn(hidden, all_grad).astype(jnp.bfloat16)
     outputs = (section_two + mlp_out.astype(jnp.float32)).astype(jnp.bfloat16)
-    d_hidden = dot_nt(all_grad, w_down)
-    d_gate_full, d_up_full = swiglu_back(gate_pre, up_pre, d_hidden)
-    d_gate = d_gate_full.astype(jnp.bfloat16)
-    d_up = d_up_full.astype(jnp.bfloat16)
-    d_norm3_part = (dot(d_gate, w_gate) + dot(d_up, w_up)).astype(jnp.bfloat16)
-    d_norm3 = lax.psum_scatter(d_norm3_part, "grp", scatter_dimension=0, tiled=True)
     d_norm3 = d_norm3.astype(jnp.float32)
-    grad_gate = dot_tn(d_gate, all_act).astype(jnp.bfloat16)
-    grad_up = dot_tn(d_up, all_act).astype(jnp.bfloat16)
-    grad_down = dot_tn(hidden, all_grad).astype(jnp.bfloat16)
+    ffn_sums = lax.psum((grad_gate, grad_up, grad_down), "rep")
     d_ln_three, d_gain_three, d_shift_three = norm_back(
         section_two, gain_three, shift_three, d_norm3
     )
@@ -785,7 +1107,6 @@
     ).astype(jnp.bfloat16)
     groups = lax.axis_size("grp")
     attention_parts = [grad_qkv, grad_out_one, grad_query_two, grad_out_two, grad_kv_two]
-    ffn_parts = [grad_gate, grad_up, grad_down]
     if groups == 8 and lax.axis_size("rep") == 4:
         norm_part = jnp.swapaxes(norm_stack.reshape(6, groups, own_width), 0, 1)
         norm_part = norm_part.reshape(groups, 1, 6 * own_width)
@@ -795,7 +1116,7 @@
         kv2_part = jnp.swapaxes(kv2_part, 1, 2).reshape(groups, kv2_rows, D)
         parts = attention_parts[:4] + [kv2_part, norm_part]
         parts = [p.reshape(2, 2, 2, -1, D) for p in parts]
-        total_a, total_f = reduce_all(parts, ffn_parts)
+        (total_a,) = reduce_all(parts, [])
         ends = []
         for p in parts:
             ends.append((ends[-1] if ends else 0) + p.shape[3])
@@ -804,8 +1125,6 @@
         kv2_total = jnp.swapaxes(pieces[4].reshape(kv2_rows, 2, D // 2), 0, 1)
         pieces[4] = kv2_total.reshape(2 * kv2_rows, D // 2)
         attention_sums = pieces[:5]
-        own = w_gate.shape[0]
-        ffn_sums = [total_f[k * own : (k + 1) * own] for k in range(3)]
     else:
         norm_total = lax.psum(norm_stack, ("grp", "rep"))
         norm_total = lax.dynamic_slice_in_dim(
@@ -815,7 +1134,6 @@
             lax.psum_scatter(g, "grp", scatter_dimension=0, tiled=True) for g in attention_parts
         ]
         attention_sums = [lax.psum(g, "rep") for g in attention_sums]
-        ffn_sums = [lax.psum(g, "rep") for g in ffn_parts]
     norm_total = norm_total.astype(jnp.float32)
     grad_qkv, grad_out_one, grad_query_two, grad_out_two, grad_kv_two = (
         g.astype(jnp.float32) for g in attention_sums

time: 1040 us -> 861 us (0.83); the launches traced: 1020 us -> 853 us
  waiting for transfers between devices: 200 us -> 0.04 us
  Pallas kernels: 416 us -> 564 us
  matrix products: 249 us -> 137 us
    pallas_call x0 -> x1, Pallas kernels: none -> 137 us  [ffn_all(): pl.pallas_call(ffn_kernel, out_shape=[jax.ShapeDtypeStruct((seq_len, wide...]
    reduce_scatter x2 -> x0, waiting for transfers between devices: 105 us -> none  [the longest x1 76.5 us: per_device(): mlp_out = lax.psum_scatter(mlp_part, 'grp', scatter_dimension=0, tiled=True)]
    all_gather x1 -> x0, waiting for transfers between devices: 57 us -> none  [per_device(): all_act = lax.all_gather(act_three, 'grp', axis=0, tiled=True)]
    dot_general x8 -> x5, matrix products: 64.2 us -> 20.9 us  [dot_nt(): lax.dot_general(left_side, right_side, (((1,), (1,)), ((), ())), preferre...]
    dot_general x7 -> x4, matrix products: 63.2 us -> 22.1 us  [dot(): return jnp.dot(left_side, right_side, preferred_element_type=jnp.float32)]
    all_gather x1, waiting for transfers between devices: 37.6 us -> 0.01 us  [per_device(): all_grad = lax.all_gather(grad_mlp, 'grp', axis=0, tiled=True)]
    dot_general x8 -> x5, matrix products: 68.1 us -> 34.4 us  [dot_tn(): lax.dot_general(left_side, right_side, (((0,), (0,)), ((), ())), preferre...]
  transfers between devices with their start and end apart: 4 -> 2, of which waited for: 4 -> 0; matrix products, arithmetic and copies ran while one was open for 7% -> 18% of each run, Pallas kernels for 0% -> 50%
where the time goes in v2:
time: 861 us; the launch traced here: 853 us
  Pallas kernels  564 us (66%)
  matrix products  137 us (16%)
  local copies, waits for them, and re-layouts  73.6 us (9%)
  other arithmetic  62 us (7%)
  between operations  16.6 us (2%)
    pallas_call x1, Pallas kernels, reduce_all(): pl.pallas_call(functools.partial(reduce_kernel, pieces, ffn_count), out_s...  284 us
    pallas_call x1, Pallas kernels, gather_all(): pl.pallas_call(functools.partial(gather_kernel, pieces), out_shape=[jax.S...  142 us
    pallas_call x1, Pallas kernels, ffn_all(): pl.pallas_call(ffn_kernel, out_shape=[jax.ShapeDtypeStruct((seq_len, wide...  137 us
    dot_general x5, matrix products, dot_tn(): lax.dot_general(left_side, right_side, (((0,), (0,)), ((), ())), preferre...  34.4 us
    dot_general x4, matrix products, dot(): return jnp.dot(left_side, right_side, preferred_element_type=jnp.float32)  22.1 us
    dot_general x5, matrix products, dot_nt(): lax.dot_general(left_side, right_side, (((1,), (1,)), ((), ())), preferre...  20.9 us
    unnamed x225, local copies, waits for them, and re-layouts  19.9 us
    dot_general x2, matrix products, one_block(): jnp.einsum('qhd,khd->hqk', grad_block, value_heads, preferred_element_typ...  18.4 us
  transfers between devices with their start and end apart: 2, of which 0 were waited for; matrix products, arithmetic and copies ran while one was open for 18% of the time, Pallas kernels for 50%

profile of v2, /device:TPU:24, one launch (start us, length us, event | category | flops | bytes accessed | tf_op | source)
XLA Modules:
  0.0 852.7 jit_solution(17826957011775414862)
XLA Ops:
  8.0 2.5 bitcast_convert_fusion
  11.3 141.8 %shard_map.306 = (bf16[8,16,256]{2,1,0:T(8,128)(2,1)}, bf16[8,576,1536]{2,1,0:T(8,128)(2,1)}, bf16[8,192,1536]{2,1,0:T(8,128)(2,1)}, bf16[8,384,768]{2,1,0:T(8,1...) custom-call(bf16[16,256]{1,0:T(8,128)(2,1)} %pad.8.refs_0_, bf16[576,1536]{1,0:T(8,128)(2,1)} %refs_1_.1, ...), custom_call_target="tpu_custom_call" | custom-call | tf_op jit(solution)/shard_map/pallas_call | solution.py:290
  154.9 9.3 %fusion.50 = f32[384,4608]{1,0:T(8,128)S(1)} fusion(bf16[4608,1536]{1,0:T(8,128)(2,1)} %bitcast.196, bf16[1,384,1536]{2,1,0:T(8,128)(2,1)S(1)} %copy-done.7, f32[1536]{0:T(1024)S(1)} %add.145, f32[1536]{0:T(1024)S(1)} %mul.388, f32[384]{0:T(512)S(1)} %fusion.67, f32[384]{0:T(512)S(1)} %broadcast_multiply_fusion.2), kind=kOutput, calls=%fused_computation.95 | convolution fusion | flops 5439356928 | bytes 22428672 | tf_op jit(solution)/shard_map/dot_general | solution.py:67
  164.2 2.8 copy-done.31
  167.2 1.4 copy.59
  168.6 4.9 fusion.84
  173.5 3.0 copy.61
  176.5 1.3 slice.229
  177.8 3.0 copy.60
  180.9 1.3 slice.230
  182.3 4.2 fusion.8
  187.3 1.2 copy.81
  189.4 1.9 subtract_convert_fusion.3
  191.4 6.6 multiply_reduce_fusion.1
  198.1 7.5 fusion
  205.7 8.4 fusion.39
  214.1 2.1 fusion.87
  217.7 3.2 convolution_convert_fusion.8
  220.8 1.9 copy.63
  225.3 1.6 copy-done.1
  226.9 1.4 fusion.38
  229.8 2.2 fusion.88
  233.3 1.5 add_convert_fusion.1.act_in
  234.9 137.3 %shard_map.307 = (bf16[384,1536]{1,0:T(8,128)(2,1)}, bf16[384,1536]{1,0:T(8,128)(2,1)}, bf16[768,1536]{1,0:T(8,128)(2,1)}, bf16[768,1536]{1,0:T(8,128)(2,1)}, bf16[768,1536]{1,0:T(8,128)(2,1)}) custom-call(bf16[384,1536]{1,0:T(8,128)(2,1)} %add_convert_fusion.1.act_in, bf16[3072,1536]{1,0:T(8,128)(2,1)} %all-gather.2.cloned.1.call-done.cot_in, ...), custom_call_target="tpu_custom_call" | custom-call | tf_op jit(solution)/shard_map/pallas_call | solution.py:944
  372.2 3.6 fusion.28
  375.8 3.3 fusion.83
  381.5 5.4 convolution_convert_fusion.7
  386.9 2.2 copy.66
  389.1 4.3 multiply_reduce_fusion.2
  393.5 1.2 multiply_convert_fusion.1
  395.5 1.2 copy-done.20
  396.7 3.2 multiply_reduce_fusion.4
  402.4 1.4 copy-done.23
  404.9 3.0 convolution_convert_fusion.6
  407.9 2.4 copy.69
  410.3 9.2 %fusion.40 = bf16[24,64,384]{2,1,0:T(8,128)(2,1)} fusion(bf16[384,24,64]{0,2,1:T(8,128)(2,1)} %bitcast.155, f32[24,384,384]{1,2,0:T(8,128)} %get-tuple-element.181, f32[24,384]{1,0:T(8,128)S(1)} %log_add_fusion), kind=kOutput, calls=%fused_computation.89 | convolution fusion | flops 464191488 | bytes 16551936 | tf_op jit(solution)/shard_map/while/body/eval_jaxpr/hqk,qhd->khd/dot_general | solution.py:137
  419.5 14.1 %multiply_reduce_fusion = (f32[24,384]{1,0:T(8,128)S(1)}, f32[24,384,384]{1,2,0:T(8,128)}) fusion(f32[24,384,384]{1,2,0:T(8,128)} %get-tuple-element.181, f32[24,384]{1,0:T(8,128)S(1)} %log_add_fusion, bf16[384,24,64]{0,2,1:T(8,128)(2,1)S(1)} %bitcast.156, bf16[384,24,64]{0,2,1:T(8,128)(2,1)} %bitcast.171), kind=kOutput, calls=%fused_computation.2 | convolution fusion | flops 467131392 | bytes 30744576 | tf_op jit(solution)/shard_map/while/body/eval_jaxpr/qhd,khd->hqk/dot_general | solution.py:123
  433.7 7.2 multiply_convert_fusion
  440.9 2.8 copy-done.2
  443.8 2.7 multiply_bitcast_fusion.1
  446.5 7.2 multiply_bitcast_fusion
  453.7 1.3 fusion.44
  455.0 2.1 reduce.1
  457.1 1.5 slice.228
  458.6 1.4 slice.227
  460.0 1.6 subtract_convert_fusion.1
  463.8 10.5 %fusion.81 = (bf16[1536]{0:T(1024)(128)(2,1)S(1)}, f32[384]{0:T(512)S(1)}, f32[384,1536]{1,0:T(8,128)}) fusion(f32[1536]{0:T(1024)S(1)} %copy-done.60, f32[384]{0:T(512)S(1)} %broadcast_multiply_fusion.2, bf16[1,384,1536]{2,1,0:T(8,128)(2,1)S(1)} %copy-done.8, bf16[4608,1536]{1,0:T(8,128)(2,1)} %bitcast.197, bf16[384,1536]{0,1:T(8,128)(2,1)S(1)} %bitcast.178, ...), kind=kOutput, calls=%fused_computation.176 | convolution fusion | flops 5449971712 | bytes 21245952 | tf_op jit(solution)/shard_map/dot_general | solution.py:79
  474.3 2.5 multiply_convert_fusion.3
  476.9 3.6 convolution_convert_fusion.4
  480.5 10.1 %copy.85 = bf16[8,2,192,768]{3,1,2,0:T(2,128)(2,1)} copy(bf16[8,2,192,768]{3,2,1,0:T(8,128)(2,1)} %bitcast.174) | data formatting | bytes 9437184 | tf_op jit(solution)/shard_map/reshape | solution.py:1115
  490.6 11.3 %reshape_reshape.16.refs_4_ = bf16[2,2,2,192,1536]{4,3,2,1,0:T(8,128)(2,1)} reshape(bf16[8,192,2,768]{3,2,1,0:T(2,128)(2,1)} %bitcast.153) | data formatting | bytes 9437184 | tf_op jit(solution)/shard_map/reshape;reshape | solution.py:1118
  502.0 2.8 fusion.26
  505.5 1.1 pad.9.clone
  506.6 5.7 convolution_convert_fusion.1
  512.4 4.6 convolution_convert_fusion.3
  517.0 4.6 convolution_convert_fusion.2
  521.6 16.0 %convolution_convert_fusion = bf16[4608,1536]{1,0:T(8,128)(2,1)} fusion(bf16[384,1536]{0,1:T(8,128)(2,1)S(1)} %bitcast.179, bf16[384,1536]{0,1:T(8,128)(2,1)S(1)} %bitcast.186, bf16[384,1536]{0,1:T(8,128)(2,1)S(1)} %bitcast.184, bf16[1,384,1536]{2,1,0:T(8,128)(2,1)S(1)} %copy-done.9, f32[1536]{0:T(1024)S(1)} %copy-done.77, f32[384]{0:T(512)S(1)} %copy-done.70, ...), kind=kOutput, calls=%fused_computation | convolution fusion | flops 5457051648 | bytes 18889728 | tf_op jit(solution)/shard_map/dot_general | solution.py:73
  537.6 284.5 %shard_map.308 = bf16[1392,1536]{1,0:T(8,128)(2,1)} custom-call(bf16[2,2,2,576,1536]{4,3,2,1,0:T(8,128)(2,1)} %bitcast.154, bf16[2,2,2,192,1536]{4,3,2,1,0:T(8,128)(2,1)} %bitcast.169, bf16[2,2,2,192,1536]{4,3,2,1,0:T(8,128)(2,1)} %bitcast.170, bf16[2,2,2,192,1536]{4,3,2,1,0:T(8,128)(2,1)} %bitcast.168, ...), custom_call_target="tpu_custom_call" | custom-call | tf_op jit(solution)/shard_map/pallas_call | solution.py:638
  822.1 3.6 slice_convert_fusion.6
  829.0 3.9 slice_convert_fusion.1
  832.9 2.2 add_bitcast_fusion
  835.1 4.6 convert_element_type.249
  839.8 2.8 convert_element_type.250
  842.6 2.8 convert_element_type.251
  (294 shorter events, 24.3 us)
Async XLA Ops:
  7.2 175.1 %copy-start = (bf16[1,130,768]{2,1,0:T(8,128)(2,1)S(1)}, bf16[1,130,768]{2,1,0:T(8,128)(2,1)}, u32[]{:S(2)}) copy-start(bf16[1,130,768]{2,1,0:T(8,128)(2,1)} %param.20) | copy-start | bytes 599044
  7.3 227.6 %all-gather.2.cloned.1.call-start = ((), (), s32[]{:S(2)}) async-start(), calls=%async_computation | async-start | bytes 10616832 | tf_op jit(solution)/shard_map/all_gather | solution.py:1046
  10.5 143.6 %copy-start.7 = (bf16[1,384,1536]{2,1,0:T(8,128)(2,1)S(1)}, bf16[1,384,1536]{2,1,0:T(8,128)(2,1)}, u32[]{:S(2)}) copy-start(bf16[1,384,1536]{2,1,0:T(8,128)(2,1)} %param.19) | copy-start | bytes 3538948
  10.5 824.6 %all-reduce.5.cloned.1.call-start = ((), (), s32[]{:S(2)}) async-start(), calls=%async_computation.1 | async-start | bytes 14155776 | tf_op jit(solution)/shard_map/psum | solution.py:1069
  154.1 10.1 %copy-start.76 = (f32[1536]{0:T(1024)}, f32[1536]{0:T(1024)S(1)}, u32[]{:S(2)}) copy-start(f32[1536]{0:T(1024)S(1)} %add.145) | copy-start | bytes 18436
  154.8 9.3 %copy-start.65 = (f32[384]{0:T(512)}, f32[384]{0:T(512)S(1)}, u32[]{:S(2)}) copy-start(f32[384]{0:T(512)S(1)} %fusion.29) | copy-start | bytes 4612
  154.9 9.3 %copy-start.69 = (f32[384]{0:T(512)}, f32[384]{0:T(512)S(1)}, u32[]{:S(2)}) copy-start(f32[384]{0:T(512)S(1)} %fusion.67) | copy-start | bytes 4612
  182.2 9.2 %copy-start.29 = (bf16[384,24,32]{0,2,1:T(8,128)(2,1)}, bf16[384,24,32]{0,2,1:T(8,128)(2,1)S(1)}, u32[]{:S(2)}) copy-start(bf16[384,24,32]{0,2,1:T(8,128)(2,1)S(1)} %slice.230) | copy-start | bytes 1769476
  188.5 28.1 %copy-start.78 = (f32[1536]{0:T(1024)}, f32[1536]{0:T(1024)S(1)}, u32[]{:S(2)}) copy-start(f32[1536]{0:T(1024)S(1)} %add.152) | copy-start | bytes 18436
  188.6 211.2 %copy-start.61 = (f32[1536]{0:T(1024)}, f32[1536]{0:T(1024)S(1)}, u32[]{:S(2)}) copy-start(f32[1536]{0:T(1024)S(1)} %mul.409) | copy-start | bytes 18436
  189.4 8.6 %copy-start.56 = (f32[384,16]{0,1:T(8,128)}, f32[384,16]{0,1:T(8,128)S(1)}, u32[]{:S(2)}) copy-start(f32[384,16]{0,1:T(8,128)S(1)} %get-tuple-element.179) | copy-start | bytes 73732
  191.4 6.7 copy-start.35
  191.4 6.7 copy-start.37
  191.4 6.7 copy-start.39
  191.4 6.7 copy-start.41
  198.1 7.5 copy-start.32
  198.1 16.0 %slice-start.8 = ((s8[4718592]{0:T(1024)(128)(4,1)}), s8[524288]{0:T(1024)(128)(4,1)S(1)}, s32[]{:S(2)}) async-start(s8[4718592]{0:T(1024)(128)(4,1)} %bitcast.198), calls=%async_computation.10 | async-start | bytes 1048576
  205.7 8.4 slice-start.9
  216.3 183.6 %copy-start.63 = (f32[384]{0:T(512)}, f32[384]{0:T(512)S(1)}, u32[]{:S(2)}) copy-start(f32[384]{0:T(512)S(1)} %broadcast_multiply_fusion.1) | copy-start | bytes 4612
  216.7 4.2 copy-start.73
  224.4 4.2 slice-start.16
  372.2 3.6 copy-start.68
  372.2 3.6 copy-start.4
  372.2 3.6 copy-start.14
  389.1 4.3 copy-start.12
  389.1 4.3 slice-start.4
  389.1 4.3 slice-start.5
  389.1 6.4 slice-start.14
  395.5 4.4 copy-start.50
  399.9 3.9 slice-start.10
  410.3 9.2 %copy-start.11 = (bf16[384,1536]{0,1:T(8,128)(2,1)S(1)}, bf16[384,1536]{0,1:T(8,128)(2,1)}, u32[]{:S(2)}) copy-start(bf16[384,1536]{0,1:T(8,128)(2,1)} %copy.69) | copy-start | bytes 3538948
  410.3 23.3 %slice-start = ((s8[14155776]{0:T(1024)(128)(4,1)}), s8[4194304]{0:T(1024)(128)(4,1)S(1)}, s32[]{:S(2)}) async-start(s8[14155776]{0:T(1024)(128)(4,1)} %bitcast.147), calls=%async_computation.2 | async-start | bytes 8388608
  410.3 23.3 %slice-start.1 = ((s8[14155776]{0:T(1024)(128)(4,1)}), s8[4194304]{0:T(1024)(128)(4,1)S(1)}, s32[]{:S(2)}) async-start(s8[14155776]{0:T(1024)(128)(4,1)} %bitcast.147), calls=%async_computation.3 | async-start | bytes 8388608
  419.5 14.1 %slice-start.2 = ((s8[14155776]{0:T(1024)(128)(4,1)}), s8[4194304]{0:T(1024)(128)(4,1)S(1)}, s32[]{:S(2)}) async-start(s8[14155776]{0:T(1024)(128)(4,1)} %bitcast.147), calls=%async_computation.4 | async-start | bytes 8388608
  419.5 14.1 %slice-start.3 = ((s8[14155776]{0:T(1024)(128)(4,1)}), s8[1572864]{0:T(1024)(128)(4,1)S(1)}, s32[]{:S(2)}) async-start(s8[14155776]{0:T(1024)(128)(4,1)} %bitcast.147), calls=%async_computation.5 | async-start | bytes 3145728
  433.7 10.1 %copy-start.40 = (bf16[384,24,16]{0,2,1:T(8,128)(2,1)S(1)}, bf16[384,24,16]{0,2,1:T(8,128)(2,1)}, u32[]{:S(2)}) copy-start(bf16[384,24,16]{0,2,1:T(8,128)(2,1)} %copy-done.39) | copy-start | bytes 884740
  433.7 10.1 %copy-start.42 = (bf16[384,24,16]{0,2,1:T(8,128)(2,1)S(1)}, bf16[384,24,16]{0,2,1:T(8,128)(2,1)}, u32[]{:S(2)}) copy-start(bf16[384,24,16]{0,2,1:T(8,128)(2,1)} %copy-done.41) | copy-start | bytes 884740
  443.8 9.9 %slice-start.6 = ((s8[5013504]{0:T(1024)(128)(4,1)}), s8[4194304]{0:T(1024)(128)(4,1)S(1)}, s32[]{:S(2)}) async-start(s8[5013504]{0:T(1024)(128)(4,1)} %bitcast.151), calls=%async_computation.8 | async-start | bytes 8388608
  446.5 7.2 slice-start.7
  446.5 7.2 copy-start.13
  455.0 4.9 copy-start.57
  455.0 4.9 copy-start.58
  462.0 12.3 %copy-start.52 = (bf16[384,24,64]{0,2,1:T(8,128)(2,1)}, bf16[384,24,64]{0,2,1:T(8,128)(2,1)S(1)}, u32[]{:S(2)}) copy-start(bf16[384,24,64]{0,2,1:T(8,128)(2,1)S(1)} %get-tuple-element.194) | copy-start | bytes 3538948
  462.0 12.3 %copy-start.54 = (bf16[384,24,64]{0,2,1:T(8,128)(2,1)}, bf16[384,24,64]{0,2,1:T(8,128)(2,1)S(1)}, u32[]{:S(2)}) copy-start(bf16[384,24,64]{0,2,1:T(8,128)(2,1)S(1)} %get-tuple-element.195) | copy-start | bytes 3538948
  490.6 11.4 %copy-start.66 = (f32[384]{0:T(512)S(1)}, f32[384]{0:T(512)}, u32[]{:S(2)}) copy-start(f32[384]{0:T(512)} %copy-done.65) | copy-start | bytes 4612
  490.6 11.4 %copy-start.9 = (bf16[1,384,1536]{2,1,0:T(8,128)(2,1)S(1)}, bf16[1,384,1536]{2,1,0:T(8,128)(2,1)}, u32[]{:S(2)}) copy-start(bf16[1,384,1536]{2,1,0:T(8,128)(2,1)} %param.19) | copy-start | bytes 3538948
  490.6 11.4 %copy-start.70 = (f32[384]{0:T(512)S(1)}, f32[384]{0:T(512)}, u32[]{:S(2)}) copy-start(f32[384]{0:T(512)} %copy-done.69) | copy-start | bytes 4612
  502.0 4.6 copy-start.49
  506.6 5.8 copy-start.24
  506.6 5.8 copy-start.90
  512.3 4.6 copy-start.21
  512.3 4.6 copy-start.51
  512.4 4.6 copy-start.62
  512.4 4.6 copy-start.64
  512.4 4.6 copy-start.75
  512.4 4.6 copy-start.79
  517.0 4.6 copy-start.47
  517.0 4.6 copy-start.53
  517.0 4.6 copy-start.55
  517.0 4.6 copy-start.77
  826.5 6.4 copy-start.25
  829.0 3.9 copy-start.10
  829.0 3.9 copy-start.22
  835.1 4.7 copy-start.44
  (48 other events, 116.2 us)
Sparse Core Ops, SparseCore 0:
  10.6 97.9 all-gather.1
  474.5 339.6 all-reduce.4

commit v3 on v2

--- a/solution.py
+++ b/solution.py
@@ -27,11 +27,6 @@
     return center * lax.rsqrt(spread + epsilon) * gain + shift
 
 
-def norm_back(tensor, gain, shift, d_normed):
-    _, pullback = jax.vjp(layer_norm, tensor, gain, shift)
-    return pullback(d_normed)
-
-
 def swiglu(gate_part, up_part):
     return jax.nn.silu(gate_part) * up_part
 
@@ -39,28 +34,6 @@
 def swiglu_back(gate_part, up_part, d_hidden):
     _, pullback = jax.vjp(swiglu, gate_part, up_part)
     return pullback(d_hidden)
-
-
-def angles(positions, head_size):
-    quarter = head_size // 4
-    frequency = jnp.exp(jnp.arange(quarter, dtype=jnp.float32) * (-math.log(10000.0) / quarter))
-    turned = positions.astype(jnp.float32)[:, None] * frequency[None, :]
-    return (jnp.cos(turned)[:, None, :], jnp.sin(turned)[:, None, :])
-
-
-def rotate(tensor, cosine, sin_table):
-    quarter = tensor.shape[-1] // 4
-    first_half = tensor[..., :quarter]
-    second_half = tensor[..., quarter : 2 * quarter]
-    remainder = tensor[..., 2 * quarter :]
-    return jnp.concatenate(
-        [
-            first_half * cosine - second_half * sin_table,
-            first_half * sin_table + second_half * cosine,
-            remainder,
-        ],
-        axis=-1,
-    )
 
 
 def dot_nt(left_side, right_side):
@@ -79,74 +52,21 @@
     return jnp.dot(left_side, right_side, preferred_element_type=jnp.float32)
 
 
-def part_grad(grad_cols, activation):
-    return dot_tn(grad_cols, activation).astype(jnp.bfloat16)
-
-
-def attend(queries, key_heads, value_heads):
-    seq_len = queries.shape[0]
-    span = min(seq_len, 512)
-    blocked = queries.reshape(seq_len // span, span, queries.shape[1], queries.shape[2])
-
-    def one_block(query_block):
-        scores = (
-            jnp.einsum("qhd,khd->hqk", query_block, key_heads, preferred_element_type=jnp.float32)
-            * score_scale
-        )
-        largest = jnp.max(scores, axis=-1, keepdims=True)
-        shifted = jnp.exp(scores - largest)
-        totals = jnp.sum(shifted, axis=-1, keepdims=True)
-        probability = (shifted / totals).astype(jnp.bfloat16)
-        result = jnp.einsum(
-            "hqk,khd->qhd", probability, value_heads, preferred_element_type=jnp.float32
-        )
-        return (result.astype(jnp.bfloat16), (largest + jnp.log(totals))[..., 0])
-
-    outcome, log_sums = lax.map(one_block, blocked)
-    return (outcome.reshape(queries.shape), log_sums)
-
-
-def attend_back(queries, key_heads, value_heads, log_sums, grad_heads):
-    seq_len = queries.shape[0]
-    span = min(seq_len, 512)
-    block_count = seq_len // span
-    query_blocks = queries.reshape(block_count, span, queries.shape[1], queries.shape[2])
-    grad_blocks = grad_heads.reshape(block_count, span, queries.shape[1], queries.shape[2])
-
-    def one_block(carried, inputs_block):
-        query_block, log_block, grad_block = inputs_block
-        scores = (
-            jnp.einsum("qhd,khd->hqk", query_block, key_heads, preferred_element_type=jnp.float32)
-            * score_scale
-        )
-        probability = jnp.exp(scores - log_block[..., None])
-        d_prob = jnp.einsum(
-            "qhd,khd->hqk", grad_block, value_heads, preferred_element_type=jnp.float32
-        )
-        inner = jnp.sum(probability * d_prob, axis=-1, keepdims=True)
-        d_scores = (probability * (d_prob - inner)).astype(jnp.bfloat16)
-        d_query = (
-            jnp.einsum("hqk,khd->qhd", d_scores, key_heads, preferred_element_type=jnp.float32)
-            * score_scale
-        )
-        d_key = (
-            carried[0]
-            + jnp.einsum("hqk,qhd->khd", d_scores, query_block, preferred_element_type=jnp.float32)
-            * score_scale
-        )
-        d_value = carried[1] + jnp.einsum(
-            "hqk,qhd->khd",
-            probability.astype(jnp.bfloat16),
-            grad_block,
-            preferred_element_type=jnp.float32,
-        )
-        return ((d_key, d_value), d_query)
-
-    start_zero = jnp.zeros(key_heads.shape, jnp.float32)
-    (d_key, d_value), d_query = lax.scan(
-        one_block, (start_zero, start_zero), (query_blocks, log_sums, grad_blocks)
+def turn_tables(positions):
+    quarter = HD // 4
+    frequency = jnp.exp(jnp.arange(quarter, dtype=jnp.float32) * (-math.log(10000.0) / quarter))
+    turned = positions.astype(jnp.float32)[:, None] * frequency[None, :]
+    cosine, sine = jnp.cos(turned), jnp.sin(turned)
+    none, one = jnp.zeros_like(sine), jnp.ones_like(sine)
+
+    def heads(*parts):
+        return jnp.tile(jnp.concatenate(parts, axis=1), (1, 2))
+
+    return (
+        heads(cosine, cosine, one, one),
+        heads(-sine, none, none, none),
+        heads(none, sine, none, none),
     )
-    return (d_query.reshape(queries.shape), d_key, d_value)
 
 
 def meet(peers, lower=None, upper=None, rep_index=None):
@@ -172,133 +92,147 @@
 GATHER_WINDOW = 4
 
 
-def gather_kernel(pieces, *refs):
-    count = len(pieces)
-    sources = refs[:count]
-    fulls = refs[count : 2 * count]
-    send_sem, recv_sem, local_sem = refs[2 * count :]
-    me = lax.axis_index("grp")
-    plane = lax.axis_index("rep")
-    odd = lax.rem(plane, 2)
-    first_bit = 2 + 2 * odd
-    second_bit = 6 - first_bit
-    first = me ^ first_bit
-    second = me ^ second_bit
-    across = me ^ 6
-    first_dev = (first, plane)
-    second_dev = (second, plane)
-    rep_dev = (me, plane ^ 1)
-    mate_dev = (me ^ 1, plane)
-    meet([first_dev, second_dev, rep_dev, mate_dev])
-    total = sum(n for n, _ in pieces)
-
-    def each(i, body):
+class Gather:
+    def __init__(self, pieces, sources, fulls, send_sem, recv_sem, local_sem):
+        self.pieces, self.sources, self.fulls = pieces, sources, fulls
+        self.send_sem, self.recv_sem, self.local_sem = send_sem, recv_sem, local_sem
+        self.total = sum(n for n, _ in pieces)
+        self.steps = self.total + GATHER_WINDOW + 2
+        self.me = me = lax.axis_index("grp")
+        self.plane = plane = lax.axis_index("rep")
+        first_bit = 2 + 2 * lax.rem(plane, 2)
+        self.first, self.second, self.across = me ^ first_bit, me ^ (6 - first_bit), me ^ 6
+        self.first_dev = (self.first, plane)
+        self.second_dev = (self.second, plane)
+        self.rep_dev = (me, plane ^ 1)
+        self.mate_dev = (me ^ 1, plane)
+
+    def start(self):
+        meet([self.first_dev, self.second_dev, self.rep_dev, self.mate_dev])
+
+    def own_copy(self, k):
+        n, rows = self.pieces[k]
+        row = pl.multiple_of(self.me * (n * rows), 16)
+        return pltpu.make_async_copy(
+            self.sources[k], self.fulls[k].at[pl.ds(row, n * rows)], self.local_sem.at[k]
+        )
+
+    def each(self, i, body):
         base = 0
-        for k, (n, rows) in enumerate(pieces):
-            if n == 1:
-
-                @pl.when(i == base)
-                def _(k=k, rows=rows):
-                    body(k, pl.ds(0, rows))
-
-            else:
-
-                @pl.when((i >= base) & (i < base + n))
-                def _(k=k, rows=rows, base=base):
-                    body(k, pl.ds(pl.multiple_of((i - base) * rows, 16), rows))
+        for k, (n, rows) in enumerate(self.pieces):
+
+            @pl.when((i >= base) & (i < base + n))
+            def _(k=k, rows=rows, base=base):
+                body(k, (i - base) * rows)
 
             base += n
 
-    def push(k, cut, i, owner, lane, device, own=False):
-        src = sources[k].at[cut] if own else fulls[k].at[owner, cut]
+    def push(self, k, offset, i, owner, lane, device, own=False):
+        n, rows = self.pieces[k]
+        cut = pl.ds(pl.multiple_of(offset, 16), rows)
+        place = self.fulls[k].at[pl.ds(pl.multiple_of(owner * (n * rows) + offset, 16), rows)]
         return pltpu.make_async_remote_copy(
-            src_ref=src,
-            dst_ref=fulls[k].at[owner, cut],
-            send_sem=send_sem.at[lane, i],
-            recv_sem=recv_sem.at[lane, i],
+            src_ref=self.sources[k].at[cut] if own else place,
+            dst_ref=place,
+            send_sem=self.send_sem.at[lane, i],
+            recv_sem=self.recv_sem.at[lane, i],
             device_id=device,
             device_id_type=MESH,
         )
 
-    def stage_own(i):
-        def body(k, cut):
-            push(k, cut, i, me, 0, first_dev, own=True).start()
-            push(k, cut, i, me, 3, mate_dev, own=True).start()
-            pltpu.make_async_copy(sources[k].at[cut], fulls[k].at[me, cut], local_sem.at[i]).start()
-
-        each(i, body)
-
-    def stage_first(i):
-        def body(k, cut):
-            push(k, cut, i, first, 0, first_dev).wait_recv()
-            push(k, cut, i, first, 1, second_dev).start()
-            push(k, cut, i, first, 2, rep_dev).start()
-            push(k, cut, i, first, 4, mate_dev).start()
-
-        each(i, body)
-
-    def stage_rest(i):
-        def body(k, cut):
-            push(k, cut, i, across, 1, second_dev).wait_recv()
-            push(k, cut, i, across, 5, mate_dev).start()
-            push(k, cut, i, second, 2, rep_dev).wait_recv()
-            push(k, cut, i, second, 6, mate_dev).start()
-
-        each(i, body)
-
-    def stage_end(i):
-        def body(k, cut):
-            pltpu.make_async_copy(
-                sources[k].at[cut], fulls[k].at[me, cut], local_sem.at[i]
-            ).wait()
-            push(k, cut, i, me, 0, first_dev, own=True).wait_send()
-            push(k, cut, i, first, 1, second_dev).wait_send()
-            push(k, cut, i, first, 2, rep_dev).wait_send()
-            push(k, cut, i, me, 3, mate_dev, own=True).wait()
-            push(k, cut, i, first, 4, mate_dev).wait()
-            push(k, cut, i, across, 5, mate_dev).wait()
-            push(k, cut, i, second, 6, mate_dev).wait()
-
-        each(i, body)
-
-    def step(t, carry):
-        for stage, lag in ((stage_own, 0), (stage_first, GATHER_WINDOW), (stage_rest, GATHER_WINDOW + 2)):
+    def stage_own(self, i):
+        def body(k, offset):
+            self.push(k, offset, i, self.me, 0, self.first_dev, own=True).start()
+            self.push(k, offset, i, self.me, 3, self.mate_dev, own=True).start()
+
+        self.each(i, body)
+
+    def stage_first(self, i):
+        def body(k, offset):
+            self.push(k, offset, i, self.first, 0, self.first_dev).wait_recv()
+            self.push(k, offset, i, self.first, 1, self.second_dev).start()
+            self.push(k, offset, i, self.first, 2, self.rep_dev).start()
+            self.push(k, offset, i, self.first, 4, self.mate_dev).start()
+
+        self.each(i, body)
+
+    def stage_rest(self, i):
+        def body(k, offset):
+            self.push(k, offset, i, self.across, 1, self.second_dev).wait_recv()
+            self.push(k, offset, i, self.across, 5, self.mate_dev).start()
+            self.push(k, offset, i, self.second, 2, self.rep_dev).wait_recv()
+            self.push(k, offset, i, self.second, 6, self.mate_dev).start()
+
+        self.each(i, body)
+
+    def step(self, t):
+        for stage, lag in (
+            (self.stage_own, 0),
+            (self.stage_first, GATHER_WINDOW),
+            (self.stage_rest, GATHER_WINDOW + 2),
+        ):
             i = t - lag
 
-            @pl.when((i >= 0) & (i < total))
+            @pl.when((i >= 0) & (i < self.total))
             def _(stage=stage, i=i):
                 stage(i)
 
-        return carry
-
-    lax.fori_loop(0, total + GATHER_WINDOW + 2, step, 0)
-
-    def finish(i, carry):
-        stage_end(i)
-        return carry
-
-    lax.fori_loop(0, total, finish, 0)
-
-
-def gather_all(arrays, rows):
-    groups = lax.axis_size("grp")
-    if groups != 8 or lax.axis_size("rep") % 2 != 0:
-        return [lax.all_gather(a, "grp", axis=0) for a in arrays]
-    pieces = tuple((a.shape[0] // n, n) for a, n in zip(arrays, rows))
-    total = sum(n for n, _ in pieces)
-    hbm = pl.BlockSpec(memory_space=pltpu.HBM)
-    return pl.pallas_call(
-        functools.partial(gather_kernel, pieces),
-        out_shape=[jax.ShapeDtypeStruct((groups,) + a.shape, a.dtype) for a in arrays],
-        in_specs=[hbm] * len(arrays),
-        out_specs=[hbm] * len(arrays),
-        scratch_shapes=[
-            pltpu.SemaphoreType.DMA((7, total)),
-            pltpu.SemaphoreType.DMA((7, total)),
-            pltpu.SemaphoreType.DMA((total,)),
-        ],
-        compiler_params=pltpu.CompilerParams(collective_id=0, has_side_effects=True),
-    )(*arrays)
+    def run(self, first, last):
+        def body(t, carry):
+            self.step(t)
+            return carry
+
+        lax.fori_loop(first, last, body, 0)
+
+    def need(self, k):
+        base = sum(n for n, _ in self.pieces[:k])
+        n, rows = self.pieces[k]
+
+        def body(j, carry):
+            for lane in (3, 4, 5, 6):
+                self.push(k, j * rows, base + j, self.me, lane, self.mate_dev).wait_recv()
+            return carry
+
+        lax.fori_loop(0, n, body, 0)
+        self.own_copy(k).wait()
+
+    def finish(self):
+        def sent(i, carry):
+            def body(k, offset):
+                self.push(k, offset, i, self.me, 0, self.first_dev, own=True).wait_send()
+                self.push(k, offset, i, self.me, 3, self.mate_dev, own=True).wait_send()
+                for lane in (1, 2, 4, 5, 6):
+                    self.push(k, offset, i, self.first, lane, self.mate_dev).wait_send()
+
+            self.each(i, body)
+            return carry
+
+        lax.fori_loop(0, self.total, sent, 0)
+
+
+class Loads:
+    steps = 0
+
+    def __init__(self, sources, fulls, local_sem):
+        self.sources, self.fulls, self.local_sem = sources, fulls, local_sem
+
+    def start(self):
+        pass
+
+    def own_copy(self, k):
+        return pltpu.make_async_copy(self.sources[k], self.fulls[k], self.local_sem.at[k])
+
+    def step(self, t):
+        pass
+
+    def run(self, first, last):
+        pass
+
+    def need(self, k):
+        self.own_copy(k).wait()
+
+    def finish(self):
+        pass
 
 
 CUT = 48
@@ -309,10 +243,11 @@
 FFN_SLOTS = 12
 
 
-def reduce_kernel(pieces, ffn_count, *refs):
+def reduce_kernel(pieces, ffn_pieces, *refs):
     count = len(pieces)
     parts = refs[:count]
-    ffn = refs[count : count + (3 if ffn_count else 0)]
+    ffn_count = sum(ffn_pieces)
+    ffn = refs[count : count + len(ffn_pieces)]
     refs = refs[len(ffn) :]
     out_a = refs[count]
     out_f = refs[count + 1] if ffn_count else None
@@ -469,16 +404,19 @@
         either(i, body)
 
     def ffn_load(j):
-        for k in range(3):
-
-            @pl.when(j // (ffn_count // 3) == k)
-            def _(k=k):
-                row = pl.multiple_of((j - k * (ffn_count // 3)) * FCUT, 16)
+        base = 0
+        for k, n in enumerate(ffn_pieces):
+
+            @pl.when((j >= base) & (j < base + n))
+            def _(k=k, base=base):
+                row = pl.multiple_of((j - base) * FCUT, 16)
                 pltpu.make_async_copy(
                     ffn[k].at[pl.ds(row, FCUT)],
                     ffn_buf.at[lax.rem(j, FFN_SLOTS)],
                     ffn_sem.at[lax.rem(j, FFN_SLOTS)],
                 ).start()
+
+            base += n
 
     def ffn_wait(j):
         pltpu.make_async_copy(
@@ -595,24 +533,23 @@
 
         kinds(j, body)
 
+    lag = max(1, 5 - ffn_count)
     stages = (
         (load, 0, total),
-        (ffn_load, 0, ffn_count),
+        (ffn_load, lag - 1, ffn_count),
         (pair, 1, total),
         (plane_one, 3, total),
         (plane_two, 5, total),
-        (inward, 5, chain_total),
-        (middle, 7, chain_total),
-        (root, 9, chain_total),
-        (outward, 11, chain_total),
-        (drain, 13, chain_total),
+        (inward, lag, chain_total),
+        (middle, lag + 2, chain_total),
+        (root, lag + 4, chain_total),
+        (outward, lag + 6, chain_total),
+        (drain, lag + 8, chain_total),
     )
-    if not ffn_count:
-        stages = stages[:1] + stages[2:]
 
     def step(t, carry):
-        for stage, lag, limit in stages:
-            i = t - lag
+        for stage, behind, limit in stages:
+            i = t - behind
 
             @pl.when((i >= 0) & (i < limit))
             def _(stage=stage, i=i):
@@ -620,7 +557,7 @@
 
         return carry
 
-    lax.fori_loop(0, chain_total + 13, step, 0)
+    lax.fori_loop(0, chain_total + lag + 8, step, 0)
     for i in range(max(total - MATE_SLOTS, 0), total):
         mate_copy(0, pl.ds(0, CUT), i % MATE_SLOTS).wait_send()
 
@@ -630,13 +567,14 @@
     total = sum(pieces)
     wide = parts[0].shape[-1]
     ffn_rows = sum(f.shape[0] for f in ffn)
-    ffn_count = ffn_rows // FCUT
+    ffn_pieces = tuple(f.shape[0] // FCUT for f in ffn)
+    ffn_count = sum(ffn_pieces)
     chain_total = total + ffn_count
     hbm = pl.BlockSpec(memory_space=pltpu.HBM)
     low = jnp.bfloat16
     dma = pltpu.SemaphoreType.DMA
     return pl.pallas_call(
-        functools.partial(reduce_kernel, pieces, ffn_count),
+        functools.partial(reduce_kernel, pieces, ffn_pieces),
         out_shape=[
             jax.ShapeDtypeStruct((total * CUT, wide), low),
             jax.ShapeDtypeStruct((ffn_rows, wide), low),
@@ -980,6 +918,717 @@
     )(act, cot, w_gate, w_up, w_down)
 
 
+PAIR = 128
+COND_ROWS = 256
+NORM_ROWS = 32
+
+
+def normalise(read, gain, shift, write, rows):
+    def block(n, carry):
+        cut = pl.ds(pl.multiple_of(n * NORM_ROWS, NORM_ROWS), NORM_ROWS)
+        write[cut] = layer_norm(read[cut].astype(jnp.float32), gain[...], shift[...]).astype(
+            write.dtype
+        )
+        return carry
+
+    lax.fori_loop(0, rows // NORM_ROWS, block, 0)
+
+
+def normalise_back(read, gain, d_read, straight, write, sums, row, rows):
+    wide = read.shape[1]
+
+    def block(n, carry):
+        d_gain, d_shift = carry
+        cut = pl.ds(pl.multiple_of(n * NORM_ROWS, NORM_ROWS), NORM_ROWS)
+        tensor = read[cut].astype(jnp.float32)
+        center = tensor - jnp.mean(tensor, axis=-1, keepdims=True)
+        spread = jnp.mean(center * center, axis=-1, keepdims=True)
+        inverse = lax.rsqrt(spread + epsilon)
+        hat = center * inverse
+        d_out = d_read[cut].astype(jnp.float32)
+        scaled = d_out * gain[...]
+        dv = inverse * (
+            scaled
+            - jnp.mean(scaled, axis=-1, keepdims=True)
+            - hat * jnp.mean(scaled * hat, axis=-1, keepdims=True)
+        )
+        write[cut] = straight[cut].astype(jnp.float32) + dv
+        d_gain = d_gain + jnp.sum((d_out * hat).reshape(NORM_ROWS // 8, 8, wide), axis=0)
+        d_shift = d_shift + jnp.sum(d_out.reshape(NORM_ROWS // 8, 8, wide), axis=0)
+        return d_gain, d_shift
+
+    zero = jnp.zeros((8, wide), jnp.float32)
+    d_gain, d_shift = lax.fori_loop(0, rows // NORM_ROWS, block, (zero, zero))
+    sums[row : row + 1] = jnp.sum(d_gain, axis=0, keepdims=True)
+    sums[row + 1 : row + 2] = jnp.sum(d_shift, axis=0, keepdims=True)
+
+
+def turn(tensor, cosine, sine_left, sine_right):
+    return (
+        tensor * cosine
+        + pltpu.roll(tensor, PAIR - HD // 4, 1) * sine_left
+        + pltpu.roll(tensor, HD // 4, 1) * sine_right
+    )
+
+
+def tiles_of(count, body):
+    def step(n, carry):
+        body(pl.ds(pl.multiple_of(n * TILE, TILE), TILE))
+        return carry
+
+    lax.fori_loop(0, count // TILE, step, 0)
+
+
+def pair_loop(body):
+    def step(p, carry):
+        body(p, pl.multiple_of(p * PAIR, PAIR))
+        return carry
+
+    lax.fori_loop(0, HEADS * HD // PAIR, step, 0)
+
+
+def first_head(rows):
+    return lax.broadcasted_iota(jnp.int32, (rows, PAIR), 1) < HD
+
+
+def head_softmax(query, key, mine, keys):
+    scores = dot_nt(jnp.where(mine, query, jnp.zeros_like(query)), key) * score_scale
+    if keys < key.shape[0]:
+        lanes = lax.broadcasted_iota(jnp.int32, scores.shape, 1)
+        scores = jnp.where(lanes < keys, scores, -1e30)
+    shifted = jnp.exp(scores - jnp.max(scores, axis=-1, keepdims=True))
+    return (shifted * (1.0 / jnp.sum(shifted, axis=-1, keepdims=True))).astype(jnp.bfloat16)
+
+
+def attend_pair(query, key, value, keys, keep):
+    mask = first_head(query.shape[0])
+    results = []
+    for head in range(2):
+        probability = head_softmax(query, key, mask if head == 0 else ~mask, keys)
+        keep(head, probability)
+        results.append(dot(probability, value))
+    return jnp.where(mask, results[0], results[1]).astype(jnp.bfloat16)
+
+
+def attend_pair_back(query, key, value, grad, probabilities):
+    mask, key_mask = first_head(query.shape[0]), first_head(key.shape[0])
+    d_queries, d_keys, d_values = [], [], []
+    for head in range(2):
+        probability = probabilities[head]
+        mine = mask if head == 0 else ~mask
+        d_prob = dot_nt(jnp.where(mine, grad, jnp.zeros_like(grad)), value)
+        wide = probability.astype(jnp.float32)
+        inner = jnp.sum(wide * d_prob, axis=-1, keepdims=True)
+        d_scores = (wide * (d_prob - inner)).astype(jnp.bfloat16)
+        d_queries.append(dot(d_scores, key))
+        d_keys.append(dot_tn(d_scores, query))
+        d_values.append(dot_tn(probability, grad))
+    return (
+        jnp.where(mask, d_queries[0], d_queries[1]) * score_scale,
+        jnp.where(key_mask, d_keys[0], d_keys[1]) * score_scale,
+        jnp.where(key_mask, d_values[0], d_values[1]),
+    )
+
+
+def attention_forward_kernel(
+    pieces,
+    x_in,
+    cond_in,
+    cosine,
+    sine_left,
+    sine_right,
+    norms_in,
+    qkv_in,
+    out_in,
+    kv2_in,
+    query2_in,
+    out2_in,
+    norms_out,
+    qkv_out,
+    out_out,
+    query2_out,
+    out2_out,
+    act_one_out,
+    heads_out,
+    prob_out,
+    flat_one_out,
+    section_one_out,
+    act_two_out,
+    query_two_out,
+    kv_two_out,
+    prob_two_out,
+    flat_two_out,
+    section_two_out,
+    act_three_out,
+    x,
+    cond,
+    norm_parts,
+    w_qkv,
+    w_out,
+    w_kv2,
+    w_query2,
+    w_out2,
+    act,
+    heads,
+    flat,
+    section,
+    query_two,
+    kv_two,
+    prob,
+    prob_two,
+    in_sem,
+    out_sem,
+    prob_sem,
+    local_sem,
+    *gather_sems,
+):
+    rows, wide = x.shape
+    low = jnp.bfloat16
+    sources = (norms_in, qkv_in, out_in, kv2_in, query2_in, out2_in)
+    fulls = (norm_parts, w_qkv, w_out, w_kv2, w_query2, w_out2)
+    if pieces is None:
+        gather = Loads(sources, fulls, local_sem)
+    else:
+        gather = Gather(pieces, sources, fulls, *gather_sems, local_sem)
+    gather.start()
+    loads = []
+    for k, (src, dst) in enumerate(((x_in, x), (cond_in, cond))):
+        loads.append(pltpu.make_async_copy(src, dst, in_sem.at[k]))
+        loads[-1].start()
+    for k in range(len(sources)):
+        gather.own_copy(k).start()
+    stores = []
+
+    def save(src, dst):
+        stores.append(pltpu.make_async_copy(src, dst, out_sem.at[len(stores)]))
+        stores[-1].start()
+        return stores[-1]
+
+    lead = GATHER_WINDOW + 2
+    gather.run(0, 1 + lead)
+    loads[0].wait()
+    gather.need(0)
+    norms_out[...] = jnp.sum(
+        norm_parts[...].astype(jnp.float32).reshape(norm_parts.shape[0] // 16, 16, wide), axis=0
+    )
+    gains = [norms_out.at[pl.ds(k, 1)] for k in range(6)]
+    normalise(x, gains[0], gains[1], act, rows)
+    act_one_done = save(act, act_one_out)
+    done = 13 + lead
+    gather.run(1 + lead, done)
+    gather.need(1)
+    save(w_qkv, qkv_out)
+
+    def project(cut, rotated):
+        result = dot_nt(act[...], w_qkv[cut])
+        for part in range(TILE // PAIR):
+            piece = result[:, part * PAIR : (part + 1) * PAIR]
+            if rotated:
+                piece = turn(piece, cosine[...], sine_left[...], sine_right[...])
+            heads[:, pl.ds(pl.multiple_of(cut.start + part * PAIR, PAIR), PAIR)] = piece.astype(low)
+
+    for part in range(3):
+        tiles_of(
+            wide,
+            lambda cut, part=part: project(
+                pl.ds(pl.multiple_of(cut.start + part * wide, TILE), TILE), part < 2
+            ),
+        )
+        gather.step(done + part)
+    done += 3
+    save(heads, heads_out)
+
+    def prob_copy(buf, out, p, slot):
+        return pltpu.make_async_copy(buf.at[slot], out.at[p], prob_sem.at[slot])
+
+    def self_pair(p, lane):
+        slot = lax.rem(p, 2)
+
+        @pl.when(p >= 2)
+        def _():
+            prob_copy(prob, prob_out, p, slot).wait()
+
+        def keep(head, probability):
+            prob[slot, head] = probability
+
+        cols = [pl.ds(pl.multiple_of(lane + k * wide, PAIR), PAIR) for k in range(3)]
+        flat[:, cols[0]] = attend_pair(
+            heads[:, cols[0]], heads[:, cols[1]], heads[:, cols[2]], rows, keep
+        )
+        prob_copy(prob, prob_out, p, slot).start()
+        serve(p, SELF_EVERY)
+
+    def serve(p, every):
+        if gather.steps:
+
+            @pl.when(lax.rem(p, every) == every - 1)
+            def _():
+                gather.step(done + p // every)
+
+    pairs = wide // PAIR
+    pair_loop(self_pair)
+    done += pairs // SELF_EVERY
+    for slot in range(2):
+        prob_copy(prob, prob_out, 0, slot).wait()
+    flat_one_done = save(flat, flat_one_out)
+    gather.run(done, 17 + lead)
+    done = max(done, 17 + lead)
+    gather.need(2)
+    save(w_out, out_out)
+
+    def first_section(cut):
+        section[:, cut] = x[:, cut].astype(jnp.float32) + dot_nt(flat[...], w_out[cut])
+
+    tiles_of(wide, first_section)
+    section_one_done = save(section, section_one_out)
+    gather.run(done, 21 + lead)
+    gather.step(max(done, 21 + lead))
+    done = max(done, 21 + lead) + 1
+    act_one_done.wait()
+    normalise(section, gains[2], gains[3], act, rows)
+    act_two_done = save(act, act_two_out)
+    loads[1].wait()
+    gather.need(3)
+
+    def condition(cut):
+        kv_two[:, cut] = dot_nt(cond[...], w_kv2[cut]).astype(low)
+
+    tiles_of(2 * wide, condition)
+    save(kv_two, kv_two_out)
+    gather.run(done, 25 + lead)
+    done = max(done, 25 + lead)
+    gather.need(4)
+    save(w_query2, query2_out)
+
+    def query(cut):
+        query_two[:, cut] = dot_nt(act[...], w_query2[cut]).astype(low)
+
+    tiles_of(wide, query)
+    save(query_two, query_two_out)
+    flat_one_done.wait()
+
+    def cross_pair(p, lane):
+        slot = lax.rem(p, 2)
+
+        @pl.when(p >= 2)
+        def _():
+            prob_copy(prob_two, prob_two_out, p, slot).wait()
+
+        def keep(head, probability):
+            prob_two[slot, head] = probability
+
+        cols = [pl.ds(pl.multiple_of(lane + k * wide, PAIR), PAIR) for k in range(2)]
+        flat[:, cols[0]] = attend_pair(
+            query_two[:, cols[0]], kv_two[:, cols[0]], kv_two[:, cols[1]], NC, keep
+        )
+        prob_copy(prob_two, prob_two_out, p, slot).start()
+        serve(p, CROSS_EVERY)
+
+    pair_loop(cross_pair)
+    done += pairs // CROSS_EVERY
+    gather.run(done, 29 + lead)
+    for slot in range(2):
+        prob_copy(prob_two, prob_two_out, 0, slot).wait()
+    save(flat, flat_two_out)
+    gather.need(5)
+    save(w_out2, out2_out)
+    section_one_done.wait()
+
+    def second_section(cut):
+        section[:, cut] = section[:, cut] + dot_nt(flat[...], w_out2[cut])
+
+    tiles_of(wide, second_section)
+    save(section, section_two_out)
+    act_two_done.wait()
+    normalise(section, gains[4], gains[5], act, rows)
+    save(act, act_three_out)
+    waited = [id(c) for c in (act_one_done, flat_one_done, section_one_done, act_two_done)]
+    gather.finish()
+    for copy in stores:
+        if id(copy) not in waited:
+            copy.wait()
+
+
+SELF_EVERY = 2
+CROSS_EVERY = 3
+
+
+def attention_forward(x, cond, tables, norms, weights):
+    rows, wide = x.shape
+    low, full = jnp.bfloat16, jnp.float32
+    pairs = wide // PAIR
+    hbm = pl.BlockSpec(memory_space=pltpu.HBM)
+    vmem = pl.BlockSpec(memory_space=pltpu.VMEM)
+    dma = pltpu.SemaphoreType.DMA
+    shape = jax.ShapeDtypeStruct
+    groups = lax.axis_size("grp")
+    parameters = [norms] + list(weights)
+    whole = [(groups * w.shape[0], w.shape[1]) for w in parameters]
+    sems = []
+    pieces = None
+    options = {}
+    if groups == 8 and lax.axis_size("rep") % 2 == 0:
+        piece_rows = (16, 48, 48, 96, 48, 48)
+        pieces = tuple((w.shape[0] // n, n) for w, n in zip(parameters, piece_rows))
+        total = sum(n for n, _ in pieces)
+        sems = [dma((7, total)), dma((7, total))]
+        options = dict(collective_id=0, has_side_effects=True)
+    else:
+        parameters = [lax.all_gather(w, "grp", axis=0, tiled=True) for w in parameters]
+    results = pl.pallas_call(
+        functools.partial(attention_forward_kernel, pieces),
+        out_shape=[
+            shape((16, wide), full),
+            *[shape(whole[k], low) for k in (1, 2, 4, 5)],
+            shape((rows, wide), low),
+            shape((rows, 3 * wide), low),
+            shape((pairs, 2, rows, rows), low),
+            shape((rows, wide), low),
+            shape((rows, wide), full),
+            shape((rows, wide), low),
+            shape((rows, wide), low),
+            shape((COND_ROWS, 2 * wide), low),
+            shape((pairs, 2, rows, COND_ROWS), low),
+            shape((rows, wide), low),
+            shape((rows, wide), full),
+            shape((rows, wide), low),
+        ],
+        in_specs=[hbm, hbm] + [vmem] * 3 + [hbm] * 6,
+        out_specs=[vmem] + [hbm] * 16,
+        scratch_shapes=[
+            pltpu.VMEM((rows, wide), low),
+            pltpu.VMEM(cond.shape, low),
+            *[pltpu.VMEM(s, low) for s in whole],
+            pltpu.VMEM((rows, wide), low),
+            pltpu.VMEM((rows, 3 * wide), low),
+            pltpu.VMEM((rows, wide), low),
+            pltpu.VMEM((rows, wide), full),
+            pltpu.VMEM((rows, wide), low),
+            pltpu.VMEM((COND_ROWS, 2 * wide), low),
+            pltpu.VMEM((2, 2, rows, rows), low),
+            pltpu.VMEM((2, 2, rows, COND_ROWS), low),
+            dma((2,)),
+            dma((14,)),
+            dma((2,)),
+            dma((6,)),
+            *sems,
+        ],
+        compiler_params=pltpu.CompilerParams(vmem_limit_bytes=VMEM_LIMIT, **options),
+    )(x, cond, *tables, *parameters)
+    return results[0], results[1:5], results[5:]
+
+
+def attention_backward_kernel(
+    x_in,
+    cond_in,
+    norms,
+    cosine,
+    sine_left,
+    sine_right,
+    qkv_in,
+    out_in,
+    query2_in,
+    out2_in,
+    act_one_in,
+    heads_in,
+    prob_in,
+    flat_one_in,
+    section_one_in,
+    act_two_in,
+    query_two_in,
+    kv_two_in,
+    prob_two_in,
+    flat_two_in,
+    section_two_in,
+    d_norm_in,
+    d_out_in,
+    d_inputs_out,
+    sums,
+    grad_qkv,
+    grad_out,
+    grad_query2,
+    grad_out2,
+    grad_kv2,
+    w_qkv,
+    w_out,
+    w_query2,
+    w_out2,
+    x,
+    cond,
+    act_one,
+    heads,
+    flat_one,
+    section_one,
+    act_two,
+    query_two,
+    kv_two,
+    flat_two,
+    section_two,
+    d_norm,
+    d_low,
+    d_heads,
+    d_kv,
+    d_att,
+    prob,
+    prob_two,
+    grad_buf,
+    in_sem,
+    prob_sem,
+    grad_sem,
+    end_sem,
+):
+    rows, wide = x.shape
+    low = jnp.bfloat16
+    loads = {}
+    for k, (name, src, dst) in enumerate(
+        (
+            ("section_two", section_two_in, section_two),
+            ("d_norm", d_norm_in, d_norm),
+            ("d_out", d_out_in, d_low),
+            ("w_out2", out2_in, w_out2),
+            ("flat_two", flat_two_in, flat_two),
+            ("query_two", query_two_in, query_two),
+            ("kv_two", kv_two_in, kv_two),
+            ("cond", cond_in, cond),
+            ("act_two", act_two_in, act_two),
+            ("w_query2", query2_in, w_query2),
+            ("section_one", section_one_in, section_one),
+            ("w_out", out_in, w_out),
+            ("flat_one", flat_one_in, flat_one),
+            ("heads", heads_in, heads),
+            ("act_one", act_one_in, act_one),
+            ("x", x_in, x),
+            ("w_qkv", qkv_in, w_qkv),
+        )
+    ):
+        loads[name] = pltpu.make_async_copy(src, dst, in_sem.at[k])
+        loads[name].start()
+
+    def need(*names):
+        for name in names:
+            loads[name].wait()
+
+    gains = [norms.at[pl.ds(2 * k, 1)] for k in range(3)]
+
+    def prob_copy(src, buf, p, slot):
+        return pltpu.make_async_copy(src.at[p], buf.at[slot], prob_sem.at[slot])
+
+    def prob_start(src, buf):
+        for p in range(2):
+            prob_copy(src, buf, p, p).start()
+
+    pairs = wide // PAIR
+    used = [0]
+
+    def grad_copy(target, cut, slot):
+        return pltpu.make_async_copy(grad_buf.at[slot], target.at[cut], grad_sem.at[slot])
+
+    def weight_rows(left, right, target, count):
+        before = used[0]
+
+        def step(n, carry):
+            cut = pl.ds(pl.multiple_of(n * TILE, TILE), TILE)
+            slot = lax.rem(n + before, 2)
+
+            @pl.when(n + before >= 2)
+            def _():
+                grad_copy(target, cut, slot).wait()
+
+            columns = left[:, cut]
+            for m in range(wide // 512):
+                piece = slice(m * 512, (m + 1) * 512)
+                grad_buf[slot, :, piece] = dot_tn(columns, right[:, piece]).astype(low)
+            grad_copy(target, cut, slot).start()
+            return carry
+
+        lax.fori_loop(0, count // TILE, step, 0)
+        used[0] = before + count // TILE
+
+    prob_start(prob_two_in, prob_two)
+    need("section_two", "d_norm", "d_out")
+    normalise_back(section_two, gains[2], d_norm, d_low, section_two, sums, 4, rows)
+    d_section = section_two
+
+    def round_rows():
+        def block(n, carry):
+            cut = pl.ds(pl.multiple_of(n * NORM_ROWS, NORM_ROWS), NORM_ROWS)
+            d_low[cut] = d_section[cut].astype(low)
+            return carry
+
+        lax.fori_loop(0, rows // NORM_ROWS, block, 0)
+
+    round_rows()
+    need("w_out2")
+
+    def through(weight):
+        def body(cut):
+            d_att[:, cut] = dot(d_low[...], weight[:, cut]).astype(low)
+
+        tiles_of(wide, body)
+
+    through(w_out2)
+    need("flat_two")
+    weight_rows(d_low, flat_two, grad_out2, wide)
+    need("query_two", "kv_two")
+
+    def cross_pair(p, lane):
+        slot = lax.rem(p, 2)
+        prob_copy(prob_two_in, prob_two, p, slot).wait()
+        cols = [pl.ds(pl.multiple_of(lane + k * wide, PAIR), PAIR) for k in range(2)]
+        d_query, d_key, d_value = attend_pair_back(
+            query_two[:, cols[0]],
+            kv_two[:, cols[0]],
+            kv_two[:, cols[1]],
+            d_att[:, cols[0]],
+            [prob_two[slot, head] for head in range(2)],
+        )
+        d_low[:, cols[0]] = d_query.astype(low)
+        d_kv[:, cols[0]] = d_key.astype(low)
+        d_kv[:, cols[1]] = d_value.astype(low)
+
+        @pl.when(p + 2 < pairs)
+        def _():
+            prob_copy(prob_two_in, prob_two, p + 2, slot).start()
+
+    pair_loop(cross_pair)
+    prob_start(prob_in, prob)
+    need("w_query2")
+
+    def second_norm(cut):
+        d_norm[:, cut] = dot(d_low[...], w_query2[:, cut]).astype(low)
+
+    tiles_of(wide, second_norm)
+    need("act_two")
+    weight_rows(d_low, act_two, grad_query2, wide)
+    need("cond")
+    blocks = 2 * wide // 384
+    before = used[0]
+
+    def cond_rows(n, carry):
+        slot = lax.rem(n + before, 2)
+        part = grad_buf.at[slot, pl.ds(0, 192)]
+        copy = pltpu.make_async_copy(
+            part, grad_kv2.at[pl.ds(pl.multiple_of(n * 192, 16), 192)], grad_sem.at[slot]
+        )
+
+        @pl.when(n < 2)
+        def _():
+            grad_copy(grad_qkv, pl.ds(0, TILE), slot).wait()
+
+        @pl.when(n >= 2)
+        def _():
+            copy.wait()
+
+        result = dot_tn(d_kv[:, pl.ds(pl.multiple_of(n * 384, 128), 384)], cond[...]).astype(low)
+        grad_buf[slot, :192, : wide // 2] = result[:192]
+        grad_buf[slot, :192, wide // 2 :] = result[192:]
+        copy.start()
+        return carry
+
+    lax.fori_loop(0, blocks, cond_rows, 0)
+    for slot in range(2):
+        pltpu.make_async_copy(
+            grad_buf.at[slot, pl.ds(0, 192)], grad_kv2.at[pl.ds(0, 192)], grad_sem.at[slot]
+        ).wait()
+    used[0] = 0
+    need("section_one")
+    normalise_back(section_one, gains[1], d_norm, d_section, d_section, sums, 2, rows)
+    round_rows()
+    need("w_out")
+    through(w_out)
+    need("flat_one")
+    weight_rows(d_low, flat_one, grad_out, wide)
+    need("heads")
+
+    def self_pair(p, lane):
+        slot = lax.rem(p, 2)
+        prob_copy(prob_in, prob, p, slot).wait()
+        cols = [pl.ds(pl.multiple_of(lane + k * wide, PAIR), PAIR) for k in range(3)]
+        d_query, d_key, d_value = attend_pair_back(
+            heads[:, cols[0]],
+            heads[:, cols[1]],
+            heads[:, cols[2]],
+            d_att[:, cols[0]],
+            [prob[slot, head] for head in range(2)],
+        )
+        back = (cosine[...], -sine_left[...], -sine_right[...])
+        d_heads[:, cols[0]] = turn(d_query, *back).astype(low)
+        d_heads[:, cols[1]] = turn(d_key, *back).astype(low)
+        d_heads[:, cols[2]] = d_value.astype(low)
+
+        @pl.when(p + 2 < pairs)
+        def _():
+            prob_copy(prob_in, prob, p + 2, slot).start()
+
+    pair_loop(self_pair)
+    need("act_one")
+    weight_rows(d_heads, act_one, grad_qkv, 3 * wide)
+    need("w_qkv")
+
+    def first_norm(cut):
+        d_norm[:, cut] = dot(d_heads[...], w_qkv[:, cut]).astype(low)
+
+    tiles_of(wide, first_norm)
+    need("x")
+    normalise_back(x, gains[0], d_norm, d_section, d_section, sums, 0, rows)
+    end = pltpu.make_async_copy(d_section, d_inputs_out, end_sem)
+    end.start()
+    for slot in range(2):
+        grad_copy(grad_qkv, pl.ds(0, TILE), slot).wait()
+    end.wait()
+
+
+def attention_backward(x, cond, norms, tables, weights, kept, d_norm, d_out):
+    rows, wide = x.shape
+    low, full = jnp.bfloat16, jnp.float32
+    hbm = pl.BlockSpec(memory_space=pltpu.HBM)
+    vmem = pl.BlockSpec(memory_space=pltpu.VMEM)
+    dma = pltpu.SemaphoreType.DMA
+    shape = jax.ShapeDtypeStruct
+    buf = lambda s, t=low: pltpu.VMEM(s, t)
+    return pl.pallas_call(
+        attention_backward_kernel,
+        out_shape=[
+            shape((rows, wide), full),
+            shape((8, wide), full),
+            shape((3 * wide, wide), low),
+            shape((wide, wide), low),
+            shape((wide, wide), low),
+            shape((wide, wide), low),
+            shape((wide, wide), low),
+        ],
+        in_specs=[hbm, hbm] + [vmem] * 4 + [hbm] * 17,
+        out_specs=[hbm, vmem] + [hbm] * 5,
+        scratch_shapes=[
+            *[buf(w.shape) for w in weights],
+            buf((rows, wide)),
+            buf(cond.shape),
+            buf((rows, wide)),
+            buf((rows, 3 * wide)),
+            buf((rows, wide)),
+            buf((rows, wide), full),
+            buf((rows, wide)),
+            buf((rows, wide)),
+            buf((COND_ROWS, 2 * wide)),
+            buf((rows, wide)),
+            buf((rows, wide), full),
+            buf((rows, wide)),
+            buf((rows, wide)),
+            buf((rows, 3 * wide)),
+            buf((COND_ROWS, 2 * wide)),
+            buf((rows, wide)),
+            buf((2, 2, rows, rows)),
+            buf((2, 2, rows, COND_ROWS)),
+            buf((2, TILE, wide)),
+            dma((17,)),
+            dma((2,)),
+            dma((2,)),
+            dma,
+        ],
+        compiler_params=pltpu.CompilerParams(vmem_limit_bytes=VMEM_LIMIT),
+    )(x, cond, norms, *tables, *weights, *kept, d_norm, d_out)
+
+
 def per_device(
     inputs,
     conditioning,
@@ -1001,49 +1650,24 @@
     w_up,
     w_down,
 ):
-    tokens = inputs[0].astype(jnp.float32)
-    seq_len = tokens.shape[0]
     cond_rows = conditioning[0]
     norms = jnp.stack(
         [norm1_gain, norm1_shift, norm2_gain, norm2_shift, norm3_gain, norm3_shift], axis=0
     )
     own_width = norms.shape[1]
-    norms = jnp.pad(norms, ((0, 10), (0, -own_width % 128)))
-    norms, full_qkv, full_out, full_kv2, full_query2, full_out2 = gather_all(
-        [norms, w_qkv, w_out, w_kv2, w_query2, w_out2], [16, 48, 48, 96, 48, 48]
+    norms = lax.dynamic_update_slice(
+        jnp.zeros((16, D), norms.dtype), norms, (0, lax.axis_index("grp") * own_width)
     )
-    norms = jnp.swapaxes(norms[:, :6, :own_width], 0, 1).reshape(6, D).astype(jnp.float32)
-    gain_one, shift_one, gain_two, shift_two, gain_three, shift_three = (norms[k] for k in range(6))
-    full_qkv = full_qkv.reshape(-1, D)
-    full_out = full_out.reshape(-1, D)
-    full_kv2 = full_kv2.reshape(-1, cond_rows.shape[1])
-    full_query2 = full_query2.reshape(-1, D)
-    full_out2 = full_out2.reshape(-1, D)
-    cosine, sin_table = angles(positions[0], HD)
-    act_one = layer_norm(tokens, gain_one, shift_one).astype(jnp.bfloat16)
-    qkv_rows = dot_nt(act_one, full_qkv)
-    queries = rotate(qkv_rows[:, :D].reshape(seq_len, HEADS, HD), cosine, sin_table).astype(
+    grad_mlp = (cotangent[0].astype(jnp.float32) * slot_valid[0].astype(jnp.float32)).astype(
         jnp.bfloat16
     )
-    key_heads = rotate(
-        qkv_rows[:, D : 2 * D].reshape(seq_len, HEADS, HD), cosine, sin_table
-    ).astype(jnp.bfloat16)
-    value_heads = qkv_rows[:, 2 * D :].reshape(seq_len, HEADS, HD).astype(jnp.bfloat16)
-    attended, log_one = attend(queries, key_heads, value_heads)
-    flat_one = attended.reshape(seq_len, D)
-    section_one = tokens + dot_nt(flat_one, full_out)
-    act_two = layer_norm(section_one, gain_two, shift_two).astype(jnp.bfloat16)
-    query_two = dot_nt(act_two, full_query2).astype(jnp.bfloat16).reshape(seq_len, HEADS, HD)
-    kv_two = dot_nt(cond_rows, full_kv2).astype(jnp.bfloat16)
-    key_two = kv_two[:, :D].reshape(NC, HEADS, HD)
-    value_two = kv_two[:, D:].reshape(NC, HEADS, HD)
-    attended_two, log_two = attend(query_two, key_two, value_two)
-    flat_two = attended_two.reshape(seq_len, D)
-    section_two = section_one + dot_nt(flat_two, full_out2)
-    act_three = layer_norm(section_two, gain_three, shift_three).astype(jnp.bfloat16)
-    grad_out = cotangent[0].astype(jnp.float32) * slot_valid[0].astype(jnp.float32)
-    grad_mlp = grad_out.astype(jnp.bfloat16)
     all_grad = lax.all_gather(grad_mlp, "grp", axis=0, tiled=True)
+    tables = turn_tables(positions[0])
+    padded_cond = jnp.pad(cond_rows, ((0, COND_ROWS - NC), (0, 0)))
+    norms, whole, kept = attention_forward(
+        inputs[0], padded_cond, tables, norms, [w_qkv, w_out, w_kv2, w_query2, w_out2]
+    )
+    act_three, section_two = kept[-1], kept[-2]
     if lax.axis_size("grp") == 8:
         mlp_out, d_norm3, grad_gate, grad_up, grad_down = ffn_all(
             act_three, all_grad, w_gate, w_up, w_down
@@ -1065,58 +1689,31 @@
         grad_up = dot_tn(d_up, all_act).astype(jnp.bfloat16)
         grad_down = dot_tn(hidden, all_grad).astype(jnp.bfloat16)
     outputs = (section_two + mlp_out.astype(jnp.float32)).astype(jnp.bfloat16)
-    d_norm3 = d_norm3.astype(jnp.float32)
-    ffn_sums = lax.psum((grad_gate, grad_up, grad_down), "rep")
-    d_ln_three, d_gain_three, d_shift_three = norm_back(
-        section_two, gain_three, shift_three, d_norm3
+    ffn_sums = list(lax.psum((grad_gate, grad_up), "rep"))
+    d_tokens, norm_sums, grad_qkv, grad_out_one, grad_query_two, grad_out_two, grad_kv_two = (
+        attention_backward(
+            inputs[0],
+            padded_cond,
+            norms,
+            tables,
+            whole,
+            kept[:-1],
+            d_norm3,
+            grad_mlp,
+        )
     )
-    d_section_two = grad_out + d_ln_three
-    d_cross = d_section_two.astype(jnp.bfloat16)
-    grad_out_two = part_grad(d_cross, flat_two)
-    d_att_two = dot(d_cross, full_out2).astype(jnp.bfloat16).reshape(seq_len, HEADS, HD)
-    d_query_full, d_key_full, d_value_full = attend_back(
-        query_two, key_two, value_two, log_two, d_att_two
-    )
-    d_query_two = d_query_full.reshape(seq_len, D).astype(jnp.bfloat16)
-    d_kv_two = jnp.concatenate(
-        [d_key_full.reshape(NC, D), d_value_full.reshape(NC, D)], axis=1
-    ).astype(jnp.bfloat16)
-    grad_query_two = part_grad(d_query_two, act_two)
-    grad_kv_two = part_grad(d_kv_two, cond_rows)
-    d_norm2 = dot(d_query_two, full_query2)
-    d_ln_two, d_gain_two, d_shift_two = norm_back(section_one, gain_two, shift_two, d_norm2)
-    d_section_one = d_section_two + d_ln_two
-    d_attn = d_section_one.astype(jnp.bfloat16)
-    grad_out_one = part_grad(d_attn, flat_one)
-    d_att = dot(d_attn, full_out).astype(jnp.bfloat16).reshape(seq_len, HEADS, HD)
-    d_query, d_key, d_value = attend_back(queries, key_heads, value_heads, log_one, d_att)
-    d_qkv = jnp.concatenate(
-        [
-            rotate(d_query, cosine, -sin_table).reshape(seq_len, D),
-            rotate(d_key, cosine, -sin_table).reshape(seq_len, D),
-            d_value.reshape(seq_len, D),
-        ],
-        axis=1,
-    ).astype(jnp.bfloat16)
-    grad_qkv = part_grad(d_qkv, act_one)
-    d_norm1 = dot(d_qkv, full_qkv)
-    d_ln_one, d_gain_one, d_shift_one = norm_back(tokens, gain_one, shift_one, d_norm1)
-    d_tokens = d_section_one + d_ln_one
-    norm_stack = jnp.stack(
-        [d_gain_one, d_shift_one, d_gain_two, d_shift_two, d_gain_three, d_shift_three], axis=0
-    ).astype(jnp.bfloat16)
+    norm_stack = norm_sums[:6].astype(jnp.bfloat16)
     groups = lax.axis_size("grp")
     attention_parts = [grad_qkv, grad_out_one, grad_query_two, grad_out_two, grad_kv_two]
     if groups == 8 and lax.axis_size("rep") == 4:
         norm_part = jnp.swapaxes(norm_stack.reshape(6, groups, own_width), 0, 1)
         norm_part = norm_part.reshape(groups, 1, 6 * own_width)
         norm_part = jnp.pad(norm_part, ((0, 0), (0, CUT - 1), (0, D - 6 * own_width)))
-        kv2_rows = grad_kv_two.shape[0] // groups // 2
-        kv2_part = grad_kv_two.reshape(groups, 2, kv2_rows, D // 2)
-        kv2_part = jnp.swapaxes(kv2_part, 1, 2).reshape(groups, kv2_rows, D)
-        parts = attention_parts[:4] + [kv2_part, norm_part]
+        kv2_rows = grad_kv_two.shape[0] // groups
+        parts = attention_parts + [norm_part]
         parts = [p.reshape(2, 2, 2, -1, D) for p in parts]
-        (total_a,) = reduce_all(parts, [])
+        total_a, total_f = reduce_all(parts, [grad_down])
+        ffn_sums.append(total_f)
         ends = []
         for p in parts:
             ends.append((ends[-1] if ends else 0) + p.shape[3])
@@ -1126,6 +1723,8 @@
         pieces[4] = kv2_total.reshape(2 * kv2_rows, D // 2)
         attention_sums = pieces[:5]
     else:
+        kv2_part = jnp.swapaxes(grad_kv_two.reshape(-1, 192, 2, D // 2), 1, 2)
+        attention_parts[4] = kv2_part.reshape(2 * D, D // 2)
         norm_total = lax.psum(norm_stack, ("grp", "rep"))
         norm_total = lax.dynamic_slice_in_dim(
             norm_total, lax.axis_index("grp") * own_width, own_width, axis=1
@@ -1134,6 +1733,7 @@
             lax.psum_scatter(g, "grp", scatter_dimension=0, tiled=True) for g in attention_parts
         ]
         attention_sums = [lax.psum(g, "rep") for g in attention_sums]
+        ffn_sums.append(lax.psum(grad_down, "rep"))
     norm_total = norm_total.astype(jnp.float32)
     grad_qkv, grad_out_one, grad_query_two, grad_out_two, grad_kv_two = (
         g.astype(jnp.float32) for g in attention_sums

time: 861 us -> 693 us (0.80)
  matrix products: 137 us -> 0 us
  Pallas kernels: 564 us -> 640 us
  local copies, waits for them, and re-layouts: 73.6 us -> 12.9 us
  other arithmetic: 62 us -> 24 us
    dot_general x26 -> x0, matrix products: 137 us -> none  [the longest x5 34.4 us: dot_tn(): lax.dot_general(left_side, right_side, (((0,), (0,)), ((), ())), preferre...]
    pallas_call x2 -> x3, Pallas kernels: 426 us -> 503 us  [the longest x1 253 us: reduce_all(): pl.pallas_call(functools.partial(reduce_kernel, pieces, ffn_pieces), out_...]
    reduce_sum x11 -> x0, other arithmetic: 22.3 us -> none  [the longest x3 8.46 us: layer_norm(): return center * lax.rsqrt(spread + epsilon) * gain + shift]
    slice x11 -> x1, local copies, waits for them, and re-layouts: 19 us -> 0.81 us  [per_device(): norm_stack = norm_sums[:6].astype(jnp.bfloat16)]
    unnamed x225 -> x28, local copies, waits for them, and re-layouts: 19.9 us -> 1.9 us
    reshape x3 -> x2, local copies, waits for them, and re-layouts: 11.5 us -> 0.11 us  [per_device(): norm_part = jnp.swapaxes(norm_stack.reshape(6, groups, own_width), 0, 1)]
    convert_element_type x7 -> x3, other arithmetic: 13.6 us -> 3.7 us  [the longest x2 3.68 us: per_device(): (cotangent[0].astype(jnp.float32) * slot_valid[0].astype(jnp.float32)).as...]
    another operation x8 -> x6, local copies, waits for them, and re-layouts: 11.9 us -> 2.48 us  [heads(): return jnp.tile(jnp.concatenate(parts, axis=1), (1, 2))]
  transfers between devices with their start and end apart: 2 -> 2, of which waited for: 0 -> 0; matrix products, arithmetic and copies ran while one was open for 18% -> 4% of each run, Pallas kernels for 50% -> 73%
where the time goes in v3:
time: 693 us; the launch traced here: 692 us
  Pallas kernels  640 us (92%)
  other arithmetic  24 us (3%)
  between operations  15 us (2%)
  local copies, waits for them, and re-layouts  12.9 us (2%)
    pallas_call x1, Pallas kernels, reduce_all(): pl.pallas_call(functools.partial(reduce_kernel, pieces, ffn_pieces), out_...  253 us
    pallas_call x1, Pallas kernels, attention_forward(): pl.pallas_call(functools.partial(attention_forward_kernel, pieces), out_s...  156 us
    pallas_call x1, Pallas kernels, ffn_all(): pl.pallas_call(ffn_kernel, out_shape=[jax.ShapeDtypeStruct((seq_len, wide...  137 us
    pallas_call x1, Pallas kernels, attention_backward(): pl.pallas_call(attention_backward_kernel, out_shape=[shape((rows, wide),...  94.7 us
  transfers between devices with their start and end apart: 2, of which 0 were waited for; matrix products, arithmetic and copies ran while one was open for 4% of the time, Pallas kernels for 73%

profile of v3, /device:TPU:24, one launch (start us, length us, event | category | flops | bytes accessed | tf_op | source)
XLA Modules:
  0.0 692.3 jit_solution(3709531702135261306)
XLA Ops:
  7.2 0.0 copy-start.8
  7.2 0.0 copy-start.9
  7.2 0.0 copy-start.10
  7.2 0.0 copy-start.11
  7.2 0.0 copy-start.12
  7.2 0.0 copy-start.13
  7.2 0.0 copy-start.7
  7.3 0.0 all-gather.3.cloned.1.call-start
  7.9 2.5 multiply_convert_fusion
  10.4 0.0 copy-start.5
  10.4 0.0 all-gather.3.cloned.1.call-update
  10.5 0.0 all-reduce.6.cloned.1.call-start
  10.5 0.1 pad.16.clone
  10.6 0.1 pad.13.clone
  10.7 0.0 copy-done.8
  10.7 0.0 copy-done.9
  10.7 0.0 copy-done.10
  10.7 0.0 copy-done.11
  10.8 0.0 copy-done.12
  10.8 0.0 copy-done.13
  10.8 0.0 copy-done.7
  10.8 0.2 multiply_sine_fusion
  11.1 0.8 copy.38.sine_left
  11.9 0.1 maximum_maximum_fusion
  12.0 0.8 copy.37.cosine
  12.8 0.8 copy.39.sine_right
  13.6 0.0 copy-done.5
  13.6 0.8 pad.9.cond_in
  14.4 0.5 dynamic_update_slice.3.norms_in
  14.9 0.0 copy-start.6
  14.9 0.6 copy-done.6
  15.6 155.5 %shard_map.306 = (f32[16,1536]{1,0:T(8,128)}, bf16[4608,1536]{1,0:T(8,128)(2,1)}, bf16[1536,1536]{1,0:T(8,128)(2,1)}, bf16[1536,1536]{1,0:T(8,128)(2,1)}, bf16[1...) custom-call(bf16[384,1536]{1,0:T(8,128)(2,1)} %bitcast.37, ...), custom_call_target="tpu_custom_call" | custom-call | tf_op jit(solution)/shard_map/pallas_call | solution.py:1278
  171.1 0.0 all-gather.3.cloned.1.call-done
  171.1 137.1 %shard_map.307 = (bf16[384,1536]{1,0:T(8,128)(2,1)}, bf16[384,1536]{1,0:T(8,128)(2,1)}, bf16[768,1536]{1,0:T(8,128)(2,1)}, bf16[768,1536]{1,0:T(8,128)(2,1)}, bf16[768,1536]{1,0:T(8,128)(2,1)}) custom-call(bf16[384,1536]{1,0:T(8,128)(2,1)} %get-tuple-element.48.act_in, bf16[3072,1536]{1,0:T(8,128)(2,1)} %bitcast.30, bf16[768,1536]{1,0:T(8,128)(2,1)} %gate_in.1, ...), custom_call_target="tpu_custom_call" | custom-call | tf_op jit(solution)/shard_map/pallas_call | solution.py:882
  308.2 0.0 copy-start.1
  308.2 0.0 all-reduce.6.cloned.1.call-update
  308.2 1.2 copy-done.1
  309.5 1.2 fusion.3.d_out_in
  310.7 94.7 %shard_map.308 = (f32[384,1536]{1,0:T(8,128)}, f32[8,1536]{1,0:T(8,128)}, bf16[4608,1536]{1,0:T(8,128)(2,1)}, bf16[1536,1536]{1,0:T(8,128)(2,1)}, bf16[1536,1536...) custom-call(bf16[384,1536]{1,0:T(8,128)(2,1)} %bitcast.38, bf16[256,768]{1,0:T(8,128)(2,1)} %pad.9.cond_in, ...), custom_call_target="tpu_custom_call" | custom-call | tf_op jit(solution)/shard_map/pallas_call | solution.py:1589
  405.4 0.8 slice.75
  406.2 0.1 reshape.108
  406.3 0.1 reshape.115
  406.4 1.1 pad.10.clone
  407.5 253.0 %shard_map.309 = (bf16[1392,1536]{1,0:T(8,128)(2,1)}, bf16[768,1536]{1,0:T(8,128)(2,1)}) custom-call(bf16[2,2,2,576,1536]{4,3,2,1,0:T(8,128)(2,1)} %bitcast.29, bf16[2,2,2,192,1536]{4,3,2,1,0:T(8,128)(2,1)} %bitcast.31, bf16[2,2,2,192,1536]{4,3,2,1,0:T(8,128)(2,1)} %bitcast.32, bf16[2,2,2,192,1536]{4,3,2,1,0:T(8,128)(2,1)} %bitcast.33, ...), custom_call_target="tpu_custom_call" | custom-call | tf_op jit(solution)/shard_map/pallas_call | solution.py:576
  660.5 0.0 copy-start.2
  660.5 4.6 convert_element_type.93
  665.2 0.0 copy-done.2
  665.2 2.0 slice_convert_fusion.1
  667.2 0.0 copy-start
  667.2 1.8 reshape.112
  669.0 0.0 copy-start.4
  669.0 2.5 copy.45
  671.5 0.7 slice_convert_fusion.6
  672.2 0.6 fusion.2
  672.8 0.0 copy-done
  672.8 0.0 copy-done.4
  672.8 1.4 fusion
  674.2 3.7 slice_convert_fusion
  678.0 0.0 all-reduce.6.cloned.1.call-done
  678.0 0.0 copy-start.3
  678.0 4.6 convert_element_type.91
  682.6 0.0 copy-done.3
  682.6 2.8 convert_element_type.92
  (19 shorter events, 0.2 us)
Async XLA Ops:
  7.2 3.5 copy-start.8
  7.2 3.5 copy-start.9
  7.2 3.5 copy-start.10
  7.2 3.5 copy-start.11
  7.2 3.5 copy-start.12
  7.2 3.5 copy-start.13
  7.2 3.6 copy-start.7
  7.3 163.9 %all-gather.3.cloned.1.call-start = ((), (), s32[]{:S(2)}) async-start(), calls=%async_computation | async-start | bytes 10616832 | tf_op jit(solution)/shard_map/all_gather | solution.py:1664
  10.4 3.2 copy-start.5
  10.5 667.5 %all-reduce.6.cloned.1.call-start = ((), (), s32[]{:S(2)}) async-start(), calls=%async_computation.1 | async-start | bytes 9437184 | tf_op jit(solution)/shard_map/psum | solution.py:1692
  14.9 0.6 copy-start.6
  308.2 1.3 copy-start.1
  660.5 4.7 copy-start.2
  667.2 5.6 copy-start
  669.0 3.8 copy-start.4
  678.0 4.7 copy-start.3
Sparse Core Ops, SparseCore 0:
  10.6 98.1 all-gather.2
  308.4 234.8 all-reduce.5

commit v4 on v3

--- a/solution.py
+++ b/solution.py
@@ -236,64 +236,69 @@
 
 
 CUT = 48
-FCUT = 96
-MATE_SLOTS = 6
-OWN_SLOTS = 3
-SUM_SLOTS = 8
-FFN_SLOTS = 12
-
-
-def reduce_kernel(pieces, ffn_pieces, *refs):
-    count = len(pieces)
-    parts = refs[:count]
-    ffn_count = sum(ffn_pieces)
-    ffn = refs[count : count + len(ffn_pieces)]
-    refs = refs[len(ffn) :]
-    out_a = refs[count]
-    out_f = refs[count + 1] if ffn_count else None
-    refs = refs[count + (2 if ffn_count else 1) :]
-    (
-        mate_buf,
-        own_buf,
-        sums,
-        one_buf,
-        two_buf,
-        done,
-        ffn_buf,
-        low_a,
-        up_a,
-        low_f,
-        up_f,
-        mate_send,
-        mate_recv,
-        own_sem,
-        one_send,
-        one_recv,
-        two_send,
-        two_recv,
-        ffn_sem,
-        chain_send,
-        chain_recv,
-        out_sem,
-        credit,
-    ) = refs
-    me = lax.axis_index("grp")
-    plane = lax.axis_index("rep")
-    core = lax.rem(me, 2)
-    x = lax.rem(me // 2, 2)
-    y = me // 4
-    mate_dev = (me ^ 1, plane)
-    x_dev = (me ^ 2, plane)
-    y_dev = (me ^ 4, plane)
-    low_dev = (me, plane - 1)
-    up_dev = (me, plane + 1)
-    meet([mate_dev, x_dev, y_dev], low_dev, up_dev, plane)
-    total = sum(pieces)
-    chain_total = ffn_count + total
-
-    def each(i, body):
+FCUT = 64
+UNIT = 192
+MATE_SLOTS = 4
+OWN_SLOTS = 2
+SUM_SLOTS = 9
+FFN_SLOTS = 14
+LAND_SLOTS = 3
+
+
+class Sums:
+    def __init__(self, pieces, ffn_pieces, parts, ffn, outs, lands, bufs, sems):
+        self.pieces, self.ffn_pieces, self.parts, self.ffn = pieces, ffn_pieces, parts, ffn
+        self.out_a, self.out_f = outs
+        self.one_land, self.two_land, self.low_a, self.up_a, self.low_f, self.up_f = lands
+        (
+            self.mate_buf,
+            self.own_buf,
+            self.sums,
+            self.done,
+            self.ffn_buf,
+            self.one_buf,
+            self.two_buf,
+            self.low_buf,
+            self.up_buf,
+        ) = bufs
+        (
+            self.mate_send,
+            self.mate_recv,
+            self.own_sem,
+            self.one_send,
+            self.one_recv,
+            self.one_sem,
+            self.two_send,
+            self.two_recv,
+            self.two_sem,
+            self.ffn_sem,
+            self.chain_send,
+            self.chain_recv,
+            self.low_sem,
+            self.up_sem,
+            self.out_sem,
+            self.credit,
+        ) = sems
+        me = lax.axis_index("grp")
+        self.plane = plane = lax.axis_index("rep")
+        self.core = lax.rem(me, 2)
+        self.x = lax.rem(me // 2, 2)
+        self.y = me // 4
+        self.mate_dev = (me ^ 1, plane)
+        self.x_dev = (me ^ 2, plane)
+        self.y_dev = (me ^ 4, plane)
+        self.low_dev = (me, plane - 1)
+        self.up_dev = (me, plane + 1)
+        self.total = sum(pieces)
+        self.ffn_count = sum(ffn_pieces)
+        self.chain_total = self.ffn_count + self.total
+
+    def start(self):
+        meet([self.mate_dev, self.x_dev, self.y_dev], self.low_dev, self.up_dev, self.plane)
+
+    def each(self, i, body):
         base = 0
-        for k, n in enumerate(pieces):
+        for k, n in enumerate(self.pieces):
 
             @pl.when((i >= base) & (i < base + n))
             def _(k=k, base=base):
@@ -301,54 +306,56 @@
 
             base += n
 
-    def mate_copy(k, cut, slot):
+    def mate_copy(self, k, cut, slot):
         return pltpu.make_async_remote_copy(
-            src_ref=parts[k].at[:, :, 1 - core, cut],
-            dst_ref=mate_buf.at[slot],
-            send_sem=mate_send.at[slot],
-            recv_sem=mate_recv.at[slot],
-            device_id=mate_dev,
+            src_ref=self.parts[k].at[:, :, 1 - self.core, cut],
+            dst_ref=self.mate_buf.at[slot],
+            send_sem=self.mate_send.at[slot],
+            recv_sem=self.mate_recv.at[slot],
+            device_id=self.mate_dev,
             device_id_type=MESH,
         )
 
-    def own_copy(k, cut, slot):
+    def own_copy(self, k, cut, slot):
         return pltpu.make_async_copy(
-            parts[k].at[:, :, core, cut], own_buf.at[slot], own_sem.at[slot]
-        )
-
-    def load(i):
+            self.parts[k].at[:, :, self.core, cut], self.own_buf.at[slot], self.own_sem.at[slot]
+        )
+
+    def load(self, i):
         @pl.when(i >= MATE_SLOTS)
         def _():
-            pl.semaphore_wait(credit, 1)
-            mate_copy(0, pl.ds(0, CUT), lax.rem(i, MATE_SLOTS)).wait_send()
+            pl.semaphore_wait(self.credit, 1)
+            self.mate_copy(0, pl.ds(0, CUT), lax.rem(i, MATE_SLOTS)).wait_send()
 
         def body(k, cut):
-            mate_copy(k, cut, lax.rem(i, MATE_SLOTS)).start()
-            own_copy(k, cut, lax.rem(i, OWN_SLOTS)).start()
-
-        each(i, body)
-
-    def one_copy(i, slot, by_x):
+            self.mate_copy(k, cut, lax.rem(i, MATE_SLOTS)).start()
+            self.own_copy(k, cut, lax.rem(i, OWN_SLOTS)).start()
+
+        self.each(i, body)
+
+    def one_copy(self, i, slot, by_x):
         return pltpu.make_async_remote_copy(
-            src_ref=sums.at[slot, :, 1 - x] if by_x else sums.at[slot, 1 - y],
-            dst_ref=one_buf.at[i],
-            send_sem=one_send.at[slot],
-            recv_sem=one_recv.at[i],
-            device_id=x_dev if by_x else y_dev,
+            src_ref=self.sums.at[slot, :, 1 - self.x] if by_x else self.sums.at[slot, 1 - self.y],
+            dst_ref=self.one_land.at[i],
+            send_sem=self.one_send.at[slot],
+            recv_sem=self.one_recv.at[i],
+            device_id=self.x_dev if by_x else self.y_dev,
             device_id_type=MESH,
         )
 
-    def two_copy(i, slot, by_x):
+    def two_copy(self, i, slot, by_x):
         return pltpu.make_async_remote_copy(
-            src_ref=sums.at[slot, 1 - y, x] if by_x else sums.at[slot, y, 1 - x],
-            dst_ref=two_buf.at[i],
-            send_sem=two_send.at[slot],
-            recv_sem=two_recv.at[i],
-            device_id=y_dev if by_x else x_dev,
+            src_ref=self.sums.at[slot, 1 - self.y, self.x]
+            if by_x
+            else self.sums.at[slot, self.y, 1 - self.x],
+            dst_ref=self.two_land.at[i],
+            send_sem=self.two_send.at[slot],
+            recv_sem=self.two_recv.at[i],
+            device_id=self.y_dev if by_x else self.x_dev,
             device_id_type=MESH,
         )
 
-    def either(i, body):
+    def either(self, i, body):
         @pl.when(lax.rem(i, 2) == 0)
         def _():
             body(True)
@@ -357,259 +364,328 @@
         def _():
             body(False)
 
-    def add(a, b):
-        return (a.astype(jnp.float32) + b.astype(jnp.float32)).astype(jnp.bfloat16)
-
-    def pair(i):
-        mate_slot, own_slot, slot = (
-            lax.rem(i, MATE_SLOTS),
-            lax.rem(i, OWN_SLOTS),
-            lax.rem(i, SUM_SLOTS),
-        )
-        mate_copy(0, pl.ds(0, CUT), mate_slot).wait_recv()
-        own_copy(0, pl.ds(0, CUT), own_slot).wait()
+    def one_load(self, i):
+        slot = lax.rem(i, LAND_SLOTS)
+        return pltpu.make_async_copy(self.one_land.at[i], self.one_buf.at[slot], self.one_sem.at[slot])
+
+    def two_load(self, i):
+        slot = lax.rem(i, LAND_SLOTS)
+        return pltpu.make_async_copy(self.two_land.at[i], self.two_buf.at[slot], self.two_sem.at[slot])
+
+    def pair(self, i):
+        mate_slot, own_slot = lax.rem(i, MATE_SLOTS), lax.rem(i, OWN_SLOTS)
+        slot = lax.rem(i, SUM_SLOTS)
+        self.mate_copy(0, pl.ds(0, CUT), mate_slot).wait_recv()
+        self.own_copy(0, pl.ds(0, CUT), own_slot).wait()
         for u in range(2):
             for v in range(2):
-                sums[slot, u, v] = add(own_buf[own_slot, u, v], mate_buf[mate_slot, u, v])
-
-        @pl.when(i + MATE_SLOTS < total)
+                self.sums[slot, u, v] = add(
+                    self.own_buf[own_slot, u, v], self.mate_buf[mate_slot, u, v]
+                )
+
+        @pl.when(i + MATE_SLOTS < self.total)
         def _():
-            pl.semaphore_signal(credit, inc=1, device_id=mate_dev, device_id_type=MESH)
-
-        either(i, lambda by_x: one_copy(i, slot, by_x).start())
-
-    def plane_one(i):
+            pl.semaphore_signal(
+                self.credit, inc=1, device_id=self.mate_dev, device_id_type=MESH
+            )
+
+        self.either(i, lambda by_x: self.one_copy(i, slot, by_x).start())
+
+    def one_arrives(self, i):
+        self.either(i, lambda by_x: self.one_copy(i, lax.rem(i, SUM_SLOTS), by_x).wait_recv())
+        self.one_load(i).start()
+
+    def plane_one(self, i):
+        slot, land = lax.rem(i, SUM_SLOTS), lax.rem(i, LAND_SLOTS)
+        self.one_load(i).wait()
+
+        def body(by_x):
+            for u in range(2):
+                at = (slot, u, self.x) if by_x else (slot, self.y, u)
+                self.sums[at] = add(self.sums[at], self.one_buf[land, u])
+            self.two_copy(i, slot, by_x).start()
+
+        self.either(i, body)
+
+    def two_arrives(self, i):
+        self.either(i, lambda by_x: self.two_copy(i, lax.rem(i, SUM_SLOTS), by_x).wait_recv())
+        self.two_load(i).start()
+
+    def plane_two(self, i):
         slot = lax.rem(i, SUM_SLOTS)
+        self.two_load(i).wait()
+        self.done[i] = add(self.sums[slot, self.y, self.x], self.two_buf[lax.rem(i, LAND_SLOTS)])
 
         def body(by_x):
-            one_copy(i, slot, by_x).wait_recv()
-            for u in range(2):
-                if by_x:
-                    sums[slot, u, x] = add(sums[slot, u, x], one_buf[i, u])
-                else:
-                    sums[slot, y, u] = add(sums[slot, y, u], one_buf[i, u])
-            two_copy(i, slot, by_x).start()
-
-        either(i, body)
-
-    def plane_two(i):
-        slot = lax.rem(i, SUM_SLOTS)
-
-        def body(by_x):
-            two_copy(i, slot, by_x).wait_recv()
-            done[i] = add(sums[slot, y, x], two_buf[i])
-            one_copy(i, slot, by_x).wait_send()
-            two_copy(i, slot, by_x).wait_send()
-
-        either(i, body)
-
-    def ffn_load(j):
+            self.one_copy(i, slot, by_x).wait_send()
+            self.two_copy(i, slot, by_x).wait_send()
+
+        self.either(i, body)
+
+    def ffn_load(self, j):
         base = 0
-        for k, n in enumerate(ffn_pieces):
+        for k, n in enumerate(self.ffn_pieces):
 
             @pl.when((j >= base) & (j < base + n))
             def _(k=k, base=base):
                 row = pl.multiple_of((j - base) * FCUT, 16)
                 pltpu.make_async_copy(
-                    ffn[k].at[pl.ds(row, FCUT)],
-                    ffn_buf.at[lax.rem(j, FFN_SLOTS)],
-                    ffn_sem.at[lax.rem(j, FFN_SLOTS)],
+                    self.ffn[k].at[pl.ds(row, FCUT)],
+                    self.ffn_buf.at[lax.rem(j, FFN_SLOTS)],
+                    self.ffn_sem.at[lax.rem(j, FFN_SLOTS)],
                 ).start()
 
             base += n
 
-    def ffn_wait(j):
+    def ffn_wait(self, j):
         pltpu.make_async_copy(
-            ffn[0].at[pl.ds(0, FCUT)],
-            ffn_buf.at[lax.rem(j, FFN_SLOTS)],
-            ffn_sem.at[lax.rem(j, FFN_SLOTS)],
+            self.ffn[0].at[pl.ds(0, FCUT)],
+            self.ffn_buf.at[lax.rem(j, FFN_SLOTS)],
+            self.ffn_sem.at[lax.rem(j, FFN_SLOTS)],
         ).wait()
 
-    def views(j, is_ffn):
-        if is_ffn:
+    def role(self, j, plane, body):
+        slot = lax.rem(j, LAND_SLOTS)
+        key = self.plane + jnp.where(j < self.ffn_count, 0, 4)
+        key = jnp.where((j >= 0) & (j < self.chain_total), key, 8)
+
+        @pl.when(key == plane)
+        def _():
             rows = pl.ds(pl.multiple_of(j * FCUT, 16), FCUT)
-            return ffn_buf.at[lax.rem(j, FFN_SLOTS)], low_f.at[j], up_f.at[j], out_f.at[rows]
-        i = j - ffn_count
-        rows = pl.ds(pl.multiple_of(i * CUT, 16), CUT)
-        return done.at[i], low_a.at[i], up_a.at[i], out_a.at[rows]
-
-    def chain(j, lane, src, dst, device):
+            body(
+                self.ffn_buf.at[lax.rem(j, FFN_SLOTS)],
+                self.low_f.at[j],
+                self.up_f.at[j],
+                self.low_buf.at[slot],
+                self.up_buf.at[slot],
+                self.out_f.at[rows],
+            )
+
+        @pl.when(key == plane + 4)
+        def _():
+            i = j - self.ffn_count
+            rows = pl.ds(pl.multiple_of(i * CUT, 16), CUT)
+            part = pl.ds(0, CUT)
+            body(
+                self.done.at[i],
+                self.low_a.at[i],
+                self.up_a.at[i],
+                self.low_buf.at[slot, part],
+                self.up_buf.at[slot, part],
+                self.out_a.at[rows],
+            )
+
+    def chain(self, j, lane, src, dst, device):
         return pltpu.make_async_remote_copy(
             src_ref=src,
             dst_ref=dst,
-            send_sem=chain_send.at[lane, j],
-            recv_sem=chain_recv.at[lane, j],
+            send_sem=self.chain_send.at[lane, j],
+            recv_sem=self.chain_recv.at[lane, j],
             device_id=device,
             device_id_type=MESH,
         )
 
-    def kinds(j, body):
-        if ffn_count:
-
-            @pl.when(j < ffn_count)
-            def _():
-                body(*views(j, True))
-
-        @pl.when(j >= ffn_count)
+    def low_load(self, j, land, buf):
+        return pltpu.make_async_copy(land, buf, self.low_sem.at[lax.rem(j, LAND_SLOTS)])
+
+    def up_load(self, j, land, buf):
+        return pltpu.make_async_copy(land, buf, self.up_sem.at[lax.rem(j, LAND_SLOTS)])
+
+    def inward(self, j):
+        @pl.when((j >= 0) & (j < self.ffn_count))
         def _():
-            body(*views(j, False))
-
-    def inward(j):
-        if ffn_count:
-
-            @pl.when(j < ffn_count)
-            def _():
-                ffn_wait(j)
-
-        def body(mine, low, up, out):
-            @pl.when(plane == 0)
-            def _():
-                chain(j, 0, mine, low, up_dev).start()
-
-            @pl.when(plane == 3)
-            def _():
-                chain(j, 1, mine, up, low_dev).start()
-
-        kinds(j, body)
-
-    def middle(j):
-        def body(mine, low, up, out):
-            @pl.when(plane == 2)
-            def _():
-                chain(j, 1, mine, up, low_dev).wait_recv()
-                mine[...] = add(mine[...], up[...])
-                chain(j, 1, mine, up, low_dev).start()
-
-        kinds(j, body)
-
-    def root(j):
-        def body(mine, low, up, out):
-            @pl.when(plane == 1)
-            def _():
-                chain(j, 0, mine, low, up_dev).wait_recv()
-                chain(j, 1, mine, up, low_dev).wait_recv()
-                mine[...] = (
-                    mine[...].astype(jnp.float32)
-                    + low[...].astype(jnp.float32)
-                    + up[...].astype(jnp.float32)
-                ).astype(jnp.bfloat16)
-                chain(j, 0, mine, out, up_dev).start()
-                chain(j, 1, mine, out, low_dev).start()
-                pltpu.make_async_copy(mine, out, out_sem.at[j]).start()
-
-        kinds(j, body)
-
-    def outward(j):
-        def body(mine, low, up, out):
-            @pl.when(plane == 2)
-            def _():
-                chain(j, 0, mine, out, up_dev).wait_recv()
-                chain(j, 0, out, out, up_dev).start()
-
-        kinds(j, body)
-
-    def drain(j):
-        def body(mine, low, up, out):
-            @pl.when(plane == 0)
-            def _():
-                chain(j, 0, mine, low, up_dev).wait_send()
-                chain(j, 1, mine, out, low_dev).wait_recv()
-
-            @pl.when(plane == 3)
-            def _():
-                chain(j, 1, mine, up, low_dev).wait_send()
-                chain(j, 0, mine, out, up_dev).wait_recv()
-
-            @pl.when(plane == 1)
-            def _():
-                chain(j, 0, mine, out, up_dev).wait_send()
-                chain(j, 1, mine, out, low_dev).wait_send()
-                pltpu.make_async_copy(mine, out, out_sem.at[j]).wait()
-
-            @pl.when(plane == 2)
-            def _():
-                chain(j, 1, mine, up, low_dev).wait_send()
-                chain(j, 0, out, out, up_dev).wait_send()
-
-        kinds(j, body)
-
-    lag = max(1, 5 - ffn_count)
-    stages = (
-        (load, 0, total),
-        (ffn_load, lag - 1, ffn_count),
-        (pair, 1, total),
-        (plane_one, 3, total),
-        (plane_two, 5, total),
-        (inward, lag, chain_total),
-        (middle, lag + 2, chain_total),
-        (root, lag + 4, chain_total),
-        (outward, lag + 6, chain_total),
-        (drain, lag + 8, chain_total),
-    )
-
-    def step(t, carry):
-        for stage, behind, limit in stages:
-            i = t - behind
+            self.ffn_wait(j)
+
+        def lowest(mine, low, up, low_buf, up_buf, out):
+            self.chain(j, 0, mine, low, self.up_dev).start()
+
+        def highest(mine, low, up, low_buf, up_buf, out):
+            self.chain(j, 1, mine, up, self.low_dev).start()
+
+        self.role(j, 0, lowest)
+        self.role(j, 3, highest)
+
+    def middle_arrives(self, j):
+        def body(mine, low, up, low_buf, up_buf, out):
+            self.chain(j, 1, mine, up, self.low_dev).wait_recv()
+            self.up_load(j, up, up_buf).start()
+
+        self.role(j, 2, body)
+
+    def middle(self, j):
+        def body(mine, low, up, low_buf, up_buf, out):
+            self.up_load(j, up, up_buf).wait()
+            mine[...] = add(mine[...], up_buf[...])
+            self.chain(j, 1, mine, up, self.low_dev).start()
+
+        self.role(j, 2, body)
+
+    def root_arrives(self, j):
+        def body(mine, low, up, low_buf, up_buf, out):
+            self.chain(j, 0, mine, low, self.up_dev).wait_recv()
+            self.low_load(j, low, low_buf).start()
+            self.chain(j, 1, mine, up, self.low_dev).wait_recv()
+            self.up_load(j, up, up_buf).start()
+
+        self.role(j, 1, body)
+
+    def root(self, j):
+        def body(mine, low, up, low_buf, up_buf, out):
+            self.low_load(j, low, low_buf).wait()
+            self.up_load(j, up, up_buf).wait()
+            mine[...] = add(mine[...], low_buf[...], up_buf[...])
+            self.chain(j, 0, mine, out, self.up_dev).start()
+            self.chain(j, 1, mine, out, self.low_dev).start()
+            pltpu.make_async_copy(mine, out, self.out_sem.at[j]).start()
+
+        self.role(j, 1, body)
+
+    def outward(self, j):
+        def body(mine, low, up, low_buf, up_buf, out):
+            self.chain(j, 0, mine, out, self.up_dev).wait_recv()
+            self.chain(j, 0, out, out, self.up_dev).start()
+
+        self.role(j, 2, body)
+
+    def drain(self, j):
+        def lowest(mine, low, up, low_buf, up_buf, out):
+            self.chain(j, 0, mine, low, self.up_dev).wait_send()
+            self.chain(j, 1, mine, out, self.low_dev).wait_recv()
+
+        def holder(mine, low, up, low_buf, up_buf, out):
+            self.chain(j, 0, mine, out, self.up_dev).wait_send()
+            self.chain(j, 1, mine, out, self.low_dev).wait_send()
+            pltpu.make_async_copy(mine, out, self.out_sem.at[j]).wait()
+
+        def between(mine, low, up, low_buf, up_buf, out):
+            self.chain(j, 1, mine, up, self.low_dev).wait_send()
+            self.chain(j, 0, out, out, self.up_dev).wait_send()
+
+        def highest(mine, low, up, low_buf, up_buf, out):
+            self.chain(j, 1, mine, up, self.low_dev).wait_send()
+            self.chain(j, 0, mine, out, self.up_dev).wait_recv()
+
+        for plane, body in enumerate((lowest, holder, between, highest)):
+            self.role(j, plane, body)
+
+    def stages(self, at, limit, pairs):
+        for stage, behind in pairs:
+            i = at - behind
 
             @pl.when((i >= 0) & (i < limit))
             def _(stage=stage, i=i):
                 stage(i)
 
-        return carry
-
-    lax.fori_loop(0, chain_total + lag + 8, step, 0)
-    for i in range(max(total - MATE_SLOTS, 0), total):
-        mate_copy(0, pl.ds(0, CUT), i % MATE_SLOTS).wait_send()
-
-
-def reduce_all(parts, ffn):
-    pieces = tuple(p.shape[3] // CUT for p in parts)
-    total = sum(pieces)
-    wide = parts[0].shape[-1]
-    ffn_rows = sum(f.shape[0] for f in ffn)
-    ffn_pieces = tuple(f.shape[0] // FCUT for f in ffn)
-    ffn_count = sum(ffn_pieces)
-    chain_total = total + ffn_count
-    hbm = pl.BlockSpec(memory_space=pltpu.HBM)
-    low = jnp.bfloat16
-    dma = pltpu.SemaphoreType.DMA
-    return pl.pallas_call(
-        functools.partial(reduce_kernel, pieces, ffn_pieces),
-        out_shape=[
-            jax.ShapeDtypeStruct((total * CUT, wide), low),
-            jax.ShapeDtypeStruct((ffn_rows, wide), low),
-        ][: 2 if ffn else 1],
-        in_specs=[hbm] * (len(parts) + len(ffn)),
-        out_specs=[hbm] * (2 if ffn else 1),
-        scratch_shapes=[
-            pltpu.VMEM((MATE_SLOTS, 2, 2, CUT, wide), low),
-            pltpu.VMEM((OWN_SLOTS, 2, 2, CUT, wide), low),
-            pltpu.VMEM((SUM_SLOTS, 2, 2, CUT, wide), low),
-            pltpu.VMEM((total, 2, CUT, wide), low),
-            pltpu.VMEM((total, CUT, wide), low),
-            pltpu.VMEM((total, CUT, wide), low),
-            pltpu.VMEM((FFN_SLOTS if ffn else 1, FCUT, wide), low),
-            pltpu.VMEM((total, CUT, wide), low),
-            pltpu.VMEM((total, CUT, wide), low),
-            pltpu.VMEM((max(ffn_count, 1), FCUT, wide), low),
-            pltpu.VMEM((max(ffn_count, 1), FCUT, wide), low),
+    def xy_step(self, i):
+        self.stages(
+            i,
+            self.total,
+            (
+                (self.load, 0),
+                (self.pair, 1),
+                (self.plane_two, 7),
+                (self.plane_one, 4),
+                (self.two_arrives, 6),
+                (self.one_arrives, 3),
+            ),
+        )
+
+    def z_step(self, j):
+        self.stages(j + 1, self.ffn_count, ((self.ffn_load, 0),))
+        for stage, behind in (
+            (self.inward, 0),
+            (self.root, 6),
+            (self.middle, 3),
+            (self.outward, 8),
+            (self.root_arrives, 5),
+            (self.middle_arrives, 2),
+            (self.drain, 11),
+        ):
+            stage(j - behind)
+
+    def begin(self):
+        self.ffn_load(jnp.int32(0))
+
+    def finish(self, z_next, xy_next):
+        steps = self.chain_total + 12 - z_next
+
+        def body(u, carry):
+            self.z_step(z_next + u)
+            self.xy_step(xy_next + u)
+            return carry
+
+        lax.fori_loop(0, steps, body, 0)
+        for i in range(max(self.total - MATE_SLOTS, 0), self.total):
+            self.mate_copy(0, pl.ds(0, CUT), i % MATE_SLOTS).wait_send()
+
+    @staticmethod
+    def shapes(pieces, ffn_pieces, wide):
+        total, ffn_count = sum(pieces), sum(ffn_pieces)
+        chain_total = total + ffn_count
+        low = jnp.bfloat16
+        dma = pltpu.SemaphoreType.DMA
+        shape = lambda *s: jax.ShapeDtypeStruct(s, low)
+        buf = lambda *s: pltpu.VMEM(s, low)
+        outs = [shape(total * CUT, wide), shape(ffn_count * FCUT, wide)]
+        lands = [
+            shape(total, 2, CUT, wide),
+            *[shape(total, CUT, wide)] * 3,
+            *[shape(ffn_count, FCUT, wide)] * 2,
+        ]
+        bufs = [
+            buf(MATE_SLOTS, 2, 2, CUT, wide),
+            buf(OWN_SLOTS, 2, 2, CUT, wide),
+            buf(SUM_SLOTS, 2, 2, CUT, wide),
+            buf(total, CUT, wide),
+            buf(FFN_SLOTS, FCUT, wide),
+            buf(LAND_SLOTS, 2, CUT, wide),
+            buf(LAND_SLOTS, CUT, wide),
+            buf(LAND_SLOTS, FCUT, wide),
+            buf(LAND_SLOTS, FCUT, wide),
+        ]
+        sems = [
             dma((MATE_SLOTS,)),
             dma((MATE_SLOTS,)),
             dma((OWN_SLOTS,)),
             dma((SUM_SLOTS,)),
             dma((total,)),
+            dma((LAND_SLOTS,)),
             dma((SUM_SLOTS,)),
             dma((total,)),
+            dma((LAND_SLOTS,)),
             dma((FFN_SLOTS,)),
             dma((2, chain_total)),
             dma((2, chain_total)),
+            dma((LAND_SLOTS,)),
+            dma((LAND_SLOTS,)),
             dma((chain_total,)),
             pltpu.SemaphoreType.REGULAR,
-        ],
-        compiler_params=pltpu.CompilerParams(
-            collective_id=1, has_side_effects=True, vmem_limit_bytes=VMEM_LIMIT
-        ),
-    )(*parts, *ffn)
+        ]
+        return outs, lands, bufs, sems
+
+
+class NoSums:
+    def start(self):
+        pass
+
+    def begin(self):
+        pass
+
+    def z_step(self, j):
+        pass
+
+    def xy_step(self, i):
+        pass
+
+    def finish(self, z_next, xy_next):
+        pass
+
+
+def add(*terms):
+    total = terms[0].astype(jnp.float32)
+    for term in terms[1:]:
+        total = total + term.astype(jnp.float32)
+    return total.astype(jnp.bfloat16)
 
 
 STEP_CHIP = (0, 0, 1, 2, 1, 2, 3, 3)
@@ -730,12 +806,6 @@
             (pair.at[kind, 7], passed.at[kind, 1], y_dev),
         )[lane]
         return remote(src, dst, flow_send.at[kind, lane], flow_recv.at[kind, lane], device)
-
-    def add(*terms):
-        total = terms[0].astype(jnp.float32)
-        for term in terms[1:]:
-            total = total + term.astype(jnp.float32)
-        return total.astype(low)
 
     def forward_tiles(t):
         def tile(n, carry):
@@ -1318,87 +1388,62 @@
     return results[0], results[1:5], results[5:]
 
 
-def attention_backward_kernel(
-    x_in,
-    cond_in,
-    norms,
-    cosine,
-    sine_left,
-    sine_right,
-    qkv_in,
-    out_in,
-    query2_in,
-    out2_in,
-    act_one_in,
-    heads_in,
-    prob_in,
-    flat_one_in,
-    section_one_in,
-    act_two_in,
-    query_two_in,
-    kv_two_in,
-    prob_two_in,
-    flat_two_in,
-    section_two_in,
-    d_norm_in,
-    d_out_in,
-    d_inputs_out,
-    sums,
-    grad_qkv,
-    grad_out,
-    grad_query2,
-    grad_out2,
-    grad_kv2,
-    w_qkv,
-    w_out,
-    w_query2,
-    w_out2,
-    x,
-    cond,
-    act_one,
-    heads,
-    flat_one,
-    section_one,
-    act_two,
-    query_two,
-    kv_two,
-    flat_two,
-    section_two,
-    d_norm,
-    d_low,
-    d_heads,
-    d_kv,
-    d_att,
-    prob,
-    prob_two,
-    grad_buf,
-    in_sem,
-    prob_sem,
-    grad_sem,
-    end_sem,
-):
+GRAD_TILE = 2 * UNIT
+
+
+def attention_backward_kernel(plan, *refs):
+    refs = list(refs)
+
+    def take(n):
+        taken = refs[:n]
+        del refs[:n]
+        return taken
+
+    x_in, cond_in, norms, cosine, sine_left, sine_right = take(6)
+    qkv_in, out_in, query2_in, out2_in = take(4)
+    act_one_in, heads_in, prob_in, flat_one_in, section_one_in, act_two_in = take(6)
+    query_two_in, kv_two_in, prob_two_in, flat_two_in, section_two_in = take(5)
+    d_norm_in, d_out_in = take(2)
+    ffn_in = take(3) if plan else []
+    d_inputs_out, sums = take(2)
+    grad_out2, grad_query2, grad_kv2, grad_out, grad_qkv = take(5)
+    if plan:
+        (grad_norm,) = take(1)
+        sum_outs, lands = take(2), take(6)
+    w_small, w_tile = take(2)
+    x, cond, act_one, heads, flat_one, section_one, act_two = take(7)
+    query_two, kv_two, flat_two, section_two, d_norm = take(5)
+    d_low, d_heads, d_kv, d_att, prob, prob_two, grad_buf = take(7)
+    in_sem, weight_sem, tile_sem, prob_sem, grad_sem, end_sem = take(6)
+    if plan:
+        norm_buf, norm_sem = take(2)
+        bufs, sems = take(9), take(16)
+        parts = (grad_out2, grad_query2, grad_kv2, grad_out, grad_qkv, grad_norm)
+        work = Sums(plan[0], plan[1], parts, ffn_in, sum_outs, lands, bufs, sems)
+    else:
+        work = NoSums()
     rows, wide = x.shape
+    pairs = wide // PAIR
     low = jnp.bfloat16
+    work.start()
+    work.begin()
     loads = {}
     for k, (name, src, dst) in enumerate(
         (
             ("section_two", section_two_in, section_two),
             ("d_norm", d_norm_in, d_norm),
             ("d_out", d_out_in, d_low),
-            ("w_out2", out2_in, w_out2),
+            ("w_out2", out2_in, w_small),
             ("flat_two", flat_two_in, flat_two),
             ("query_two", query_two_in, query_two),
             ("kv_two", kv_two_in, kv_two),
             ("cond", cond_in, cond),
             ("act_two", act_two_in, act_two),
-            ("w_query2", query2_in, w_query2),
             ("section_one", section_one_in, section_one),
-            ("w_out", out_in, w_out),
             ("flat_one", flat_one_in, flat_one),
             ("heads", heads_in, heads),
             ("act_one", act_one_in, act_one),
             ("x", x_in, x),
-            ("w_qkv", qkv_in, w_qkv),
         )
     ):
         loads[name] = pltpu.make_async_copy(src, dst, in_sem.at[k])
@@ -1408,6 +1453,10 @@
         for name in names:
             loads[name].wait()
 
+    def next_weight(name, src, k):
+        loads[name] = pltpu.make_async_copy(src, w_small, weight_sem.at[k])
+        loads[name].start()
+
     gains = [norms.at[pl.ds(2 * k, 1)] for k in range(3)]
 
     def prob_copy(src, buf, p, slot):
@@ -1417,37 +1466,45 @@
         for p in range(2):
             prob_copy(src, buf, p, p).start()
 
-    pairs = wide // PAIR
-    used = [0]
-
-    def grad_copy(target, cut, slot):
-        return pltpu.make_async_copy(grad_buf.at[slot], target.at[cut], grad_sem.at[slot])
-
-    def weight_rows(left, right, target, count):
-        before = used[0]
-
+    def unit_copy(target, n, half, slot):
+        src = grad_buf.at[slot, pl.ds(half * UNIT, UNIT)]
+        unit = 2 * n + half
+        if plan:
+            per = target.shape[3] // UNIT
+            block = unit // per
+            row = pl.multiple_of(lax.rem(unit, per) * UNIT, 16)
+            place = target.at[block // 4, lax.rem(block // 2, 2), lax.rem(block, 2), pl.ds(row, UNIT)]
+        else:
+            place = target.at[pl.ds(pl.multiple_of(unit * UNIT, 16), UNIT)]
+        return pltpu.make_async_copy(src, place, grad_sem.at[slot, half])
+
+    def grad_rows(target, count, compute):
         def step(n, carry):
-            cut = pl.ds(pl.multiple_of(n * TILE, TILE), TILE)
-            slot = lax.rem(n + before, 2)
-
-            @pl.when(n + before >= 2)
+            slot = lax.rem(n, 2)
+
+            @pl.when(n >= 2)
             def _():
-                grad_copy(target, cut, slot).wait()
-
-            columns = left[:, cut]
+                for half in range(2):
+                    unit_copy(target, n, half, slot).wait()
+
+            compute(n, slot)
+            for half in range(2):
+                unit_copy(target, n, half, slot).start()
+            return carry
+
+        lax.fori_loop(0, count, step, 0)
+        for slot in range(2):
+            for half in range(2):
+                unit_copy(target, 0, half, slot).wait()
+
+    def weight_rows(left, right, target):
+        def compute(n, slot):
+            columns = left[:, pl.ds(pl.multiple_of(n * GRAD_TILE, 128), GRAD_TILE)]
             for m in range(wide // 512):
                 piece = slice(m * 512, (m + 1) * 512)
                 grad_buf[slot, :, piece] = dot_tn(columns, right[:, piece]).astype(low)
-            grad_copy(target, cut, slot).start()
-            return carry
-
-        lax.fori_loop(0, count // TILE, step, 0)
-        used[0] = before + count // TILE
-
-    prob_start(prob_two_in, prob_two)
-    need("section_two", "d_norm", "d_out")
-    normalise_back(section_two, gains[2], d_norm, d_low, section_two, sums, 4, rows)
-    d_section = section_two
+
+        grad_rows(target, left.shape[1] // GRAD_TILE, compute)
 
     def round_rows():
         def block(n, carry):
@@ -1457,18 +1514,37 @@
 
         lax.fori_loop(0, rows // NORM_ROWS, block, 0)
 
+    def through(target):
+        def body(cut):
+            target[:, cut] = dot(d_low[...], w_small[:, cut]).astype(low)
+
+        tiles_of(wide, body)
+
+    at = {"z": 0, "xy": 0}
+
+    def serve(*kinds):
+        for kind in kinds:
+            (work.z_step if kind == "z" else work.xy_step)(jnp.int32(at[kind]))
+            at[kind] += 1
+
+    def serve_pairs(p, kind, every):
+        @pl.when(lax.rem(p, every) == every - 1)
+        def _():
+            (work.z_step if kind == "z" else work.xy_step)(at[kind] + p // every)
+
+    prob_start(prob_two_in, prob_two)
+    serve("z")
+    need("section_two", "d_norm", "d_out")
+    normalise_back(section_two, gains[2], d_norm, d_low, section_two, sums, 4, rows)
+    d_section = section_two
     round_rows()
     need("w_out2")
-
-    def through(weight):
-        def body(cut):
-            d_att[:, cut] = dot(d_low[...], weight[:, cut]).astype(low)
-
-        tiles_of(wide, body)
-
-    through(w_out2)
+    through(d_att)
+    next_weight("w_query2", query2_in, 0)
+    serve("z")
     need("flat_two")
-    weight_rows(d_low, flat_two, grad_out2, wide)
+    weight_rows(d_low, flat_two, grad_out2)
+    serve("xy", "z")
     need("query_two", "kv_two")
 
     def cross_pair(p, lane):
@@ -1490,54 +1566,49 @@
         def _():
             prob_copy(prob_two_in, prob_two, p + 2, slot).start()
 
+        serve_pairs(p, "z", 3)
+        serve_pairs(p, "xy", 4)
+
     pair_loop(cross_pair)
+    at["z"] += 4
+    at["xy"] += 3
     prob_start(prob_in, prob)
     need("w_query2")
-
-    def second_norm(cut):
-        d_norm[:, cut] = dot(d_low[...], w_query2[:, cut]).astype(low)
-
-    tiles_of(wide, second_norm)
+    through(d_norm)
+    next_weight("w_out", out_in, 1)
+    serve("z")
     need("act_two")
-    weight_rows(d_low, act_two, grad_query2, wide)
+    weight_rows(d_low, act_two, grad_query2)
+    serve("z", "xy")
     need("cond")
-    blocks = 2 * wide // 384
-    before = used[0]
-
-    def cond_rows(n, carry):
-        slot = lax.rem(n + before, 2)
-        part = grad_buf.at[slot, pl.ds(0, 192)]
-        copy = pltpu.make_async_copy(
-            part, grad_kv2.at[pl.ds(pl.multiple_of(n * 192, 16), 192)], grad_sem.at[slot]
-        )
-
-        @pl.when(n < 2)
-        def _():
-            grad_copy(grad_qkv, pl.ds(0, TILE), slot).wait()
-
-        @pl.when(n >= 2)
-        def _():
-            copy.wait()
-
-        result = dot_tn(d_kv[:, pl.ds(pl.multiple_of(n * 384, 128), 384)], cond[...]).astype(low)
-        grad_buf[slot, :192, : wide // 2] = result[:192]
-        grad_buf[slot, :192, wide // 2 :] = result[192:]
-        copy.start()
-        return carry
-
-    lax.fori_loop(0, blocks, cond_rows, 0)
-    for slot in range(2):
-        pltpu.make_async_copy(
-            grad_buf.at[slot, pl.ds(0, 192)], grad_kv2.at[pl.ds(0, 192)], grad_sem.at[slot]
-        ).wait()
-    used[0] = 0
+
+    def cond_rows(n, slot):
+        for half in range(2):
+            columns = pl.ds(pl.multiple_of((2 * n + half) * GRAD_TILE, 128), GRAD_TILE)
+            result = dot_tn(d_kv[:, columns], cond[...]).astype(low)
+            at = slice(half * UNIT, (half + 1) * UNIT)
+            grad_buf[slot, at, : wide // 2] = result[:UNIT]
+            grad_buf[slot, at, wide // 2 :] = result[UNIT:]
+
+    grad_rows(grad_kv2, wide // GRAD_TILE, cond_rows)
+    serve("xy", "z")
     need("section_one")
     normalise_back(section_one, gains[1], d_norm, d_section, d_section, sums, 2, rows)
+    serve("z", "xy")
     round_rows()
     need("w_out")
-    through(w_out)
+    through(d_att)
+
+    def tile_copy(n, slot):
+        cut = pl.ds(pl.multiple_of(n * TILE, TILE), TILE)
+        return pltpu.make_async_copy(qkv_in.at[:, cut], w_tile.at[slot], tile_sem.at[slot])
+
+    for n in range(2):
+        tile_copy(n, n).start()
+    serve("xy", "z")
     need("flat_one")
-    weight_rows(d_low, flat_one, grad_out, wide)
+    weight_rows(d_low, flat_one, grad_out)
+    serve("z", "xy")
     need("heads")
 
     def self_pair(p, lane):
@@ -1560,25 +1631,49 @@
         def _():
             prob_copy(prob_in, prob, p + 2, slot).start()
 
+        serve_pairs(p, "z", 1)
+        serve_pairs(p, "xy", 2)
+
     pair_loop(self_pair)
+    at["z"] += pairs
+    at["xy"] += 6
     need("act_one")
-    weight_rows(d_heads, act_one, grad_qkv, 3 * wide)
-    need("w_qkv")
-
-    def first_norm(cut):
-        d_norm[:, cut] = dot(d_heads[...], w_qkv[:, cut]).astype(low)
-
-    tiles_of(wide, first_norm)
+    weight_rows(d_heads, act_one, grad_qkv)
+    serve("z", "xy")
+
+    def first_norm(n, carry):
+        slot = lax.rem(n, 2)
+        cut = pl.ds(pl.multiple_of(n * TILE, TILE), TILE)
+        tile_copy(n, slot).wait()
+        d_norm[:, cut] = dot(d_heads[...], w_tile[slot]).astype(low)
+
+        @pl.when(n + 2 < wide // TILE)
+        def _():
+            tile_copy(n + 2, slot).start()
+
+        return carry
+
+    lax.fori_loop(0, wide // TILE, first_norm, 0)
+    serve("z", "xy")
     need("x")
     normalise_back(x, gains[0], d_norm, d_section, d_section, sums, 0, rows)
     end = pltpu.make_async_copy(d_section, d_inputs_out, end_sem)
     end.start()
-    for slot in range(2):
-        grad_copy(grad_qkv, pl.ds(0, TILE), slot).wait()
+    if plan:
+        norm_buf[...] = jnp.zeros_like(norm_buf)
+        norm_buf[:8] = sums[...].astype(low)
+        copies = []
+        for b in range(8):
+            place = grad_norm.at[b // 4, b // 2 % 2, b % 2]
+            copies.append(pltpu.make_async_copy(norm_buf, place, norm_sem.at[b]))
+            copies[-1].start()
+        for copy in copies:
+            copy.wait()
+    work.finish(at["z"], at["xy"])
     end.wait()
 
 
-def attention_backward(x, cond, norms, tables, weights, kept, d_norm, d_out):
+def attention_backward(x, cond, norms, tables, weights, kept, d_norm, d_out, ffn):
     rows, wide = x.shape
     low, full = jnp.bfloat16, jnp.float32
     hbm = pl.BlockSpec(memory_space=pltpu.HBM)
@@ -1586,21 +1681,33 @@
     dma = pltpu.SemaphoreType.DMA
     shape = jax.ShapeDtypeStruct
     buf = lambda s, t=low: pltpu.VMEM(s, t)
-    return pl.pallas_call(
-        attention_backward_kernel,
-        out_shape=[
-            shape((rows, wide), full),
-            shape((8, wide), full),
-            shape((3 * wide, wide), low),
-            shape((wide, wide), low),
-            shape((wide, wide), low),
-            shape((wide, wide), low),
-            shape((wide, wide), low),
-        ],
-        in_specs=[hbm, hbm] + [vmem] * 4 + [hbm] * 17,
-        out_specs=[hbm, vmem] + [hbm] * 5,
+    heights = (wide, wide, wide, wide, 3 * wide)
+    more_outs, more_scratch = [], []
+    plan = None
+    options = {}
+    if ffn:
+        grads = [(2, 2, 2, h // 8, wide) for h in heights] + [(2, 2, 2, CUT, wide)]
+        plan = (
+            tuple(g[3] // CUT for g in grads),
+            tuple(f.shape[0] // FCUT for f in ffn),
+        )
+        outs, lands, bufs, sems = Sums.shapes(*plan, wide)
+        more_outs = outs + lands
+        more_scratch = [buf((CUT, wide)), dma((8,))] + bufs + sems
+        options = dict(collective_id=1, has_side_effects=True)
+    else:
+        grads = [(h, wide) for h in heights]
+    ffn = list(ffn)
+    results = pl.pallas_call(
+        functools.partial(attention_backward_kernel, plan),
+        out_shape=[shape((rows, wide), full), shape((8, wide), full)]
+        + [shape(g, low) for g in grads]
+        + more_outs,
+        in_specs=[hbm, hbm] + [vmem] * 4 + [hbm] * (17 + len(ffn)),
+        out_specs=[hbm, vmem] + [hbm] * (len(grads) + len(more_outs)),
         scratch_shapes=[
-            *[buf(w.shape) for w in weights],
+            buf((wide, wide)),
+            buf((2, 3 * wide, TILE)),
             buf((rows, wide)),
             buf(cond.shape),
             buf((rows, wide)),
@@ -1619,14 +1726,18 @@
             buf((rows, wide)),
             buf((2, 2, rows, rows)),
             buf((2, 2, rows, COND_ROWS)),
-            buf((2, TILE, wide)),
-            dma((17,)),
+            buf((2, GRAD_TILE, wide)),
+            dma((14,)),
             dma((2,)),
             dma((2,)),
+            dma((2,)),
+            dma((2, 2)),
             dma,
+            *more_scratch,
         ],
-        compiler_params=pltpu.CompilerParams(vmem_limit_bytes=VMEM_LIMIT),
-    )(x, cond, norms, *tables, *weights, *kept, d_norm, d_out)
+        compiler_params=pltpu.CompilerParams(vmem_limit_bytes=VMEM_LIMIT, **options),
+    )(x, cond, norms, *tables, *weights, *kept, d_norm, d_out, *ffn)
+    return results[0], results[1], results[2:7], results[8:10]
 
 
 def per_device(
@@ -1689,55 +1800,50 @@
         grad_up = dot_tn(d_up, all_act).astype(jnp.bfloat16)
         grad_down = dot_tn(hidden, all_grad).astype(jnp.bfloat16)
     outputs = (section_two + mlp_out.astype(jnp.float32)).astype(jnp.bfloat16)
-    ffn_sums = list(lax.psum((grad_gate, grad_up), "rep"))
-    d_tokens, norm_sums, grad_qkv, grad_out_one, grad_query_two, grad_out_two, grad_kv_two = (
-        attention_backward(
-            inputs[0],
-            padded_cond,
-            norms,
-            tables,
-            whole,
-            kept[:-1],
-            d_norm3,
-            grad_mlp,
-        )
+    groups = lax.axis_size("grp")
+    fused = groups == 8 and lax.axis_size("rep") == 4
+    ffn_grads = [grad_gate, grad_up, grad_down]
+    d_tokens, norm_sums, grads, totals = attention_backward(
+        inputs[0],
+        padded_cond,
+        norms,
+        tables,
+        whole,
+        kept[:-1],
+        d_norm3,
+        grad_mlp,
+        ffn_grads if fused else [],
     )
-    norm_stack = norm_sums[:6].astype(jnp.bfloat16)
-    groups = lax.axis_size("grp")
-    attention_parts = [grad_qkv, grad_out_one, grad_query_two, grad_out_two, grad_kv_two]
-    if groups == 8 and lax.axis_size("rep") == 4:
-        norm_part = jnp.swapaxes(norm_stack.reshape(6, groups, own_width), 0, 1)
-        norm_part = norm_part.reshape(groups, 1, 6 * own_width)
-        norm_part = jnp.pad(norm_part, ((0, 0), (0, CUT - 1), (0, D - 6 * own_width)))
-        kv2_rows = grad_kv_two.shape[0] // groups
-        parts = attention_parts + [norm_part]
-        parts = [p.reshape(2, 2, 2, -1, D) for p in parts]
-        total_a, total_f = reduce_all(parts, [grad_down])
-        ffn_sums.append(total_f)
+    own_at = lax.axis_index("grp") * own_width
+    if fused:
+        total_a, total_f = totals
         ends = []
-        for p in parts:
-            ends.append((ends[-1] if ends else 0) + p.shape[3])
-        pieces = [total_a[e - p.shape[3] : e] for e, p in zip(ends, parts)]
-        norm_total = pieces[5][0, : 6 * own_width].reshape(6, own_width)
-        kv2_total = jnp.swapaxes(pieces[4].reshape(kv2_rows, 2, D // 2), 0, 1)
-        pieces[4] = kv2_total.reshape(2 * kv2_rows, D // 2)
-        attention_sums = pieces[:5]
+        for g in grads:
+            ends.append((ends[-1] if ends else 0) + g.shape[3])
+        grad_out_two, grad_query_two, kv2_total, grad_out_one, grad_qkv = (
+            total_a[e - g.shape[3] : e] for e, g in zip(ends, grads)
+        )
+        norm_total = total_a[ends[-1] : ends[-1] + 6]
+        own = w_gate.shape[0]
+        ffn_sums = [total_f[k * own : (k + 1) * own] for k in range(3)]
+        kv2_total = kv2_total.reshape(-1, UNIT, 2, D // 2)
+        grad_kv_two = jnp.swapaxes(kv2_total, 1, 2).reshape(-1, D // 2)
     else:
-        kv2_part = jnp.swapaxes(grad_kv_two.reshape(-1, 192, 2, D // 2), 1, 2)
-        attention_parts[4] = kv2_part.reshape(2 * D, D // 2)
-        norm_total = lax.psum(norm_stack, ("grp", "rep"))
-        norm_total = lax.dynamic_slice_in_dim(
-            norm_total, lax.axis_index("grp") * own_width, own_width, axis=1
-        )
-        attention_sums = [
-            lax.psum_scatter(g, "grp", scatter_dimension=0, tiled=True) for g in attention_parts
-        ]
-        attention_sums = [lax.psum(g, "rep") for g in attention_sums]
-        ffn_sums.append(lax.psum(grad_down, "rep"))
+        grads = list(grads)
+        kv2_part = jnp.swapaxes(grads[2].reshape(-1, UNIT, 2, D // 2), 1, 2)
+        grads[2] = kv2_part.reshape(2 * D, D // 2)
+        norm_total = lax.psum(norm_sums[:6].astype(jnp.bfloat16), ("grp", "rep"))
+        shards = [lax.psum_scatter(g, "grp", scatter_dimension=0, tiled=True) for g in grads]
+        grad_out_two, grad_query_two, grad_kv_two, grad_out_one, grad_qkv = lax.psum(
+            tuple(shards), "rep"
+        )
+        ffn_sums = lax.psum(tuple(ffn_grads), "rep")
+    norm_total = lax.dynamic_slice_in_dim(norm_total, own_at, own_width, axis=1)
+    grad_qkv, grad_out_one, grad_query_two, grad_out_two, grad_kv_two = (
+        g.astype(jnp.float32)
+        for g in (grad_qkv, grad_out_one, grad_query_two, grad_out_two, grad_kv_two)
+    )
     norm_total = norm_total.astype(jnp.float32)
-    grad_qkv, grad_out_one, grad_query_two, grad_out_two, grad_kv_two = (
-        g.astype(jnp.float32) for g in attention_sums
-    )
     grad_gate, grad_up, grad_down = (g.astype(jnp.float32) for g in ffn_sums)
     return (
         outputs[None],

time: 693 us -> 653 us (0.942)
  Pallas kernels: 640 us -> 605 us
    pallas_call x2 -> x1, Pallas kernels: 348 us -> 312 us  [attention_backward(): pl.pallas_call(functools.partial(attention_backward_kernel, plan), out_sh...]
  transfers between devices with their start and end apart: 2 -> 1, of which waited for: 0 -> 0; matrix products, arithmetic and copies ran while one was open for 4% -> 1% of each run, Pallas kernels for 73% -> 24%
where the time goes in v4:
time: 653 us; the launch traced here: 652 us
  Pallas kernels  605 us (93%)
  other arithmetic  21.6 us (3%)
  between operations  15 us (2%)
  local copies, waits for them, and re-layouts  10.5 us (2%)
    pallas_call x1, Pallas kernels, attention_backward(): pl.pallas_call(functools.partial(attention_backward_kernel, plan), out_sh...  312 us
    pallas_call x1, Pallas kernels, attention_forward(): pl.pallas_call(functools.partial(attention_forward_kernel, pieces), out_s...  156 us
    pallas_call x1, Pallas kernels, ffn_all(): pl.pallas_call(ffn_kernel, out_shape=[jax.ShapeDtypeStruct((seq_len, wide...  137 us
  transfers between devices with their start and end apart: 1, of which 0 were waited for; matrix products, arithmetic and copies ran while one was open for 1% of the time, Pallas kernels for 24%

profile of v4, /device:TPU:24, one launch (start us, length us, event | category | flops | bytes accessed | tf_op | source)
XLA Modules:
  0.0 652.0 jit_solution(9352989480443560683)
XLA Ops:
  7.2 0.0 copy-start.7
  7.2 0.0 copy-start.8
  7.2 0.0 copy-start.9
  7.2 0.0 copy-start.10
  7.2 0.0 copy-start.11
  7.2 0.0 copy-start.12
  7.2 0.0 copy-start.6
  7.3 0.0 all-gather.3.cloned.1.call-start
  7.9 2.5 multiply_convert_fusion
  10.4 0.0 copy-start.4
  10.4 0.0 all-gather.3.cloned.1.call-update
  10.5 0.1 pad.11.clone
  10.5 0.1 pad.8.clone
  10.6 0.0 copy-done.7
  10.6 0.0 copy-done.8
  10.7 0.0 copy-done.9
  10.7 0.0 copy-done.10
  10.7 0.0 copy-done.11
  10.7 0.0 copy-done.12
  10.8 0.0 copy-done.6
  10.8 0.2 multiply_sine_fusion
  11.0 0.8 copy.37.sine_left.refs_4_
  11.8 0.1 maximum_maximum_fusion
  11.9 0.8 copy.36.cosine.refs_3_
  12.8 0.8 copy.38.sine_right.refs_5_
  13.6 0.0 copy-done.4
  13.6 0.8 pad.5.cond_in.refs_1_
  14.4 0.5 dynamic_update_slice.3.norms_in
  14.9 0.0 copy-start.5
  14.9 0.6 copy-done.5
  15.5 155.6 %shard_map.306 = (f32[16,1536]{1,0:T(8,128)}, bf16[4608,1536]{1,0:T(8,128)(2,1)}, bf16[1536,1536]{1,0:T(8,128)(2,1)}, bf16[1536,1536]{1,0:T(8,128)(2,1)}, bf16[1...) custom-call(bf16[384,1536]{1,0:T(8,128)(2,1)} %bitcast.22, ...), custom_call_target="tpu_custom_call" | custom-call | tf_op jit(solution)/shard_map/pallas_call | solution.py:1348
  171.1 2.5 fusion.3.refs_22_
  173.6 0.0 all-gather.3.cloned.1.call-done
  173.6 137.3 %shard_map.307 = (bf16[384,1536]{1,0:T(8,128)(2,1)}, bf16[384,1536]{1,0:T(8,128)(2,1)}, bf16[768,1536]{1,0:T(8,128)(2,1)}, bf16[768,1536]{1,0:T(8,128)(2,1)}, bf16[768,1536]{1,0:T(8,128)(2,1)}) custom-call(bf16[384,1536]{1,0:T(8,128)(2,1)} %get-tuple-element.42.act_in, bf16[3072,1536]{1,0:T(8,128)(2,1)} %bitcast.20, bf16[768,1536]{1,0:T(8,128)(2,1)} %gate_in.1, ...), custom_call_target="tpu_custom_call" | custom-call | tf_op jit(solution)/shard_map/pallas_call | solution.py:952
  310.9 312.0 %shard_map.308 = (f32[384,1536]{1,0:T(8,128)}, f32[8,1536]{1,0:T(8,128)}, bf16[2,2,2,192,1536]{4,3,2,1,0:T(8,128)(2,1)}, bf16[2,2,2,192,1536]{4,3,2,1,0:T(8,128)...) custom-call(bf16[384,1536]{1,0:T(8,128)(2,1)} %bitcast.23, ...), custom_call_target="tpu_custom_call" | custom-call | tf_op jit(solution)/shard_map/pallas_call | solution.py:1701
  622.9 0.7 slice.45
  623.6 0.0 copy-start.1
  623.6 3.9 slice_convert_fusion.3
  627.5 0.0 copy-done.1
  627.5 0.0 copy-start
  627.5 0.0 copy-start.3
  627.5 2.0 slice_convert_fusion.4
  629.5 0.9 copy-done
  630.5 0.3 copy-done.3
  630.8 1.4 fusion
  632.2 0.1 dynamic-slice_convert_fusion
  632.2 0.6 fusion.2
  632.8 0.8 reshape.67
  633.6 1.1 copy.42
  634.7 0.0 copy-start.2
  634.7 9.0 %slice_convert_fusion = (f32[768,1536]{1,0:T(8,128)}, f32[768,1536]{1,0:T(8,128)}, f32[768,1536]{1,0:T(8,128)}) fusion(bf16[2304,1536]{1,0:T(8,128)(2,1)} %get-tuple-element.65), kind=kLoop, calls=%fused_computation | loop fusion | flops 3538944 | bytes 21233664 | tf_op jit(solution)/shard_map/convert_element_type | solution.py:1847
  643.8 0.0 copy-done.2
  643.8 1.4 copy.46
  (18 shorter events, 0.2 us)
Async XLA Ops:
  7.2 3.5 copy-start.7
  7.2 3.4 copy-start.8
  7.2 3.5 copy-start.9
  7.2 3.5 copy-start.10
  7.2 3.5 copy-start.11
  7.2 3.5 copy-start.12
  7.2 3.5 copy-start.6
  7.3 166.3 %all-gather.3.cloned.1.call-start = ((), (), s32[]{:S(2)}) async-start(), calls=%async_computation | async-start | bytes 10616832 | tf_op jit(solution)/shard_map/all_gather | solution.py:1775
  10.4 3.2 copy-start.4
  14.9 0.6 copy-start.5
  623.6 3.9 copy-start.1
  627.5 2.9 copy-start
  627.5 3.3 copy-start.3
  634.7 9.0 %copy-start.2 = (f32[384,1536]{1,0:T(8,128)S(1)}, f32[384,1536]{1,0:T(8,128)}, u32[]{:S(2)}) copy-start(f32[384,1536]{1,0:T(8,128)} %get-tuple-element.63) | copy-start | bytes 7077892
Sparse Core Ops, SparseCore 0:
  10.6 98.1 all-gather.2

commit v5 on v4

--- a/solution.py
+++ b/solution.py
@@ -236,7 +236,7 @@
 
 
 CUT = 48
-FCUT = 64
+FCUT = 48
 UNIT = 192
 MATE_SLOTS = 4
 OWN_SLOTS = 2
@@ -247,8 +247,9 @@
 
 class Sums:
     def __init__(self, pieces, ffn_pieces, parts, ffn, outs, lands, bufs, sems):
+        self.near = pieces[0]
         self.pieces, self.ffn_pieces, self.parts, self.ffn = pieces, ffn_pieces, parts, ffn
-        self.out_a, self.out_f = outs
+        self.out_n, self.out_a, self.out_f = outs
         self.one_land, self.two_land, self.low_a, self.up_a, self.low_f, self.up_f = lands
         (
             self.mate_buf,
@@ -277,6 +278,7 @@
             self.low_sem,
             self.up_sem,
             self.out_sem,
+            self.near_sem,
             self.credit,
         ) = sems
         me = lax.axis_index("grp")
@@ -291,7 +293,7 @@
         self.up_dev = (me, plane + 1)
         self.total = sum(pieces)
         self.ffn_count = sum(ffn_pieces)
-        self.chain_total = self.ffn_count + self.total
+        self.chain_total = self.ffn_count + self.total - self.near
 
     def start(self):
         meet([self.mate_dev, self.x_dev, self.y_dev], self.low_dev, self.up_dev, self.plane)
@@ -416,11 +418,19 @@
         self.two_load(i).wait()
         self.done[i] = add(self.sums[slot, self.y, self.x], self.two_buf[lax.rem(i, LAND_SLOTS)])
 
+        @pl.when(i < self.near)
+        def _():
+            self.near_copy(i).start()
+
         def body(by_x):
             self.one_copy(i, slot, by_x).wait_send()
             self.two_copy(i, slot, by_x).wait_send()
 
         self.either(i, body)
+
+    def near_copy(self, i):
+        rows = pl.ds(pl.multiple_of(i * CUT, 16), CUT)
+        return pltpu.make_async_copy(self.done.at[i], self.out_n.at[rows], self.near_sem.at[i])
 
     def ffn_load(self, j):
         base = 0
@@ -467,7 +477,7 @@
             rows = pl.ds(pl.multiple_of(i * CUT, 16), CUT)
             part = pl.ds(0, CUT)
             body(
-                self.done.at[i],
+                self.done.at[i + self.near],
                 self.low_a.at[i],
                 self.up_a.at[i],
                 self.low_buf.at[slot, part],
@@ -594,9 +604,9 @@
         self.stages(j + 1, self.ffn_count, ((self.ffn_load, 0),))
         for stage, behind in (
             (self.inward, 0),
+            (self.outward, 8),
             (self.root, 6),
             (self.middle, 3),
-            (self.outward, 8),
             (self.root_arrives, 5),
             (self.middle_arrives, 2),
             (self.drain, 11),
@@ -607,29 +617,42 @@
         self.ffn_load(jnp.int32(0))
 
     def finish(self, z_next, xy_next):
-        steps = self.chain_total + 12 - z_next
+        both = (self.total + 8 - xy_next + 1) // 2
 
         def body(u, carry):
-            self.z_step(z_next + u)
-            self.xy_step(xy_next + u)
+            self.z_step(z_next + 3 * u)
+            self.xy_step(xy_next + 2 * u)
+            self.z_step(z_next + 3 * u + 1)
+            self.xy_step(xy_next + 2 * u + 1)
+            self.z_step(z_next + 3 * u + 2)
             return carry
 
-        lax.fori_loop(0, steps, body, 0)
+        def chain_only(u, carry):
+            self.z_step(u)
+            return carry
+
+        lax.fori_loop(0, both, body, 0)
+        lax.fori_loop(z_next + 3 * both, self.chain_total + 12, chain_only, 0)
         for i in range(max(self.total - MATE_SLOTS, 0), self.total):
             self.mate_copy(0, pl.ds(0, CUT), i % MATE_SLOTS).wait_send()
+        for i in range(self.near):
+            self.near_copy(i).wait()
 
     @staticmethod
     def shapes(pieces, ffn_pieces, wide):
         total, ffn_count = sum(pieces), sum(ffn_pieces)
-        chain_total = total + ffn_count
+        near = pieces[0]
+        far = total - near
+        chain_total = far + ffn_count
         low = jnp.bfloat16
         dma = pltpu.SemaphoreType.DMA
         shape = lambda *s: jax.ShapeDtypeStruct(s, low)
         buf = lambda *s: pltpu.VMEM(s, low)
-        outs = [shape(total * CUT, wide), shape(ffn_count * FCUT, wide)]
+        outs = [shape(n, wide) for n in (near * CUT, far * CUT, ffn_count * FCUT)]
         lands = [
             shape(total, 2, CUT, wide),
-            *[shape(total, CUT, wide)] * 3,
+            shape(total, CUT, wide),
+            *[shape(far, CUT, wide)] * 2,
             *[shape(ffn_count, FCUT, wide)] * 2,
         ]
         bufs = [
@@ -659,6 +682,7 @@
             dma((LAND_SLOTS,)),
             dma((LAND_SLOTS,)),
             dma((chain_total,)),
+            dma((near,)),
             pltpu.SemaphoreType.REGULAR,
         ]
         return outs, lands, bufs, sems
@@ -699,7 +723,7 @@
     gate_in,
     up_in,
     down_in,
-    out_ref,
+    out_part,
     dn_ref,
     grad_gate,
     grad_up,
@@ -715,6 +739,7 @@
     pair,
     mine,
     stage,
+    out_buf,
     passed,
     final,
     tile_buf,
@@ -729,6 +754,7 @@
     flow_recv,
     tile_sem,
     end_sem,
+    part_sem,
 ):
     me = lax.axis_index("grp")
     plane = lax.axis_index("rep")
@@ -791,21 +817,28 @@
             copy.start()
             cot_copies.append(copy)
 
-    def pair_copy(kind, t):
-        return remote(
-            stage.at[kind], pair.at[kind, t], pair_send.at[kind], pair_recv.at[kind, t], mate_dev
-        )
-
-    def flow(kind, lane):
+    def pair_copy(t):
+        return remote(stage, pair.at[t], pair_send, pair_recv.at[t], mate_dev)
+
+    def flow(lane):
         src, dst, device = (
-            (pair.at[kind, 2], final.at[kind, 0], x_dev),
-            (pair.at[kind, 4], final.at[kind, 1], x_dev),
-            (pair.at[kind, 5], final.at[kind, 2], y_dev),
-            (pair.at[kind, 3], final.at[kind, 3], y_dev),
-            (pair.at[kind, 6], passed.at[kind, 0], x_dev),
-            (pair.at[kind, 7], passed.at[kind, 1], y_dev),
+            (pair.at[2], final.at[0], x_dev),
+            (pair.at[4], final.at[1], x_dev),
+            (pair.at[5], final.at[2], y_dev),
+            (pair.at[3], final.at[3], y_dev),
+            (pair.at[6], passed.at[0], x_dev),
+            (pair.at[7], passed.at[1], y_dev),
         )[lane]
-        return remote(src, dst, flow_send.at[kind, lane], flow_recv.at[kind, lane], device)
+        return remote(src, dst, flow_send.at[lane], flow_recv.at[lane], device)
+
+    def part_copy(t, other):
+        owner = me ^ (2 * STEP_CHIP[t] + other)
+        place = out_part.at[owner // 4, lax.rem(owner // 2, 2), lax.rem(owner, 2)]
+        return pltpu.make_async_copy(
+            out_buf.at[t % 2, pl.ds(other * half, half)],
+            place.at[pl.ds(STEP_HALF[t] * half, half)],
+            part_sem.at[t % 2, other],
+        )
 
     def forward_tiles(t):
         def tile(n, carry):
@@ -828,28 +861,25 @@
     def backward_tiles(t):
         def tile(n, carry):
             cut = pl.ds(pl.multiple_of(n * TILE, TILE), TILE)
-            out = dot(hidden[t], w_down[:, cut])
-            mine[0, :, cut] = out[:half].astype(low)
-            stage[0, :, cut] = out[half:].astype(low)
+            out_buf[lax.rem(t, 2), :, cut] = dot(hidden[t], w_down[:, cut]).astype(low)
             dn = dot(d_gate[t], w_gate[:, cut]) + dot(d_up[t], w_up[:, cut])
-            mine[1, :, cut] = dn[:half].astype(low)
-            stage[1, :, cut] = dn[half:].astype(low)
+            mine[:, cut] = dn[:half].astype(low)
+            stage[:, cut] = dn[half:].astype(low)
             return carry
 
         lax.fori_loop(0, wide // TILE, tile, 0)
 
     def join(t, events):
-        for kind in range(2):
-            pair_copy(kind, t).wait()
-            pair[kind, t] = add(pair[kind, t], mine[kind])
-            for when, lane in events:
-                if when is None:
-                    flow(kind, lane).start()
-                else:
-
-                    @pl.when(t == when)
-                    def _(kind=kind, lane=lane):
-                        flow(kind, lane).start()
+        pair_copy(t).wait()
+        pair[t] = add(pair[t], mine[...])
+        for when, lane in events:
+            if when is None:
+                flow(lane).start()
+            else:
+
+                @pl.when(t == when)
+                def _(lane=lane):
+                    flow(lane).start()
 
     for copy in own_copies + weights:
         copy.wait()
@@ -878,9 +908,24 @@
         def _():
             join(t - 1, ((2, 0), (3, 3), (6, 4)))
 
+        @pl.when(t >= 2)
+        def _():
+            for other in range(2):
+                pltpu.make_async_copy(
+                    out_buf.at[lax.rem(t, 2), pl.ds(other * half, half)],
+                    out_part.at[0, 0, 0, pl.ds(0, half)],
+                    part_sem.at[lax.rem(t, 2), other],
+                ).wait()
+
         backward_tiles(t)
-        for kind in range(2):
-            pair_copy(kind, t).start()
+        pair_copy(t).start()
+        for u in range(8):
+
+            @pl.when(t == u)
+            def _(u=u):
+                for other in range(2):
+                    part_copy(u, other).start()
+
         return carry
 
     lax.fori_loop(0, 8, step, 0)
@@ -890,6 +935,12 @@
         return pltpu.make_async_copy(
             tile_buf.at[slot], target.at[:, cut], tile_sem.at[slot]
         )
+
+    def pass_on():
+        for lane, t, onward in ((4, 5, 2), (5, 4, 1)):
+            flow(lane).wait_recv()
+            pair[t] = add(pair[t], passed[lane - 4])
+            flow(onward).start()
 
     tiles = wide // TILE
     for k, (left, right, target) in enumerate(
@@ -912,30 +963,26 @@
             return carry
 
         lax.fori_loop(0, tiles, tile, 0)
+        if k == 1:
+            pass_on()
     for slot in range(2):
         write(grad_down, slot, pl.ds(0, TILE)).wait()
 
-    for kind in range(2):
-        for lane, t, onward in ((4, 5, 2), (5, 4, 1)):
-            flow(kind, lane).wait_recv()
-            pair[kind, t] = add(pair[kind, t], passed[kind, lane - 4])
-            flow(kind, onward).start()
     ends = []
-    for kind, target in enumerate((out_ref, dn_ref)):
-        for h in range(2):
-            flow(kind, h).wait_recv()
-            flow(kind, 2 + h).wait_recv()
-            pair[kind, h] = add(pair[kind, h], final[kind, h], final[kind, 2 + h])
-            copy = pltpu.make_async_copy(
-                pair.at[kind, h], target.at[pl.ds(h * half, half)], end_sem.at[kind, h]
-            )
-            copy.start()
-            ends.append(copy)
+    for h in range(2):
+        flow(h).wait_recv()
+        flow(2 + h).wait_recv()
+        pair[h] = add(pair[h], final[h], final[2 + h])
+        copy = pltpu.make_async_copy(pair.at[h], dn_ref.at[pl.ds(h * half, half)], end_sem.at[h])
+        copy.start()
+        ends.append(copy)
     for copy in ends:
         copy.wait()
-    for kind in range(2):
-        for lane in range(6):
-            flow(kind, lane).wait_send()
+    for t in (6, 7):
+        for other in range(2):
+            part_copy(t, other).wait()
+    for lane in range(6):
+        flow(lane).wait_send()
     for t in range(8):
         act_copy(t, 1).wait_send()
         if t >= 2:
@@ -951,7 +998,10 @@
     dma = pltpu.SemaphoreType.DMA
     return pl.pallas_call(
         ffn_kernel,
-        out_shape=[jax.ShapeDtypeStruct((seq_len, wide), low)] * 2
+        out_shape=[
+            jax.ShapeDtypeStruct((2, 2, 2, seq_len, wide), low),
+            jax.ShapeDtypeStruct((seq_len, wide), low),
+        ]
         + [jax.ShapeDtypeStruct((rows, wide), low)] * 3,
         in_specs=[hbm] * 5,
         out_specs=[hbm] * 5,
@@ -964,21 +1014,23 @@
             pltpu.VMEM((8, seq_len, rows), low),
             pltpu.VMEM((8, seq_len, rows), low),
             pltpu.VMEM((8, seq_len, rows), low),
-            pltpu.VMEM((2, 8, half, wide), low),
+            pltpu.VMEM((8, half, wide), low),
+            pltpu.VMEM((half, wide), low),
+            pltpu.VMEM((half, wide), low),
+            pltpu.VMEM((2, seq_len, wide), low),
             pltpu.VMEM((2, half, wide), low),
-            pltpu.VMEM((2, half, wide), low),
-            pltpu.VMEM((2, 2, half, wide), low),
-            pltpu.VMEM((2, 4, half, wide), low),
+            pltpu.VMEM((4, half, wide), low),
             pltpu.VMEM((2, rows, TILE), low),
             dma((3,)),
             dma((8, 2)),
             dma((2,)),
             dma((8, 2)),
             dma((8, 2)),
+            dma,
+            dma((8,)),
+            dma((6,)),
+            dma((6,)),
             dma((2,)),
-            dma((2, 8)),
-            dma((2, 6)),
-            dma((2, 6)),
             dma((2,)),
             dma((2, 2)),
         ],
@@ -1404,12 +1456,12 @@
     act_one_in, heads_in, prob_in, flat_one_in, section_one_in, act_two_in = take(6)
     query_two_in, kv_two_in, prob_two_in, flat_two_in, section_two_in = take(5)
     d_norm_in, d_out_in = take(2)
-    ffn_in = take(3) if plan else []
+    out_part, *ffn_in = take(4) if plan else [None]
     d_inputs_out, sums = take(2)
     grad_out2, grad_query2, grad_kv2, grad_out, grad_qkv = take(5)
     if plan:
         (grad_norm,) = take(1)
-        sum_outs, lands = take(2), take(6)
+        sum_outs, lands = take(3), take(6)
     w_small, w_tile = take(2)
     x, cond, act_one, heads, flat_one, section_one, act_two = take(7)
     query_two, kv_two, flat_two, section_two, d_norm = take(5)
@@ -1417,8 +1469,8 @@
     in_sem, weight_sem, tile_sem, prob_sem, grad_sem, end_sem = take(6)
     if plan:
         norm_buf, norm_sem = take(2)
-        bufs, sems = take(9), take(16)
-        parts = (grad_out2, grad_query2, grad_kv2, grad_out, grad_qkv, grad_norm)
+        bufs, sems = take(9), take(17)
+        parts = (out_part, grad_out2, grad_query2, grad_kv2, grad_out, grad_qkv, grad_norm)
         work = Sums(plan[0], plan[1], parts, ffn_in, sum_outs, lands, bufs, sems)
     else:
         work = NoSums()
@@ -1466,6 +1518,18 @@
         for p in range(2):
             prob_copy(src, buf, p, p).start()
 
+    at = {"z": 0, "xy": 0}
+
+    def serve(*kinds):
+        for kind in kinds:
+            (work.z_step if kind == "z" else work.xy_step)(jnp.int32(at[kind]))
+            at[kind] += 1
+
+    def serve_pairs(p, kind, every):
+        @pl.when(lax.rem(p, every) == every - 1)
+        def _():
+            (work.z_step if kind == "z" else work.xy_step)(at[kind] + p // every)
+
     def unit_copy(target, n, half, slot):
         src = grad_buf.at[slot, pl.ds(half * UNIT, UNIT)]
         unit = 2 * n + half
@@ -1478,7 +1542,7 @@
             place = target.at[pl.ds(pl.multiple_of(unit * UNIT, 16), UNIT)]
         return pltpu.make_async_copy(src, place, grad_sem.at[slot, half])
 
-    def grad_rows(target, count, compute):
+    def grad_rows(target, count, compute, every=0):
         def step(n, carry):
             slot = lax.rem(n, 2)
 
@@ -1490,6 +1554,8 @@
             compute(n, slot)
             for half in range(2):
                 unit_copy(target, n, half, slot).start()
+            if every:
+                serve_pairs(n, "z", every)
             return carry
 
         lax.fori_loop(0, count, step, 0)
@@ -1497,14 +1563,14 @@
             for half in range(2):
                 unit_copy(target, 0, half, slot).wait()
 
-    def weight_rows(left, right, target):
+    def weight_rows(left, right, target, every=0):
         def compute(n, slot):
             columns = left[:, pl.ds(pl.multiple_of(n * GRAD_TILE, 128), GRAD_TILE)]
             for m in range(wide // 512):
                 piece = slice(m * 512, (m + 1) * 512)
                 grad_buf[slot, :, piece] = dot_tn(columns, right[:, piece]).astype(low)
 
-        grad_rows(target, left.shape[1] // GRAD_TILE, compute)
+        grad_rows(target, left.shape[1] // GRAD_TILE, compute, every)
 
     def round_rows():
         def block(n, carry):
@@ -1520,28 +1586,17 @@
 
         tiles_of(wide, body)
 
-    at = {"z": 0, "xy": 0}
-
-    def serve(*kinds):
-        for kind in kinds:
-            (work.z_step if kind == "z" else work.xy_step)(jnp.int32(at[kind]))
-            at[kind] += 1
-
-    def serve_pairs(p, kind, every):
-        @pl.when(lax.rem(p, every) == every - 1)
-        def _():
-            (work.z_step if kind == "z" else work.xy_step)(at[kind] + p // every)
-
     prob_start(prob_two_in, prob_two)
-    serve("z")
+    serve("z", "xy")
     need("section_two", "d_norm", "d_out")
     normalise_back(section_two, gains[2], d_norm, d_low, section_two, sums, 4, rows)
     d_section = section_two
     round_rows()
+    serve("z", "xy")
     need("w_out2")
     through(d_att)
     next_weight("w_query2", query2_in, 0)
-    serve("z")
+    serve("z", "xy")
     need("flat_two")
     weight_rows(d_low, flat_two, grad_out2)
     serve("xy", "z")
@@ -1566,17 +1621,17 @@
         def _():
             prob_copy(prob_two_in, prob_two, p + 2, slot).start()
 
-        serve_pairs(p, "z", 3)
-        serve_pairs(p, "xy", 4)
+        serve_pairs(p, "z", 2)
+        serve_pairs(p, "xy", 3)
 
     pair_loop(cross_pair)
-    at["z"] += 4
-    at["xy"] += 3
+    at["z"] += 6
+    at["xy"] += 4
     prob_start(prob_in, prob)
     need("w_query2")
     through(d_norm)
     next_weight("w_out", out_in, 1)
-    serve("z")
+    serve("z", "xy")
     need("act_two")
     weight_rows(d_low, act_two, grad_query2)
     serve("z", "xy")
@@ -1631,14 +1686,23 @@
         def _():
             prob_copy(prob_in, prob, p + 2, slot).start()
 
-        serve_pairs(p, "z", 1)
-        serve_pairs(p, "xy", 2)
+        work.z_step(at["z"] + p + (p + 1) // 2)
+
+        @pl.when(lax.rem(p, 2) == 0)
+        def _():
+            work.z_step(at["z"] + p + 1 + p // 2)
+
+        @pl.when(p < 10)
+        def _():
+            serve_pairs(p, "xy", 1)
+
 
     pair_loop(self_pair)
-    at["z"] += pairs
-    at["xy"] += 6
+    at["z"] += pairs * 3 // 2
+    at["xy"] += 10
     need("act_one")
-    weight_rows(d_heads, act_one, grad_qkv)
+    weight_rows(d_heads, act_one, grad_qkv, 4)
+    at["z"] += 3
     serve("z", "xy")
 
     def first_norm(n, carry):
@@ -1646,6 +1710,7 @@
         cut = pl.ds(pl.multiple_of(n * TILE, TILE), TILE)
         tile_copy(n, slot).wait()
         d_norm[:, cut] = dot(d_heads[...], w_tile[slot]).astype(low)
+        serve_pairs(n, "z", 3)
 
         @pl.when(n + 2 < wide // TILE)
         def _():
@@ -1654,6 +1719,7 @@
         return carry
 
     lax.fori_loop(0, wide // TILE, first_norm, 0)
+    at["z"] += 2
     serve("z", "xy")
     need("x")
     normalise_back(x, gains[0], d_norm, d_section, d_section, sums, 0, rows)
@@ -1673,7 +1739,7 @@
     end.wait()
 
 
-def attention_backward(x, cond, norms, tables, weights, kept, d_norm, d_out, ffn):
+def attention_backward(x, cond, norms, tables, weights, kept, d_norm, d_out, out_part, ffn):
     rows, wide = x.shape
     low, full = jnp.bfloat16, jnp.float32
     hbm = pl.BlockSpec(memory_space=pltpu.HBM)
@@ -1688,7 +1754,7 @@
     if ffn:
         grads = [(2, 2, 2, h // 8, wide) for h in heights] + [(2, 2, 2, CUT, wide)]
         plan = (
-            tuple(g[3] // CUT for g in grads),
+            tuple(g[3] // CUT for g in [out_part.shape] + grads),
             tuple(f.shape[0] // FCUT for f in ffn),
         )
         outs, lands, bufs, sems = Sums.shapes(*plan, wide)
@@ -1697,7 +1763,7 @@
         options = dict(collective_id=1, has_side_effects=True)
     else:
         grads = [(h, wide) for h in heights]
-    ffn = list(ffn)
+    ffn = [out_part] + list(ffn) if ffn else []
     results = pl.pallas_call(
         functools.partial(attention_backward_kernel, plan),
         out_shape=[shape((rows, wide), full), shape((8, wide), full)]
@@ -1737,7 +1803,115 @@
         ],
         compiler_params=pltpu.CompilerParams(vmem_limit_bytes=VMEM_LIMIT, **options),
     )(x, cond, norms, *tables, *weights, *kept, d_norm, d_out, *ffn)
-    return results[0], results[1], results[2:7], results[8:10]
+    return results[0], results[1], results[2:7], results[8:11]
+
+
+END_SLOTS = 4
+
+
+def end_kernel(near, far, ffn, section, *refs):
+    outs, (low_buf, full_buf, in_sem, out_sem) = refs[:9], refs[9:]
+    outputs, out2, query2, kv2, out, qkv, gate, up, down = outs
+    wide = low_buf.shape[2]
+    jobs = []
+    base = 0
+    for target in (out2, query2, kv2, out, qkv):
+        rows = target.shape[0] * target.shape[1] // wide
+        jobs += [(far, base + r, target, r) for r in range(0, rows, UNIT)]
+        base += rows
+    base = 0
+    for target in (gate, up, down):
+        jobs += [(ffn, base + r, target, r) for r in range(0, target.shape[0], UNIT)]
+        base += target.shape[0]
+    jobs += [(near, r, outputs, r) for r in range(0, outputs.shape[0], UNIT)]
+
+    def loads(n):
+        source, row, target, place = jobs[n]
+        slot = n % END_SLOTS
+        copies = [
+            pltpu.make_async_copy(
+                source.at[pl.ds(row, UNIT)], low_buf.at[slot], in_sem.at[slot, 0]
+            )
+        ]
+        if target is outputs:
+            copies.append(
+                pltpu.make_async_copy(
+                    section.at[pl.ds(place, UNIT)], full_buf.at[slot], in_sem.at[slot, 1]
+                )
+            )
+        return copies
+
+    def stores(n):
+        _, _, target, place = jobs[n]
+        slot = n % END_SLOTS
+        if target is outputs:
+            pairs = [(low_buf.at[slot], target.at[pl.ds(place, UNIT)])]
+        elif target is kv2:
+            pairs = [
+                (
+                    full_buf.at[slot, :, pl.ds(h * (wide // 2), wide // 2)],
+                    target.at[pl.ds(2 * place + h * UNIT, UNIT)],
+                )
+                for h in range(2)
+            ]
+        else:
+            pairs = [(full_buf.at[slot], target.at[pl.ds(place, UNIT)])]
+        return [
+            pltpu.make_async_copy(src, dst, out_sem.at[slot, k])
+            for k, (src, dst) in enumerate(pairs)
+        ]
+
+    ahead = END_SLOTS - 2
+    for n in range(ahead):
+        for copy in loads(n):
+            copy.start()
+    for n in range(len(jobs)):
+        if n + ahead < len(jobs):
+            if n + ahead >= END_SLOTS:
+                for copy in stores(n + ahead - END_SLOTS):
+                    copy.wait()
+            for copy in loads(n + ahead):
+                copy.start()
+        for copy in loads(n):
+            copy.wait()
+        slot = n % END_SLOTS
+        is_output = jobs[n][2] is outputs
+
+        def block(m, carry, slot=slot, is_output=is_output):
+            cut = pl.ds(pl.multiple_of(m * 32, 32), 32)
+            value = low_buf[slot, cut].astype(jnp.float32)
+            if is_output:
+                low_buf[slot, cut] = (full_buf[slot, cut] + value).astype(low_buf.dtype)
+            else:
+                full_buf[slot, cut] = value
+            return carry
+
+        lax.fori_loop(0, UNIT // 32, block, 0)
+        for copy in stores(n):
+            copy.start()
+    for n in range(max(len(jobs) - END_SLOTS, 0), len(jobs)):
+        for copy in stores(n):
+            copy.wait()
+
+
+def end_all(near, far, ffn, section, out_shapes):
+    hbm = pl.BlockSpec(memory_space=pltpu.HBM)
+    wide = near.shape[1]
+    dma = pltpu.SemaphoreType.DMA
+    return pl.pallas_call(
+        end_kernel,
+        out_shape=[jax.ShapeDtypeStruct(near.shape, near.dtype)]
+        + [jax.ShapeDtypeStruct(s, jnp.float32) for s in out_shapes],
+        in_specs=[hbm] * 4,
+        out_specs=[hbm] * 9,
+        scratch_shapes=[
+            pltpu.VMEM((END_SLOTS, UNIT, wide), near.dtype),
+            pltpu.VMEM((END_SLOTS, UNIT, wide), jnp.float32),
+            dma((END_SLOTS, 2)),
+            dma((END_SLOTS, 2)),
+        ],
+        compiler_params=pltpu.CompilerParams(vmem_limit_bytes=VMEM_LIMIT),
+    )(near, far, ffn, section)
 
 
 def per_device(
@@ -1799,10 +1973,13 @@
         grad_gate = dot_tn(d_gate, all_act).astype(jnp.bfloat16)
         grad_up = dot_tn(d_up, all_act).astype(jnp.bfloat16)
         grad_down = dot_tn(hidden, all_grad).astype(jnp.bfloat16)
-    outputs = (section_two + mlp_out.astype(jnp.float32)).astype(jnp.bfloat16)
     groups = lax.axis_size("grp")
     fused = groups == 8 and lax.axis_size("rep") == 4
     ffn_grads = [grad_gate, grad_up, grad_down]
+    if groups == 8 and not fused:
+        mlp_out = lax.psum_scatter(
+            mlp_out.reshape(-1, D), "grp", scatter_dimension=0, tiled=True
+        )
     d_tokens, norm_sums, grads, totals = attention_backward(
         inputs[0],
         padded_cond,
@@ -1812,22 +1989,28 @@
         kept[:-1],
         d_norm3,
         grad_mlp,
+        mlp_out,
         ffn_grads if fused else [],
     )
     own_at = lax.axis_index("grp") * own_width
     if fused:
-        total_a, total_f = totals
-        ends = []
-        for g in grads:
-            ends.append((ends[-1] if ends else 0) + g.shape[3])
-        grad_out_two, grad_query_two, kv2_total, grad_out_one, grad_qkv = (
-            total_a[e - g.shape[3] : e] for e, g in zip(ends, grads)
-        )
-        norm_total = total_a[ends[-1] : ends[-1] + 6]
-        own = w_gate.shape[0]
-        ffn_sums = [total_f[k * own : (k + 1) * own] for k in range(3)]
-        kv2_total = kv2_total.reshape(-1, UNIT, 2, D // 2)
-        grad_kv_two = jnp.swapaxes(kv2_total, 1, 2).reshape(-1, D // 2)
+        mlp_out, total_a, total_f = totals
+        norm_total = total_a[total_a.shape[0] - CUT :][:6]
+        (
+            outputs,
+            grad_out_two,
+            grad_query_two,
+            grad_kv_two,
+            grad_out_one,
+            grad_qkv,
+            *ffn_sums,
+        ) = end_all(
+            mlp_out,
+            total_a,
+            total_f,
+            section_two,
+            [w.shape for w in (w_out2, w_query2, w_kv2, w_out, w_qkv, w_gate, w_up, w_down)],
+        )
     else:
         grads = list(grads)
         kv2_part = jnp.swapaxes(grads[2].reshape(-1, UNIT, 2, D // 2), 1, 2)
@@ -1838,6 +2021,7 @@
             tuple(shards), "rep"
         )
         ffn_sums = lax.psum(tuple(ffn_grads), "rep")
+        outputs = (section_two + mlp_out.astype(jnp.float32)).astype(jnp.bfloat16)
     norm_total = lax.dynamic_slice_in_dim(norm_total, own_at, own_width, axis=1)
     grad_qkv, grad_out_one, grad_query_two, grad_out_two, grad_kv_two = (
         g.astype(jnp.float32)

time: 653 us -> 614 us (0.940)
  Pallas kernels: 605 us -> 583 us
  other arithmetic: 21.6 us -> 5.32 us
    convert_element_type x3 -> x0, other arithmetic: 14.9 us -> none  [the longest x1 9.04 us: per_device(): grad_gate, grad_up, grad_down = (g.astype(jnp.float32) for g in ffn_sums)]
    pallas_call x1 -> x2, Pallas kernels: 137 us -> 126 us  [the longest x1 111 us: ffn_all(): pl.pallas_call(ffn_kernel, out_shape=[jax.ShapeDtypeStruct((2, 2, 2, seq_...]
    pallas_call x1, Pallas kernels: 312 us -> 301 us  [attention_backward(): pl.pallas_call(functools.partial(attention_backward_kernel, plan), out_sh...]
  transfers between devices with their start and end apart: 1 -> 1, of which waited for: 0 -> 0; matrix products, arithmetic and copies ran while one was open for 1% -> 1% of each run, Pallas kernels for 24% -> 25%
where the time goes in v5:
time: 614 us; the launch traced here: 612 us
  Pallas kernels  583 us (95%)
  between operations  14.9 us (2%)
  local copies, waits for them, and re-layouts  9.18 us (1%)
    pallas_call x1, Pallas kernels, attention_backward(): pl.pallas_call(functools.partial(attention_backward_kernel, plan), out_sh...  301 us
    pallas_call x1, Pallas kernels, attention_forward(): pl.pallas_call(functools.partial(attention_forward_kernel, pieces), out_s...  156 us
    pallas_call x1, Pallas kernels, ffn_all(): pl.pallas_call(ffn_kernel, out_shape=[jax.ShapeDtypeStruct((2, 2, 2, seq_...  111 us
    pallas_call x1, Pallas kernels, end_all(): pl.pallas_call(end_kernel, out_shape=[jax.ShapeDtypeStruct(near.shape, ne...  15.2 us
  transfers between devices with their start and end apart: 1, of which 0 were waited for; matrix products, arithmetic and copies ran while one was open for 1% of the time, Pallas kernels for 25%

profile of v5, /device:TPU:24, one launch (start us, length us, event | category | flops | bytes accessed | tf_op | source)
XLA Modules:
  0.0 612.3 jit_solution(14680805705882125028)
XLA Ops:
  7.2 0.0 copy-start.3
  7.2 0.0 copy-start.4
  7.2 0.0 copy-start.5
  7.2 0.0 copy-start.6
  7.2 0.0 copy-start.7
  7.2 0.0 copy-start.8
  7.2 0.0 copy-start.2
  7.3 0.0 all-gather.3.cloned.1.call-start
  7.9 2.5 multiply_convert_fusion
  10.4 0.0 copy-start
  10.4 0.0 all-gather.3.cloned.1.call-update
  10.5 0.1 pad.11.clone
  10.5 0.1 pad.8.clone
  10.6 0.0 copy-done.3
  10.6 0.0 copy-done.4
  10.7 0.0 copy-done.5
  10.7 0.0 copy-done.6
  10.7 0.0 copy-done.7
  10.7 0.0 copy-done.8
  10.8 0.0 copy-done.2
  10.8 0.2 multiply_sine_fusion
  11.0 0.8 copy.36.sine_left.refs_4_
  11.8 0.1 maximum_maximum_fusion
  11.9 0.8 copy.35.cosine.refs_3_
  12.8 0.8 copy.37.sine_right.refs_5_
  13.6 0.0 copy-done
  13.6 0.8 pad.5.cond_in.refs_1_
  14.4 0.5 dynamic_update_slice.3.norms_in
  14.9 0.0 copy-start.1
  14.9 0.6 copy-done.1
  15.5 155.6 %shard_map.306 = (f32[16,1536]{1,0:T(8,128)}, bf16[4608,1536]{1,0:T(8,128)(2,1)}, bf16[1536,1536]{1,0:T(8,128)(2,1)}, bf16[1536,1536]{1,0:T(8,128)(2,1)}, bf16[1...) custom-call(bf16[384,1536]{1,0:T(8,128)(2,1)} %bitcast.18, ...), custom_call_target="tpu_custom_call" | custom-call | tf_op jit(solution)/shard_map/pallas_call | solution.py:1400
  171.1 2.5 fusion.2.refs_22_
  173.6 0.0 all-gather.3.cloned.1.call-done
  173.6 110.7 %shard_map.307 = (bf16[2,2,2,384,1536]{4,3,2,1,0:T(8,128)(2,1)}, bf16[384,1536]{1,0:T(8,128)(2,1)}, bf16[768,1536]{1,0:T(8,128)(2,1)}, bf16[768,1536]{1,0:T(8,128)(2,1)}, bf16[768,1536]{1,0:T(8,128)(2,1)}) custom-call(bf16[384,1536]{1,0:T(8,128)(2,1)} %get-tuple-element.67.act_in, bf16[3072,1536]{1,0:T(8,128)(2,1)} %bitcast.17, bf16[768,1536]{1,0:T(8,128)(2,1)} %gate_in.1, ...), custom_call_target="tpu_custom_call" | custom-call | tf_op jit(solution)/shard_map/pallas_call | solution.py:999
  284.3 301.3 %shard_map.308 = (f32[384,1536]{1,0:T(8,128)}, f32[8,1536]{1,0:T(8,128)}, bf16[2,2,2,192,1536]{4,3,2,1,0:T(8,128)(2,1)}, bf16[2,2,2,192,1536]{4,3,2,1,0:T(8,128)...) custom-call(bf16[384,1536]{1,0:T(8,128)(2,1)} %bitcast.19, ...), custom_call_target="tpu_custom_call" | custom-call | tf_op jit(solution)/shard_map/pallas_call | solution.py:1767
  585.6 0.7 slice.23
  586.3 0.1 dynamic-slice_convert_fusion
  586.4 0.6 fusion.1
  587.0 15.2 %shard_map.309 = (bf16[384,1536]{1,0:T(8,128)(2,1)}, f32[192,1536]{1,0:T(8,128)}, f32[192,1536]{1,0:T(8,128)}, f32[384,768]{1,0:T(8,128)}, f32[192,1536]{1,0:T(8...) custom-call(bf16[384,1536]{1,0:T(8,128)(2,1)} %get-tuple-element.73.near, ...), custom_call_target="tpu_custom_call" | custom-call | tf_op jit(solution)/shard_map/pallas_call | solution.py:1901
  602.3 3.2 copy.44
  (18 shorter events, 0.2 us)
Async XLA Ops:
  7.2 3.5 copy-start.3
  7.2 3.4 copy-start.4
  7.2 3.5 copy-start.5
  7.2 3.5 copy-start.6
  7.2 3.5 copy-start.7
  7.2 3.5 copy-start.8
  7.2 3.5 copy-start.2
  7.3 166.3 %all-gather.3.cloned.1.call-start = ((), (), s32[]{:S(2)}) async-start(), calls=%async_computation | async-start | bytes 10616832 | tf_op jit(solution)/shard_map/all_gather | solution.py:1949
  10.4 3.2 copy-start
  14.9 0.6 copy-start.1
Sparse Core Ops, SparseCore 0:
  10.6 98.1 all-gather.2

commit v6 on v5

--- a/solution.py
+++ b/solution.py
@@ -714,6 +714,7 @@
 
 STEP_CHIP = (0, 0, 1, 2, 1, 2, 3, 3)
 STEP_HALF = (0, 1, 0, 1, 1, 0, 0, 1)
+FFN_TILE = 512
 TILE = 256
 
 
@@ -840,34 +841,22 @@
             part_sem.at[t % 2, other],
         )
 
-    def forward_tiles(t):
-        def tile(n, carry):
-            cut = pl.ds(pl.multiple_of(n * TILE, TILE), TILE)
-            tokens = act[t].reshape(seq_len, wide)
-            gate = dot_nt(tokens, w_gate[cut])
-            up = dot_nt(tokens, w_up[cut])
-            d_hidden = dot_nt(cot[t].reshape(seq_len, wide), w_down[cut])
-            sigmoid = 1.0 / (1.0 + jnp.exp(-gate))
-            silu = gate * sigmoid
-            hidden[t, :, cut] = (silu * up).astype(low)
-            d_gate[t, :, cut] = (
-                d_hidden * up * (sigmoid * (1.0 + gate * (1.0 - sigmoid)))
-            ).astype(low)
-            d_up[t, :, cut] = (d_hidden * silu).astype(low)
-            return carry
-
-        lax.fori_loop(0, rows // TILE, tile, 0)
-
-    def backward_tiles(t):
-        def tile(n, carry):
-            cut = pl.ds(pl.multiple_of(n * TILE, TILE), TILE)
-            out_buf[lax.rem(t, 2), :, cut] = dot(hidden[t], w_down[:, cut]).astype(low)
-            dn = dot(d_gate[t], w_gate[:, cut]) + dot(d_up[t], w_up[:, cut])
-            mine[:, cut] = dn[:half].astype(low)
-            stage[:, cut] = dn[half:].astype(low)
-            return carry
-
-        lax.fori_loop(0, wide // TILE, tile, 0)
+    def forward_part(t):
+        tokens = act[t].reshape(seq_len, wide)
+        gate = dot_nt(tokens, w_gate[...])
+        up = dot_nt(tokens, w_up[...])
+        d_hidden = dot_nt(cot[t].reshape(seq_len, wide), w_down[...])
+        sigmoid = 1.0 / (1.0 + jnp.exp(-gate))
+        silu = gate * sigmoid
+        hidden[t] = (silu * up).astype(low)
+        d_gate[t] = (d_hidden * up * (sigmoid * (1.0 + gate * (1.0 - sigmoid)))).astype(low)
+        d_up[t] = (d_hidden * silu).astype(low)
+
+    def backward_part(t):
+        out_buf[lax.rem(t, 2)] = dot(hidden[t], w_down[...]).astype(low)
+        dn = dot(d_gate[t], w_gate[...]) + dot(d_up[t], w_up[...])
+        mine[...] = dn[:half].astype(low)
+        stage[...] = dn[half:].astype(low)
 
     def join(t, events):
         pair_copy(t).wait()
@@ -902,7 +891,7 @@
             pltpu.make_async_copy(
                 cot_in.at[pl.ds(0, half)], cot.at[t, other], cot_sem.at[t, other]
             ).wait()
-        forward_tiles(t)
+        forward_part(t)
 
         @pl.when(t > 0)
         def _():
@@ -917,7 +906,7 @@
                     part_sem.at[lax.rem(t, 2), other],
                 ).wait()
 
-        backward_tiles(t)
+        backward_part(t)
         pair_copy(t).start()
         for u in range(8):
 
@@ -942,13 +931,13 @@
             pair[t] = add(pair[t], passed[lane - 4])
             flow(onward).start()
 
-    tiles = wide // TILE
+    tiles = wide // FFN_TILE
     for k, (left, right, target) in enumerate(
         ((d_gate, act, grad_gate), (d_up, act, grad_up), (hidden, cot, grad_down))
     ):
 
         def tile(n, carry, k=k, left=left, right=right, target=target):
-            cut = pl.ds(pl.multiple_of(n * TILE, TILE), TILE)
+            cut = pl.ds(pl.multiple_of(n * FFN_TILE, FFN_TILE), FFN_TILE)
             slot = lax.rem(n, 2)
 
             @pl.when(k * tiles + n >= 2)
@@ -957,7 +946,7 @@
 
             tile_buf[slot] = dot_tn(
                 left[...].reshape(8 * seq_len, rows),
-                right[:, :, :, cut].reshape(8 * seq_len, TILE),
+                right[:, :, :, cut].reshape(8 * seq_len, FFN_TILE),
             ).astype(low)
             write(target, slot, cut).start()
             return carry
@@ -966,7 +955,7 @@
         if k == 1:
             pass_on()
     for slot in range(2):
-        write(grad_down, slot, pl.ds(0, TILE)).wait()
+        write(grad_down, slot, pl.ds(0, FFN_TILE)).wait()
 
     ends = []
     for h in range(2):
@@ -1020,7 +1009,7 @@
             pltpu.VMEM((2, seq_len, wide), low),
             pltpu.VMEM((2, half, wide), low),
             pltpu.VMEM((4, half, wide), low),
-            pltpu.VMEM((2, rows, TILE), low),
+            pltpu.VMEM((2, rows, FFN_TILE), low),
             dma((3,)),
             dma((8, 2)),
             dma((2,)),
@@ -1093,12 +1082,12 @@
     )
 
 
-def tiles_of(count, body):
+def tiles_of(count, body, size=768):
     def step(n, carry):
-        body(pl.ds(pl.multiple_of(n * TILE, TILE), TILE))
+        body(pl.ds(pl.multiple_of(n * size, size), size))
         return carry
 
-    lax.fori_loop(0, count // TILE, step, 0)
+    lax.fori_loop(0, count // size, step, 0)
 
 
 def pair_loop(body):
@@ -1243,7 +1232,7 @@
 
     def project(cut, rotated):
         result = dot_nt(act[...], w_qkv[cut])
-        for part in range(TILE // PAIR):
+        for part in range(cut.size // PAIR):
             piece = result[:, part * PAIR : (part + 1) * PAIR]
             if rotated:
                 piece = turn(piece, cosine[...], sine_left[...], sine_right[...])
@@ -1253,7 +1242,7 @@
         tiles_of(
             wide,
             lambda cut, part=part: project(
-                pl.ds(pl.multiple_of(cut.start + part * wide, TILE), TILE), part < 2
+                pl.ds(pl.multiple_of(cut.start + part * wide, PAIR), cut.size), part < 2
             ),
         )
         gather.step(done + part)
@@ -1621,11 +1610,11 @@
         def _():
             prob_copy(prob_two_in, prob_two, p + 2, slot).start()
 
-        serve_pairs(p, "z", 2)
+        serve_pairs(p, "z", 1)
         serve_pairs(p, "xy", 3)
 
     pair_loop(cross_pair)
-    at["z"] += 6
+    at["z"] += 12
     at["xy"] += 4
     prob_start(prob_in, prob)
     need("w_query2")
@@ -1809,8 +1798,9 @@
 END_SLOTS = 4
 
 
-def end_kernel(near, far, ffn, section, *refs):
-    outs, (low_buf, full_buf, in_sem, out_sem) = refs[:9], refs[9:]
+def end_kernel(near, far, ffn, section, d_in, *refs):
+    d_out, *outs = refs[:10]
+    low_buf, full_buf, in_sem, out_sem = refs[10:]
     outputs, out2, query2, kv2, out, qkv, gate, up, down = outs
     wide = low_buf.shape[2]
     jobs = []
@@ -1824,14 +1814,14 @@
         jobs += [(ffn, base + r, target, r) for r in range(0, target.shape[0], UNIT)]
         base += target.shape[0]
     jobs += [(near, r, outputs, r) for r in range(0, outputs.shape[0], UNIT)]
+    jobs += [(d_in, r, d_out, r) for r in range(0, d_out.shape[0], UNIT)]
 
     def loads(n):
         source, row, target, place = jobs[n]
         slot = n % END_SLOTS
+        buf = full_buf if source is d_in else low_buf
         copies = [
-            pltpu.make_async_copy(
-                source.at[pl.ds(row, UNIT)], low_buf.at[slot], in_sem.at[slot, 0]
-            )
+            pltpu.make_async_copy(source.at[pl.ds(row, UNIT)], buf.at[slot], in_sem.at[slot, 0])
         ]
         if target is outputs:
             copies.append(
@@ -1886,7 +1876,8 @@
                 full_buf[slot, cut] = value
             return carry
 
-        lax.fori_loop(0, UNIT // 32, block, 0)
+        if jobs[n][0] is not d_in:
+            lax.fori_loop(0, UNIT // 32, block, 0)
         for copy in stores(n):
             copy.start()
     for n in range(max(len(jobs) - END_SLOTS, 0), len(jobs)):
@@ -1894,16 +1885,19 @@
             copy.wait()
 
 
-def end_all(near, far, ffn, section, out_shapes):
+def end_all(near, far, ffn, section, d_in, out_shapes):
     hbm = pl.BlockSpec(memory_space=pltpu.HBM)
     wide = near.shape[1]
     dma = pltpu.SemaphoreType.DMA
     return pl.pallas_call(
         end_kernel,
-        out_shape=[jax.ShapeDtypeStruct(near.shape, near.dtype)]
+        out_shape=[
+            jax.ShapeDtypeStruct(d_in.shape, d_in.dtype),
+            jax.ShapeDtypeStruct(near.shape, near.dtype),
+        ]
         + [jax.ShapeDtypeStruct(s, jnp.float32) for s in out_shapes],
-        in_specs=[hbm] * 4,
-        out_specs=[hbm] * 9,
+        in_specs=[hbm] * 5,
+        out_specs=[hbm] * 10,
         scratch_shapes=[
             pltpu.VMEM((END_SLOTS, UNIT, wide), near.dtype),
             pltpu.VMEM((END_SLOTS, UNIT, wide), jnp.float32),
@@ -1911,7 +1905,7 @@
             dma((END_SLOTS, 2)),
         ],
         compiler_params=pltpu.CompilerParams(vmem_limit_bytes=VMEM_LIMIT),
-    )(near, far, ffn, section)
+    )(near, far, ffn, section, d_in)
 
 
 def per_device(
@@ -1946,6 +1940,7 @@
     grad_mlp = (cotangent[0].astype(jnp.float32) * slot_valid[0].astype(jnp.float32)).astype(
         jnp.bfloat16
     )
+    grad_mlp = lax.optimization_barrier(grad_mlp)
     all_grad = lax.all_gather(grad_mlp, "grp", axis=0, tiled=True)
     tables = turn_tables(positions[0])
     padded_cond = jnp.pad(cond_rows, ((0, COND_ROWS - NC), (0, 0)))
@@ -1997,6 +1992,7 @@
         mlp_out, total_a, total_f = totals
         norm_total = total_a[total_a.shape[0] - CUT :][:6]
         (
+            d_tokens,
             outputs,
             grad_out_two,
             grad_query_two,
@@ -2009,6 +2005,7 @@
             total_a,
             total_f,
             section_two,
+            d_tokens,
             [w.shape for w in (w_out2, w_query2, w_kv2, w_out, w_qkv, w_gate, w_up, w_down)],
         )
     else:

time: 614 us -> 607 us (0.989); the launches traced: 612 us -> 597 us
  Pallas kernels: 583 us -> 572 us
    pallas_call x1, Pallas kernels: 111 us -> 104 us  [ffn_all(): pl.pallas_call(ffn_kernel, out_shape=[jax.ShapeDtypeStruct((2, 2, 2, seq_...]
  transfers between devices with their start and end apart: 1 -> 1, of which waited for: 0 -> 0; matrix products, arithmetic and copies ran while one was open for 1% -> 1% of each run, Pallas kernels for 25% -> 26%
where the time goes in v6:
time: 607 us; the launch traced here: 597 us
  Pallas kernels  572 us (94%)
  between operations  15.4 us (3%)
    pallas_call x1, Pallas kernels, attention_backward(): pl.pallas_call(functools.partial(attention_backward_kernel, plan), out_sh...  298 us
    pallas_call x1, Pallas kernels, attention_forward(): pl.pallas_call(functools.partial(attention_forward_kernel, pieces), out_s...  153 us
    pallas_call x1, Pallas kernels, ffn_all(): pl.pallas_call(ffn_kernel, out_shape=[jax.ShapeDtypeStruct((2, 2, 2, seq_...  104 us
    pallas_call x1, Pallas kernels, end_all(): pl.pallas_call(end_kernel, out_shape=[jax.ShapeDtypeStruct(d_in.shape, d_...  16.6 us
  transfers between devices with their start and end apart: 1, of which 0 were waited for; matrix products, arithmetic and copies ran while one was open for 1% of the time, Pallas kernels for 26%

profile of v6, /device:TPU:24, one launch (start us, length us, event | category | flops | bytes accessed | tf_op | source)
XLA Modules:
  0.0 596.6 jit_solution(13940094387139758814)
XLA Ops:
  7.2 0.0 copy-start.3
  7.2 0.0 copy-start.4
  7.2 0.0 copy-start.5
  7.2 0.0 copy-start.6
  7.2 0.0 copy-start.7
  7.2 0.0 copy-start.8
  7.2 0.0 copy-start.2
  7.3 0.0 all-gather.2.cloned.1.call-start
  7.9 2.5 fusion.refs_22_
  10.4 0.0 copy-start
  10.4 0.0 all-gather.2.cloned.1.call-update
  10.5 0.1 pad.11.clone
  10.5 0.1 pad.8.clone
  10.6 0.0 copy-done.3
  10.6 0.0 copy-done.4
  10.7 0.0 copy-done.5
  10.7 0.0 copy-done.6
  10.7 0.0 copy-done.7
  10.7 0.0 copy-done.8
  10.8 0.0 copy-done.2
  10.8 0.2 multiply_sine_fusion
  11.0 0.8 copy.36.sine_left.refs_4_
  11.8 0.1 maximum_maximum_fusion
  11.9 0.8 copy.35.cosine.refs_3_
  12.8 0.8 copy.37.sine_right.refs_5_
  13.6 0.0 copy-done
  13.6 0.8 pad.5.cond_in.refs_1_
  14.4 0.5 dynamic_update_slice.3.norms_in
  14.9 0.0 copy-start.1
  14.9 0.6 copy-done.1
  15.5 153.0 %shard_map.306 = (f32[16,1536]{1,0:T(8,128)}, bf16[4608,1536]{1,0:T(8,128)(2,1)}, bf16[1536,1536]{1,0:T(8,128)(2,1)}, bf16[1536,1536]{1,0:T(8,128)(2,1)}, bf16[1...) custom-call(bf16[384,1536]{1,0:T(8,128)(2,1)} %bitcast.16, ...), custom_call_target="tpu_custom_call" | custom-call | tf_op jit(solution)/shard_map/pallas_call | solution.py:1389
  168.5 0.0 all-gather.2.cloned.1.call-done.cot_in
  168.6 104.2 %shard_map.307 = (bf16[2,2,2,384,1536]{4,3,2,1,0:T(8,128)(2,1)}, bf16[384,1536]{1,0:T(8,128)(2,1)}, bf16[768,1536]{1,0:T(8,128)(2,1)}, bf16[768,1536]{1,0:T(8,128)(2,1)}, bf16[768,1536]{1,0:T(8,128)(2,1)}) custom-call(bf16[384,1536]{1,0:T(8,128)(2,1)} %get-tuple-element.68.act_in, bf16[3072,1536]{1,0:T(8,128)(2,1)} %all-gather.2.cloned.1.call-done.cot_in, ...), custom_call_target="tpu_custom_call" | custom-call | tf_op jit(solution)/shard_map/pallas_call | solution.py:988
  272.8 298.5 %shard_map.308 = (f32[384,1536]{1,0:T(8,128)}, f32[8,1536]{1,0:T(8,128)}, bf16[2,2,2,192,1536]{4,3,2,1,0:T(8,128)(2,1)}, bf16[2,2,2,192,1536]{4,3,2,1,0:T(8,128)...) custom-call(bf16[384,1536]{1,0:T(8,128)(2,1)} %bitcast.17, ...), custom_call_target="tpu_custom_call" | custom-call | tf_op jit(solution)/shard_map/pallas_call | solution.py:1756
  571.3 0.7 slice.23
  572.0 0.1 dynamic-slice_convert_fusion
  572.1 0.6 fusion.2
  572.7 16.6 %shard_map.309 = (f32[384,1536]{1,0:T(8,128)}, bf16[384,1536]{1,0:T(8,128)(2,1)}, f32[192,1536]{1,0:T(8,128)}, f32[192,1536]{1,0:T(8,128)}, f32[384,768]{1,0:T(8...) custom-call(bf16[384,1536]{1,0:T(8,128)(2,1)} %get-tuple-element.74., ...), custom_call_target="tpu_custom_call" | custom-call | tf_op jit(solution)/shard_map/pallas_call | solution.py:1892
  (18 shorter events, 0.2 us)
Async XLA Ops:
  7.2 3.4 copy-start.3
  7.2 3.4 copy-start.4
  7.2 3.5 copy-start.5
  7.2 3.5 copy-start.6
  7.2 3.5 copy-start.7
  7.2 3.5 copy-start.8
  7.2 3.5 copy-start.2
  7.3 161.3 %all-gather.2.cloned.1.call-start = ((), (), s32[]{:S(2)}) async-start(), calls=%async_computation | async-start | bytes 10616832 | tf_op jit(solution)/shard_map/all_gather | solution.py:1944
  10.4 3.2 copy-start
  14.9 0.6 copy-start.1
Sparse Core Ops, SparseCore 0:
  10.6 97.9 all-gather.1

commit v7 on v6

--- a/solution.py
+++ b/solution.py
@@ -1031,7 +1031,7 @@
 
 PAIR = 128
 COND_ROWS = 256
-NORM_ROWS = 32
+NORM_ROWS = 128
 
 
 def normalise(read, gain, shift, write, rows):
@@ -1795,7 +1795,7 @@
     return results[0], results[1], results[2:7], results[8:11]
 
 
-END_SLOTS = 4
+END_SLOTS = 6
 
 
 def end_kernel(near, far, ffn, section, d_in, *refs):

time: 607 us -> 603 us (level)
  no operation moved by 1% of the time
where the time goes in v7:
time: 603 us; the launch traced here: 593 us
  Pallas kernels  568 us (94%)
  between operations  15.4 us (3%)
    pallas_call x1, Pallas kernels, attention_backward(): pl.pallas_call(functools.partial(attention_backward_kernel, plan), out_sh...  298 us
    pallas_call x1, Pallas kernels, attention_forward(): pl.pallas_call(functools.partial(attention_forward_kernel, pieces), out_s...  151 us
    pallas_call x1, Pallas kernels, ffn_all(): pl.pallas_call(ffn_kernel, out_shape=[jax.ShapeDtypeStruct((2, 2, 2, seq_...  104 us
    pallas_call x1, Pallas kernels, end_all(): pl.pallas_call(end_kernel, out_shape=[jax.ShapeDtypeStruct(d_in.shape, d_...  15.4 us
  transfers between devices with their start and end apart: 1, of which 0 were waited for; matrix products, arithmetic and copies ran while one was open for 1% of the time, Pallas kernels for 26%

profile of v7, /device:TPU:24, one launch (start us, length us, event | category | flops | bytes accessed | tf_op | source)
XLA Modules:
  0.0 592.8 jit_solution(4987427177987467666)
XLA Ops:
  7.2 0.0 copy-start.3
  7.2 0.0 copy-start.4
  7.2 0.0 copy-start.5
  7.2 0.0 copy-start.6
  7.2 0.0 copy-start.7
  7.2 0.0 copy-start.8
  7.2 0.0 copy-start.2
  7.3 0.0 all-gather.2.cloned.1.call-start
  7.9 2.5 fusion.refs_22_
  10.4 0.0 copy-start
  10.4 0.0 all-gather.2.cloned.1.call-update
  10.5 0.1 pad.11.clone
  10.5 0.1 pad.8.clone
  10.6 0.0 copy-done.3
  10.6 0.0 copy-done.4
  10.7 0.0 copy-done.5
  10.7 0.0 copy-done.6
  10.7 0.0 copy-done.7
  10.7 0.0 copy-done.8
  10.8 0.0 copy-done.2
  10.8 0.2 multiply_sine_fusion
  11.0 0.8 copy.36.sine_left.refs_4_
  11.8 0.1 maximum_maximum_fusion
  11.9 0.8 copy.35.cosine.refs_3_
  12.8 0.8 copy.37.sine_right.refs_5_
  13.6 0.0 copy-done
  13.6 0.8 pad.5.cond_in.refs_1_
  14.4 0.5 dynamic_update_slice.3.norms_in
  14.9 0.0 copy-start.1
  14.9 0.6 copy-done.1
  15.5 151.3 %shard_map.306 = (f32[16,1536]{1,0:T(8,128)}, bf16[4608,1536]{1,0:T(8,128)(2,1)}, bf16[1536,1536]{1,0:T(8,128)(2,1)}, bf16[1536,1536]{1,0:T(8,128)(2,1)}, bf16[1...) custom-call(bf16[384,1536]{1,0:T(8,128)(2,1)} %bitcast.16, ...), custom_call_target="tpu_custom_call" | custom-call | tf_op jit(solution)/shard_map/pallas_call | solution.py:1389
  166.8 0.0 all-gather.2.cloned.1.call-done.cot_in
  166.9 104.2 %shard_map.307 = (bf16[2,2,2,384,1536]{4,3,2,1,0:T(8,128)(2,1)}, bf16[384,1536]{1,0:T(8,128)(2,1)}, bf16[768,1536]{1,0:T(8,128)(2,1)}, bf16[768,1536]{1,0:T(8,128)(2,1)}, bf16[768,1536]{1,0:T(8,128)(2,1)}) custom-call(bf16[384,1536]{1,0:T(8,128)(2,1)} %get-tuple-element.68.act_in, bf16[3072,1536]{1,0:T(8,128)(2,1)} %all-gather.2.cloned.1.call-done.cot_in, ...), custom_call_target="tpu_custom_call" | custom-call | tf_op jit(solution)/shard_map/pallas_call | solution.py:988
  271.1 297.6 %shard_map.308 = (f32[384,1536]{1,0:T(8,128)}, f32[8,1536]{1,0:T(8,128)}, bf16[2,2,2,192,1536]{4,3,2,1,0:T(8,128)(2,1)}, bf16[2,2,2,192,1536]{4,3,2,1,0:T(8,128)...) custom-call(bf16[384,1536]{1,0:T(8,128)(2,1)} %bitcast.17, ...), custom_call_target="tpu_custom_call" | custom-call | tf_op jit(solution)/shard_map/pallas_call | solution.py:1756
  568.7 0.7 slice.23
  569.4 0.1 dynamic-slice_convert_fusion
  569.5 0.6 fusion.2
  570.1 15.4 %shard_map.309 = (f32[384,1536]{1,0:T(8,128)}, bf16[384,1536]{1,0:T(8,128)(2,1)}, f32[192,1536]{1,0:T(8,128)}, f32[192,1536]{1,0:T(8,128)}, f32[384,768]{1,0:T(8...) custom-call(bf16[384,1536]{1,0:T(8,128)(2,1)} %get-tuple-element.74., ...), custom_call_target="tpu_custom_call" | custom-call | tf_op jit(solution)/shard_map/pallas_call | solution.py:1892
  (18 shorter events, 0.2 us)
Async XLA Ops:
  7.2 3.4 copy-start.3
  7.2 3.4 copy-start.4
  7.2 3.5 copy-start.5
  7.2 3.5 copy-start.6
  7.2 3.5 copy-start.7
  7.2 3.5 copy-start.8
  7.2 3.5 copy-start.2
  7.3 159.6 %all-gather.2.cloned.1.call-start = ((), (), s32[]{:S(2)}) async-start(), calls=%async_computation | async-start | bytes 10616832 | tf_op jit(solution)/shard_map/all_gather | solution.py:1944
  10.4 3.2 copy-start
  14.9 0.6 copy-start.1
Sparse Core Ops, SparseCore 0:
  10.6 97.9 all-gather.1
